TPU v7x, 256 devices: a whole 4x4x8 slice. The times are simulated.
256 devices in a mesh: row: 64 (over x, z, core), snap: 4 (over y).
Axes of the slice: x: 4, y: 4, z: 8, core: 2. Of those that a mesh axis runs over, the one named last changes fastest.
Arguments:
- anomalies: float32 [131072, 4096], P('row', 'snap'), may hold values from -600 to 600, as said below
- start_basis: float32 [4096, 128], P('snap'), may hold values from -0.09375 to 0.09375
Outputs:
- space_basis: float32 [131072, 128], P('row')
- time_basis: float32 [4096, 128], P('snap')
Inputs may be any that keep to these rules, and one draw needn't show every extreme that they name: `anomalies`: real values of order one times positive scales of grid points and snapshots.
All inputs are finite; a program needn't handle non-finite values.
Results may differ from a plain program's by a relative error of at most 0.000084.
Values sent between devices are 32-bit elements; how exact they have to be, the bound alone decides.
No kernel may reach another device: no remote copies, remote signals or barrier semaphores. Data moves between devices by JAX's collectives and lax.ppermute only.
A program may use at most 64 MiB of HBM per device.

v0:
```python
import jax
import jax.numpy as jnp
from jax import lax
from jax.sharding import PartitionSpec as P


def local_gram(block):
    return jnp.dot(
        block.T, block, precision=lax.Precision.HIGHEST, preferred_element_type=jnp.float32
    )


def apply_factor(gram, block):
    factor = jnp.linalg.cholesky(gram)
    return lax.linalg.triangular_solve(factor, block, left_side=False, lower=True, transpose_a=True)


def on_device(anomalies, start_basis):
    partial_sketch = jnp.dot(
        anomalies, start_basis, precision=lax.Precision.HIGHEST, preferred_element_type=jnp.float32
    )
    sketch = lax.psum(partial_sketch, "snap")
    gram = lax.psum(local_gram(sketch), "row")
    space_basis = apply_factor(gram, sketch)
    partial_back = lax.dot_general(
        anomalies,
        space_basis,
        (((0,), (0,)), ((), ())),
        precision=lax.Precision.HIGHEST,
        preferred_element_type=jnp.float32,
    )
    back = lax.psum(partial_back, "row")
    gram_back = lax.psum(local_gram(back), "snap")
    time_basis = apply_factor(gram_back, back)
    return (space_basis, time_basis)


def solution(mesh):
    return jax.shard_map(
        on_device,
        mesh=mesh,
        in_specs=(P("row", "snap"), P("snap", None)),
        out_specs=(P("row", None), P("snap", None)),
        check_vma=False,
    )
```

profile of v0, /device:TPU:1, one launch (start us, length us, event | category | flops | bytes accessed | tf_op | source)
XLA Modules:
  0.0 538.1 jit_solution(18386211112313162382)
XLA Ops:
  7.2 0.0 copy-start
  7.2 0.0 all-reduce.5.cloned.1.call-start
  7.2 1.0 copy-done
  8.2 9.8 %fusion.8 = f32[2048,128]{1,0:T(8,128)} fusion(f32[2048,1024]{1,0:T(8,128)} %param.3, f32[1024,128]{1,0:T(8,128)S(1)} %copy-done), kind=kOutput, calls=%fused_computation.19 | convolution fusion | flops 3221225472 | bytes 9961472 | tf_op jit(solution)/shard_map/dot_general | solution.py:19
  18.0 0.0 all-reduce.5.cloned.1.call-update
  18.1 0.0 all-reduce.7.cloned.1.call-start
  18.1 53.5 %all-reduce.5.cloned.1.call-done = f32[2048,128]{1,0:T(8,128)} async-done(((f32[2048,128]{1,0:T(8,128)}), f32[2048,128]{1,0:T(8,128)}) %all-reduce.5.cloned.1.call-update) | async-done | bytes 1048592 | tf_op jit(solution)/shard_map/psum | solution.py:22
  71.6 4.0 fusion.9
  75.6 0.0 all-reduce.7.cloned.1.call-update
  75.6 0.2 all-reduce.9.cloned.1.call-start
  75.8 170.5 %all-reduce.7.cloned.1.call-done = f32[128,128]{0,1:T(8,128)} async-done(((f32[128,128]{0,1:T(8,128)}), f32[128,128]{0,1:T(8,128)}) %all-reduce.7.cloned.1.call-update) | async-done | bytes 65552 | tf_op jit(solution)/shard_map/psum | solution.py:23
  246.3 0.9 copy.5
  247.2 0.9 fusion.7
  248.1 11.7 %cholesky.44 = f32[128,128]{1,0:T(8,128)S(1)} custom-call(f32[128,128]{1,0:T(8,128)S(1)} %fusion.7), custom_call_target="Cholesky" | custom-call | tf_op jit(solution)/shard_map/jit(cholesky)/cholesky | solution.py:14
  259.8 0.6 compare_reduce_fusion.1
  260.5 0.7 fusion
  261.1 9.8 %custom-call.8 = f32[1,128,128]{1,2,0:T(8,128)S(1)} custom-call(f32[1,128,128]{2,1,0:T(8,128)S(1)} %fusion), custom_call_target="InvertDiagBlocksLowerTriangular" | custom-call | tf_op jit(solution)/shard_map/triangular_solve | solution.py:15
  270.9 2.2 fusion.5
  273.2 8.2 %convolution_bitcast_fusion = f32[1024,128]{0,1:T(8,128)} fusion(f32[2048,128]{1,0:T(8,128)S(1)} %fusion.5, f32[2048,1024]{1,0:T(8,128)} %param.3), kind=kOutput, calls=%fused_computation | convolution fusion | flops 3221225472 | bytes 9961472 | tf_op jit(solution)/shard_map/dot_general | solution.py:25
  281.3 0.0 all-reduce.9.cloned.1.call-update
  281.3 0.3 all-reduce.11.cloned.1.call-start
  281.6 176.3 %all-reduce.9.cloned.1.call-done = f32[1024,128]{0,1:T(8,128)} async-done(((f32[1024,128]{0,1:T(8,128)}), f32[1024,128]{0,1:T(8,128)}) %all-reduce.9.cloned.1.call-update) | async-done | bytes 524304 | tf_op jit(solution)/shard_map/psum | solution.py:32
  457.9 2.4 fusion.10
  460.3 0.0 all-reduce.11.cloned.1.call-update
  460.4 43.8 %all-reduce.11.cloned.1.call-done = f32[128,128]{0,1:T(8,128)} async-done(((f32[128,128]{0,1:T(8,128)}), f32[128,128]{0,1:T(8,128)}) %all-reduce.11.cloned.1.call-update) | async-done | bytes 65552 | tf_op jit(solution)/shard_map/psum | solution.py:33
  504.1 0.9 copy.7
  505.1 0.9 fusion.4
  505.9 11.7 %cholesky.55 = f32[128,128]{1,0:T(8,128)S(1)} custom-call(f32[128,128]{1,0:T(8,128)S(1)} %fusion.4), custom_call_target="Cholesky" | custom-call | tf_op jit(solution)/shard_map/jit(cholesky)/cholesky | solution.py:14
  517.7 0.6 compare_reduce_fusion
  518.3 0.7 fusion.1
  519.0 9.8 %custom-call.9 = f32[1,128,128]{1,2,0:T(8,128)S(1)} custom-call(f32[1,128,128]{2,1,0:T(8,128)S(1)} %fusion.1), custom_call_target="InvertDiagBlocksLowerTriangular" | custom-call | tf_op jit(solution)/shard_map/triangular_solve | solution.py:15
  528.8 2.8 fusion.2
  (4 shorter events, 0.1 us)
Async XLA Ops:
  7.2 1.0 copy-start
  7.2 64.4 %all-reduce.5.cloned.1.call-start = ((), (), s32[]{:S(2)}) async-start(), calls=%async_computation | async-start | bytes 2097152 | tf_op jit(solution)/shard_map/psum | solution.py:22
  18.1 228.2 %all-reduce.7.cloned.1.call-start = ((), (), s32[]{:S(2)}) async-start(), calls=%async_computation.1 | async-start | bytes 131072 | tf_op jit(solution)/shard_map/psum | solution.py:23
  75.6 382.3 %all-reduce.9.cloned.1.call-start = ((), (), s32[]{:S(2)}) async-start(), calls=%async_computation.2 | async-start | bytes 1048576 | tf_op jit(solution)/shard_map/psum | solution.py:32
  273.1 258.5 %copy-start.1 = (f32[2048,128]{1,0:T(8,128)}, f32[2048,128]{1,0:T(8,128)S(1)}, u32[]{:S(2)}) copy-start(f32[2048,128]{1,0:T(8,128)S(1)} %fusion.5) | copy-start | bytes 3145732
  281.3 222.8 %all-reduce.11.cloned.1.call-start = ((), (), s32[]{:S(2)}) async-start(), calls=%async_computation.3 | async-start | bytes 131072 | tf_op jit(solution)/shard_map/psum | solution.py:33
Sparse Core Ops, SparseCore 0:
  18.2 53.3 all-reduce.4
  76.0 170.2 all-reduce.6
  281.5 176.4 all-reduce.8
  460.8 43.3 all-reduce.10
where the time goes:
time: 540 us; the launch traced here: 538 us
  waiting for transfers between devices  444 us (82%)
  other arithmetic  47.4 us (9%)
  matrix products  29.4 us (5%)
  between operations  13.8 us (3%)
    psum x1, waiting for transfers between devices, on_device(): back = lax.psum(partial_back, 'row')  176 us
    psum x1, waiting for transfers between devices, on_device(): gram = lax.psum(local_gram(sketch), 'row')  170 us
    psum x1, waiting for transfers between devices, on_device(): sketch = lax.psum(partial_sketch, 'snap')  53.5 us
    psum x1, waiting for transfers between devices, on_device(): gram_back = lax.psum(local_gram(back), 'snap')  43.8 us
    another operation x6, other arithmetic, apply_factor(): factor = jnp.linalg.cholesky(gram)  24.8 us
    another operation x4, other arithmetic, apply_factor(): lax.linalg.triangular_solve(factor, block, left_side=False, lower=True, t...  20.9 us
  transfers between devices with their start and end apart: 4, of which 4 were waited for; matrix products, arithmetic and copies ran while one was open for 0% of the time, Pallas kernels for 0%

commit v1 on v0

v1 whole, which is shorter than its diff:
```python
import jax
import jax.numpy as jnp
from jax import lax
from jax.sharding import Mesh, PartitionSpec as P

HIGH = lax.Precision.HIGH
HIGHEST = lax.Precision.HIGHEST


def shifted(value, axis, shift):
    n = lax.axis_size(axis)
    return lax.ppermute(value, axis, [(i, (i + shift) % n) for i in range(n)])


def scatter_sum(value, axis):
    n = lax.axis_size(axis)
    pieces = value.reshape((n, value.shape[0] // n) + value.shape[1:])
    me = lax.axis_index(axis)
    total = lax.dynamic_index_in_dim(pieces, me, 0, keepdims=False)
    for shift in range(1, n):
        piece = lax.dynamic_index_in_dim(pieces, (me + shift) % n, 0, keepdims=False)
        total = total + shifted(piece, axis, shift)
    return total


def gather(value, axis):
    n = lax.axis_size(axis)
    me = lax.axis_index(axis)
    rows = value.shape[0]
    whole = jnp.zeros((n * rows,) + value.shape[1:], value.dtype)
    whole = lax.dynamic_update_slice_in_dim(whole, value, me * rows, 0)
    for shift in range(1, n):
        piece = shifted(value, axis, shift)
        whole = lax.dynamic_update_slice_in_dim(whole, piece, ((me - shift) % n) * rows, 0)
    return whole


def exchange_sum(value, axis):
    n = lax.axis_size(axis)
    pieces = value.reshape((n, value.shape[0] // n) + value.shape[1:])
    return jnp.sum(lax.all_to_all(pieces, axis, 0, 0), 0)


def exchange_gather(value, axis):
    n = lax.axis_size(axis)
    copies = jnp.broadcast_to(value[None], (n,) + value.shape)
    got = lax.all_to_all(copies, axis, 0, 0)
    return got.reshape((n * value.shape[0],) + value.shape[1:])


def local_gram(block):
    return lax.dot_general(
        block, block, (((0,), (0,)), ((), ())), precision=HIGHEST, preferred_element_type=jnp.float32
    )


def apply_factor(gram, block):
    factor = jnp.linalg.cholesky(gram)
    return lax.linalg.triangular_solve(factor, block, left_side=False, lower=True, transpose_a=True)


def on_device(anomalies, start_basis):
    partial_sketch = jnp.dot(
        anomalies, start_basis, precision=HIGH, preferred_element_type=jnp.float32
    )
    sketch = gather(exchange_sum(partial_sketch, "y"), "y")
    partial_raw = lax.dot_general(
        anomalies,
        sketch,
        (((0,), (0,)), ((), ())),
        precision=HIGH,
        preferred_element_type=jnp.float32,
    )
    stacked = jnp.concatenate([partial_raw, local_gram(sketch)], 0)
    part = scatter_sum(stacked, "c")
    part = scatter_sum(part, "x")
    part = exchange_gather(exchange_sum(part, "z"), "z")
    whole = gather(gather(part, "x"), "c")
    snaps = anomalies.shape[1]
    raw, gram = whole[:snaps], whole[snaps:]
    space_basis = apply_factor(gram, sketch)
    back = apply_factor(gram, raw)
    gram_back = local_gram(back)
    gram_back = gram_back + sum(shifted(gram_back, "y", s) for s in (1, 2, 3))
    time_basis = apply_factor(gram_back, back)
    return (space_basis, time_basis)


def solution(mesh):
    split = Mesh(mesh.devices.reshape(4, 8, 2, 4), ("x", "z", "c", "y"))
    rows = ("x", "z", "c")
    return jax.shard_map(
        on_device,
        mesh=split,
        in_specs=(P(rows, "y"), P("y", None)),
        out_specs=(P(rows, None), P("y", None)),
        check_vma=False,
    )
```

time: 540 us -> 163 us (0.30)
  waiting for transfers between devices: 444 us -> 17.3 us
  blocking collectives: 0 us -> 44.9 us
  starting transfers between devices: 0.56 us -> 23.2 us
  between operations: 13.8 us -> 0.94 us
  matrix products: 29.4 us -> 17.2 us
  local copies, waits for them, and re-layouts: 2.85 us -> 13.2 us
    psum x4 -> x0, waiting for transfers between devices: 444 us -> none  [the longest x1 176 us: on_device(): back = lax.psum(partial_back, 'row')]
    all_to_all x0 -> x3, blocking collectives: none -> 44.9 us  [the longest x2 34.7 us: exchange_sum(): return jnp.sum(lax.all_to_all(pieces, axis, 0, 0), 0)]
    ppermute x0 -> x14, starting transfers between devices: none -> 23.2 us  [shifted(): return lax.ppermute(value, axis, [(i, (i + shift) % n) for i in range(n)])]
    ppermute x0 -> x14, waiting for transfers between devices: none -> 17.3 us  [shifted(): return lax.ppermute(value, axis, [(i, (i + shift) % n) for i in range(n)])]
    dynamic_update_slice x0 -> x10, local copies, waits for them, and re-layouts: none -> 10.4 us  [the longest x7 6.48 us: gather(): lax.dynamic_update_slice_in_dim(whole, piece, (me - shift) % n * rows, 0)]
    dot_general x4, matrix products: 24.4 us -> 14 us  [the longest x1 5.81 us: on_device(): jnp.dot(anomalies, start_basis, precision=HIGH, preferred_element_type=jn...]
  transfers between devices with their start and end apart: 4 -> 14, of which waited for: 4 -> 8; matrix products, arithmetic and copies ran while one was open for 0% -> 5% of each run, Pallas kernels for 0% -> 0%
where the time goes in v1:
time: 163 us
  other arithmetic  45.9 us (28%)
  blocking collectives  44.9 us (28%)
  starting transfers between devices  23.2 us (14%)
  waiting for transfers between devices  17.3 us (11%)
  matrix products  17.2 us (11%)
  local copies, waits for them, and re-layouts  13.2 us (8%)
    all_to_all x2, blocking collectives, exchange_sum(): return jnp.sum(lax.all_to_all(pieces, axis, 0, 0), 0)  34.7 us
    another operation x6, other arithmetic, apply_factor(): factor = jnp.linalg.cholesky(gram)  24.8 us
    ppermute x14, starting transfers between devices, shifted(): return lax.ppermute(value, axis, [(i, (i + shift) % n) for i in range(n)])  23.2 us
    another operation x4, other arithmetic, apply_factor(): lax.linalg.triangular_solve(factor, block, left_side=False, lower=True, t...  20.9 us
    ppermute x14, waiting for transfers between devices, shifted(): return lax.ppermute(value, axis, [(i, (i + shift) % n) for i in range(n)])  17.3 us
    all_to_all x1, blocking collectives, exchange_gather(): got = lax.all_to_all(copies, axis, 0, 0)  10.2 us
    dynamic_update_slice x7, local copies, waits for them, and re-layouts, gather(): lax.dynamic_update_slice_in_dim(whole, piece, (me - shift) % n * rows, 0)  6.48 us
    dot_general x1, matrix products, on_device(): jnp.dot(anomalies, start_basis, precision=HIGH, preferred_element_type=jn...  5.81 us
  transfers between devices with their start and end apart: 14, of which 8 were waited for; matrix products, arithmetic and copies ran while one was open for 5% of the time, Pallas kernels for 0%

profile of v1, /device:TPU:1, one launch (start us, length us, event | category | flops | bytes accessed | tf_op | source)
XLA Modules:
  0.0 162.7 jit_solution(2989451233029729515)
XLA Ops:
  0.6 1.0 copy-done
  1.7 5.8 %fusion.11 = f32[2048,128]{1,0:T(8,128)S(1)} fusion(f32[2048,1024]{1,0:T(8,128)} %param.5, f32[1024,128]{1,0:T(8,128)S(1)} %copy-done), kind=kOutput, calls=%fused_computation.36 | convolution fusion | flops 1610612736 | bytes 9961472 | tf_op jit(solution)/shard_map/dot_general | solution.py:63
  7.5 19.0 %all_to_all.15 = f32[4,512,128]{2,1,0:T(8,128)S(1)} all-to-all(f32[4,512,128]{2,1,0:T(8,128)S(1)} %bitcast.57), channel_id=1, replica_groups=mesh['x'=4,'z'=8,'c'=2,'y'=4] {'y'}, dimensions={0} | all-to-all | bytes 2097152 | tf_op jit(solution)/shard_map/all_to_all | solution.py:41
  26.9 1.8 %collective-permute-start.1 = (f32[512,128]{1,0:T(8,128)S(1)}, f32[512,128]{1,0:T(8,128)S(1)}, u32[]{:S(2)}, u32[]{:S(2)}) collective-permute-start(f32[512,128]{1,0:T(8,128)S(1)} %reduce_sum.18), channel_id=1, source_target_pairs={{0,2},{1,3},{2,0},{3,1},{4,6},{5,7},{6,4},{7,5},{8,10},{9,11},{10,... | collective-permute-start | bytes 786440 | tf_op jit(solution)/shard_map/ppermute | solution.py:12
  29.5 4.9 %collective-permute-done = f32[512,128]{1,0:T(8,128)S(1)} collective-permute-done((f32[512,128]{1,0:T(8,128)S(1)}, f32[512,128]{1,0:T(8,128)S(1)}, u32[]{:S(2)}, u32[]{:S(2)}) %collective-permute-start) | collective-permute-done | bytes 262176 | tf_op jit(solution)/shard_map/ppermute | solution.py:12
  34.4 4.4 %collective-permute-done.1 = f32[512,128]{1,0:T(8,128)S(1)} collective-permute-done((f32[512,128]{1,0:T(8,128)S(1)}, f32[512,128]{1,0:T(8,128)S(1)}, u32[]{:S(2)}, u32[]{:S(2)}) %collective-permute-start.1) | collective-permute-done | bytes 262176 | tf_op jit(solution)/shard_map/ppermute | solution.py:12
  38.8 2.0 %collective-permute-done.2 = f32[512,128]{1,0:T(8,128)S(1)} collective-permute-done((f32[512,128]{1,0:T(8,128)S(1)}, f32[512,128]{1,0:T(8,128)S(1)}, u32[]{:S(2)}, u32[]{:S(2)}) %collective-permute-start.2) | collective-permute-done | bytes 262176 | tf_op jit(solution)/shard_map/ppermute | solution.py:12
  40.9 5.8 %convolution_bitcast_fusion.2 = f32[1024,128]{0,1:T(8,128)S(1)} fusion(f32[2048,128]{1,0:T(8,128)S(1)} %constant_dynamic-update-slice_fusion, f32[2048,1024]{1,0:T(8,128)} %param.5), kind=kOutput, calls=%fused_computation.2 | convolution fusion | flops 1610612736 | bytes 9961472 | tf_op jit(solution)/shard_map/dot_general | solution.py:67
  46.7 1.8 %fusion.12 = f32[128,128]{0,1:T(8,128)S(1)} fusion(f32[2048,128]{1,0:T(8,128)S(1)} %constant_dynamic-update-slice_fusion), kind=kOutput, calls=%fused_computation.37 | convolution fusion | flops 402653184 | bytes 1114112 | tf_op jit(solution)/shard_map/dot_general | solution.py:52
  48.8 2.0 %collective-permute-start.3 = (f32[576,128]{1,0:T(8,128)S(1)}, f32[576,128]{1,0:T(8,128)S(1)}, u32[]{:S(2)}, u32[]{:S(2)}) collective-permute-start(f32[576,128]{1,0:T(8,128)S(1)} %dynamic-slice_bitcast_fusion), channel_id=1, source_target_pairs={{0,4},{4,0},{1,5},{5,1},{2,6},{6,2},{3,7},{7,3},{8,12},{12,8},{9,1... | collective-permute-start | bytes 884744 | tf_op jit(solution)/shard_map/ppermute | solution.py:12
  50.9 1.2 collective-permute-done.3
  52.2 1.3 collective-permute-start.4
  53.4 2.5 %collective-permute-start.5 = (f32[144,128]{1,0:T(8,128)S(1)}, f32[144,128]{1,0:T(8,128)S(1)}, u32[]{:S(2)}, u32[]{:S(2)}) collective-permute-start(f32[144,128]{1,0:T(8,128)S(1)} %get-tuple-element.10), channel_id=1, source_target_pairs={{0,128},{64,192},{128,0},{192,64},{1,129},{65,193},{129,1},{193,65... | collective-permute-start | bytes 221192 | tf_op jit(solution)/shard_map/ppermute | solution.py:12
  55.9 1.1 collective-permute-start.6
  57.0 2.1 %collective-permute-done.5 = f32[144,128]{1,0:T(8,128)S(1)} collective-permute-done((f32[144,128]{1,0:T(8,128)S(1)}, f32[144,128]{1,0:T(8,128)S(1)}, u32[]{:S(2)}, u32[]{:S(2)}) %collective-permute-start.5) | collective-permute-done | bytes 73760 | tf_op jit(solution)/shard_map/ppermute | solution.py:12
  59.5 15.7 %all_to_all.16 = f32[8,18,128]{2,1,0:T(8,128)S(1)} all-to-all(f32[8,18,128]{2,1,0:T(8,128)S(1)} %reshape.37), channel_id=1, replica_groups=mesh['x'=4,'z'=8,'c'=2,'y'=4] {'z'}, dimensions={0} | all-to-all | bytes 147456 | tf_op jit(solution)/shard_map/all_to_all | solution.py:41
  75.2 10.2 %all_to_all.17 = f32[8,18,128]{2,1,0:T(8,128)S(1)} all-to-all(f32[8,18,128]{2,1,0:T(8,128)S(1)} %broadcast_in_dim.19), channel_id=1, replica_groups=mesh['x'=4,'z'=8,'c'=2,'y'=4] {'z'}, dimensions={0} | all-to-all | bytes 147456 | tf_op jit(solution)/shard_map/all_to_all | solution.py:47
  85.6 3.1 %collective-permute-start.8 = (f32[144,128]{0,1:T(8,128)S(1)}, f32[144,128]{0,1:T(8,128)S(1)}, u32[]{:S(2)}, u32[]{:S(2)}) collective-permute-start(f32[144,128]{0,1:T(8,128)S(1)} %copy.14), channel_id=1, source_target_pairs={{0,128},{64,192},{128,0},{192,64},{1,129},{65,193},{129,1},{193,65... | collective-permute-start | bytes 221192 | tf_op jit(solution)/shard_map/ppermute | solution.py:12
  88.7 1.0 collective-permute-start.9
  89.7 1.1 dynamic_update_slice.34
  92.4 1.0 dynamic_update_slice.36
  93.5 1.3 dynamic_update_slice.37
  94.8 5.8 %collective-permute-start.10 = (f32[576,128]{0,1:T(8,128)S(1)}, f32[576,128]{0,1:T(8,128)S(1)}, u32[]{:S(2)}, u32[]{:S(2)}) collective-permute-start(f32[576,128]{0,1:T(8,128)S(1)} %dynamic_update_slice.37), channel_id=1, source_target_pairs={{0,4},{4,0},{1,5},{5,1},{2,6},{6,2},{3,7},{7,3},{8,12},{12,8},{9,1... | collective-permute-start | bytes 884744 | tf_op jit(solution)/shard_map/ppermute | solution.py:12
  100.7 2.9 %dynamic_update_slice.38 = f32[1152,128]{0,1:T(8,128)S(1)} dynamic-update-slice(f32[1152,128]{0,1:T(8,128)S(1)} %broadcast_in_dim.17, f32[576,128]{0,1:T(8,128)S(1)} %dynamic_update_slice.37, s32[]{:T(128)S(6)} %select_n.124, s32[]{:T(128)} %constant.134.clone.1) | dynamic-update-slice | bytes 589828 | tf_op jit(solution)/shard_map/dynamic_update_slice | solution.py:31
  103.5 3.2 %dynamic_update_slice.39 = f32[1152,128]{0,1:T(8,128)S(1)} dynamic-update-slice(f32[1152,128]{0,1:T(8,128)S(1)} %dynamic_update_slice.38, f32[576,128]{0,1:T(8,128)S(1)} %collective-permute-done.10, s32[]{:T(128)S(6)} %select_n.126, s32[]{:T(128)} %constant.134.clone.1) | dynamic-update-slice | bytes 589828 | tf_op jit(solution)/shard_map/dynamic_update_slice | solution.py:34
  106.9 11.7 %cholesky.44 = f32[128,128]{1,0:T(8,128)S(1)} custom-call(f32[128,128]{1,0:T(8,128)S(1)} %fusion.10), custom_call_target="Cholesky" | custom-call | tf_op jit(solution)/shard_map/jit(cholesky)/cholesky | solution.py:58
  120.0 9.8 %custom-call.8 = f32[1,128,128]{1,2,0:T(8,128)S(1)} custom-call(f32[1,128,128]{2,1,0:T(8,128)S(1)} %fusion.3), custom_call_target="InvertDiagBlocksLowerTriangular" | custom-call | tf_op jit(solution)/shard_map/triangular_solve | solution.py:59
  131.1 3.3 %collective-permute-start.12 = (f32[128,128]{0,1:T(8,128)S(1)}, f32[128,128]{0,1:T(8,128)S(1)}, u32[]{:S(2)}, u32[]{:S(2)}) collective-permute-start(f32[128,128]{0,1:T(8,128)S(1)} %fusion.13), channel_id=1, source_target_pairs={{0,2},{1,3},{2,0},{3,1},{4,6},{5,7},{6,4},{7,5},{8,10},{9,11},{10,... | collective-permute-start | bytes 196616 | tf_op jit(solution)/shard_map/ppermute | solution.py:12
  134.4 1.9 %fusion.8 = f32[2048,128]{1,0:T(8,128)} fusion(f32[2048,128]{1,0:T(8,128)S(1)} %constant_dynamic-update-slice_fusion, f32[1,128,128]{1,2,0:T(8,128)S(1)} %custom-call.8), kind=kOutput, calls=%fused_computation.21 | convolution fusion | flops 402653184 | bytes 2162688 | tf_op jit(solution)/shard_map/triangular_solve | solution.py:59
  136.4 1.7 %collective-permute-done.12 = f32[128,128]{0,1:T(8,128)S(1)} collective-permute-done((f32[128,128]{0,1:T(8,128)S(1)}, f32[128,128]{0,1:T(8,128)S(1)}, u32[]{:S(2)}, u32[]{:S(2)}) %collective-permute-start.12) | collective-permute-done | bytes 65568 | tf_op jit(solution)/shard_map/ppermute | solution.py:12
  138.2 11.7 %cholesky.55 = f32[128,128]{1,0:T(8,128)S(1)} custom-call(f32[128,128]{1,0:T(8,128)S(1)} %fusion.6), custom_call_target="Cholesky" | custom-call | tf_op jit(solution)/shard_map/jit(cholesky)/cholesky | solution.py:58
  151.2 9.8 %custom-call.11 = f32[1,128,128]{1,2,0:T(8,128)S(1)} custom-call(f32[1,128,128]{2,1,0:T(8,128)S(1)} %fusion.4), custom_call_target="InvertDiagBlocksLowerTriangular" | custom-call | tf_op jit(solution)/shard_map/triangular_solve/custom-call.2 | solution.py:59
  (50 shorter events, 9.6 us)
Async XLA Ops:
  0.6 1.0 copy-start
  26.6 7.8 %collective-permute-start = (f32[512,128]{1,0:T(8,128)S(1)}, f32[512,128]{1,0:T(8,128)S(1)}, u32[]{:S(2)}, u32[]{:S(2)}) collective-permute-start(f32[512,128]{1,0:T(8,128)S(1)} %reduce_sum.18), channel_id=1, source_target_pairs={{0,1},{1,2},{2,3},{3,0},{4,5},{5,6},{6,7},{7,4},{8,9},{9,10},{10,1... | collective-permute-start | bytes 786440 | tf_op jit(solution)/shard_map/ppermute | solution.py:12
  26.9 11.9 %collective-permute-start.1 = (f32[512,128]{1,0:T(8,128)S(1)}, f32[512,128]{1,0:T(8,128)S(1)}, u32[]{:S(2)}, u32[]{:S(2)}) collective-permute-start(f32[512,128]{1,0:T(8,128)S(1)} %reduce_sum.18), channel_id=1, source_target_pairs={{0,2},{1,3},{2,0},{3,1},{4,6},{5,7},{6,4},{7,5},{8,10},{9,11},{10,... | collective-permute-start | bytes 786440 | tf_op jit(solution)/shard_map/ppermute | solution.py:12
  28.7 12.2 %collective-permute-start.2 = (f32[512,128]{1,0:T(8,128)S(1)}, f32[512,128]{1,0:T(8,128)S(1)}, u32[]{:S(2)}, u32[]{:S(2)}) collective-permute-start(f32[512,128]{1,0:T(8,128)S(1)} %reduce_sum.18), channel_id=1, source_target_pairs={{0,3},{1,0},{2,1},{3,2},{4,7},{5,4},{6,5},{7,6},{8,11},{9,8},{10,9... | collective-permute-start | bytes 786440 | tf_op jit(solution)/shard_map/ppermute | solution.py:12
  48.8 3.2 %collective-permute-start.3 = (f32[576,128]{1,0:T(8,128)S(1)}, f32[576,128]{1,0:T(8,128)S(1)}, u32[]{:S(2)}, u32[]{:S(2)}) collective-permute-start(f32[576,128]{1,0:T(8,128)S(1)} %dynamic-slice_bitcast_fusion), channel_id=1, source_target_pairs={{0,4},{4,0},{1,5},{5,1},{2,6},{6,2},{3,7},{7,3},{8,12},{12,8},{9,1... | collective-permute-start | bytes 884744 | tf_op jit(solution)/shard_map/ppermute | solution.py:12
  52.2 4.9 %collective-permute-start.4 = (f32[144,128]{1,0:T(8,128)S(1)}, f32[144,128]{1,0:T(8,128)S(1)}, u32[]{:S(2)}, u32[]{:S(2)}) collective-permute-start(f32[144,128]{1,0:T(8,128)S(1)} %get-tuple-element.8), channel_id=1, source_target_pairs={{0,64},{64,128},{128,192},{192,0},{1,65},{65,129},{129,193},{193,1... | collective-permute-start | bytes 221192 | tf_op jit(solution)/shard_map/ppermute | solution.py:12
  53.4 5.8 %collective-permute-start.5 = (f32[144,128]{1,0:T(8,128)S(1)}, f32[144,128]{1,0:T(8,128)S(1)}, u32[]{:S(2)}, u32[]{:S(2)}) collective-permute-start(f32[144,128]{1,0:T(8,128)S(1)} %get-tuple-element.10), channel_id=1, source_target_pairs={{0,128},{64,192},{128,0},{192,64},{1,129},{65,193},{129,1},{193,65... | collective-permute-start | bytes 221192 | tf_op jit(solution)/shard_map/ppermute | solution.py:12
  55.9 3.5 %collective-permute-start.6 = (f32[144,128]{1,0:T(8,128)S(1)}, f32[144,128]{1,0:T(8,128)S(1)}, u32[]{:S(2)}, u32[]{:S(2)}) collective-permute-start(f32[144,128]{1,0:T(8,128)S(1)} %get-tuple-element.9), channel_id=1, source_target_pairs={{0,192},{64,0},{128,64},{192,128},{1,193},{65,1},{129,65},{193,129... | collective-permute-start | bytes 221192 | tf_op jit(solution)/shard_map/ppermute | solution.py:12
  85.5 5.3 %collective-permute-start.7 = (f32[144,128]{0,1:T(8,128)S(1)}, f32[144,128]{0,1:T(8,128)S(1)}, u32[]{:S(2)}, u32[]{:S(2)}) collective-permute-start(f32[144,128]{0,1:T(8,128)S(1)} %copy.14), channel_id=1, source_target_pairs={{0,64},{64,128},{128,192},{192,0},{1,65},{65,129},{129,193},{193,1... | collective-permute-start | bytes 221192 | tf_op jit(solution)/shard_map/ppermute | solution.py:12
  85.6 6.8 %collective-permute-start.8 = (f32[144,128]{0,1:T(8,128)S(1)}, f32[144,128]{0,1:T(8,128)S(1)}, u32[]{:S(2)}, u32[]{:S(2)}) collective-permute-start(f32[144,128]{0,1:T(8,128)S(1)} %copy.14), channel_id=1, source_target_pairs={{0,128},{64,192},{128,0},{192,64},{1,129},{65,193},{129,1},{193,65... | collective-permute-start | bytes 221192 | tf_op jit(solution)/shard_map/ppermute | solution.py:12
  88.7 4.8 %collective-permute-start.9 = (f32[144,128]{0,1:T(8,128)S(1)}, f32[144,128]{0,1:T(8,128)S(1)}, u32[]{:S(2)}, u32[]{:S(2)}) collective-permute-start(f32[144,128]{0,1:T(8,128)S(1)} %copy.14), channel_id=1, source_target_pairs={{0,192},{64,0},{128,64},{192,128},{1,193},{65,1},{129,65},{193,129... | collective-permute-start | bytes 221192 | tf_op jit(solution)/shard_map/ppermute | solution.py:12
  94.8 8.7 %collective-permute-start.10 = (f32[576,128]{0,1:T(8,128)S(1)}, f32[576,128]{0,1:T(8,128)S(1)}, u32[]{:S(2)}, u32[]{:S(2)}) collective-permute-start(f32[576,128]{0,1:T(8,128)S(1)} %dynamic_update_slice.37), channel_id=1, source_target_pairs={{0,4},{4,0},{1,5},{5,1},{2,6},{6,2},{3,7},{7,3},{8,12},{12,8},{9,1... | collective-permute-start | bytes 884744 | tf_op jit(solution)/shard_map/ppermute | solution.py:12
  131.0 5.4 %collective-permute-start.11 = (f32[128,128]{0,1:T(8,128)S(1)}, f32[128,128]{0,1:T(8,128)S(1)}, u32[]{:S(2)}, u32[]{:S(2)}) collective-permute-start(f32[128,128]{0,1:T(8,128)S(1)} %fusion.13), channel_id=1, source_target_pairs={{0,1},{1,2},{2,3},{3,0},{4,5},{5,6},{6,7},{7,4},{8,9},{9,10},{10,1... | collective-permute-start | bytes 196616 | tf_op jit(solution)/shard_map/ppermute | solution.py:12
  131.1 6.9 %collective-permute-start.12 = (f32[128,128]{0,1:T(8,128)S(1)}, f32[128,128]{0,1:T(8,128)S(1)}, u32[]{:S(2)}, u32[]{:S(2)}) collective-permute-start(f32[128,128]{0,1:T(8,128)S(1)} %fusion.13), channel_id=1, source_target_pairs={{0,2},{1,3},{2,0},{3,1},{4,6},{5,7},{6,4},{7,5},{8,10},{9,11},{10,... | collective-permute-start | bytes 196616 | tf_op jit(solution)/shard_map/ppermute | solution.py:12
  134.4 3.6 %collective-permute-start.13 = (f32[128,128]{0,1:T(8,128)S(1)}, f32[128,128]{0,1:T(8,128)S(1)}, u32[]{:S(2)}, u32[]{:S(2)}) collective-permute-start(f32[128,128]{0,1:T(8,128)S(1)} %fusion.13), channel_id=1, source_target_pairs={{0,3},{1,0},{2,1},{3,2},{4,7},{5,4},{6,5},{7,6},{8,11},{9,8},{10,9... | collective-permute-start | bytes 196616 | tf_op jit(solution)/shard_map/ppermute | solution.py:12

commit v2 on v0

v2 whole, which is shorter than its diff:
```python
import functools

import jax
import jax.numpy as jnp
from jax import lax
from jax.experimental import pallas as pl
from jax.experimental.pallas import tpu as pltpu
from jax.sharding import Mesh, PartitionSpec as P

F32 = jnp.float32
BF16 = jnp.bfloat16
K = 128
NB = 16
VMEM_LIMIT = 24 * 2**20
HIGHEST = lax.Precision.HIGHEST
TN = (((0,), (0,)), ((), ()))
NT = (((1,), (1,)), ((), ()))
NN = (((1,), (0,)), ((), ()))


def dot(a, b, dims, precision=None):
    return lax.dot_general(a, b, dims, precision=precision, preferred_element_type=F32)


def scalars(*values):
    return jnp.stack([jnp.asarray(v, jnp.int32) for v in values])


def vmem():
    return pl.BlockSpec(memory_space=pltpu.VMEM)


def smem():
    return pl.BlockSpec(memory_space=pltpu.SMEM)


def params():
    return pltpu.CompilerParams(vmem_limit_bytes=VMEM_LIMIT)


def cost(flops, moved):
    return pl.CostEstimate(flops=flops, bytes_accessed=moved, transcendentals=0)


def halves(x):
    high = x.astype(BF16)
    return high, (x - high.astype(F32)).astype(BF16)


def thirds(x):
    high = x.astype(BF16).astype(F32)
    mid = (x - high).astype(BF16).astype(F32)
    return high, mid, x - high - mid


CHUNKS = 2


def start_copies(a_ref, buf_ref, sems, boxes):
    copies = []
    for i, (rows, cols, at) in enumerate(boxes):
        copy = pltpu.make_async_copy(a_ref.at[rows, cols], buf_ref.at[at, cols], sems.at[i])
        copy.start()
        copies.append(copy)
    return copies


def sketch_kernel(count, where_ref, a_ref, b_ref, *refs):
    o_refs, (w_ref, basis_ref, buf_ref, sems, basis_sem) = refs[:count], refs[count:]
    rows, snaps = o_refs[0].shape[0], a_ref.shape[1]
    step = rows // CHUNKS
    basis_copy = pltpu.make_async_copy(b_ref, basis_ref, basis_sem)
    basis_copy.start()
    boxes = []
    for i in range(count * CHUNKS):
        at = pl.multiple_of(where_ref[i // CHUNKS] * rows + i % CHUNKS * step, step)
        boxes.append((pl.ds(at, step), pl.ds(0, snaps), pl.ds(i * step, step)))
    copies = start_copies(a_ref, buf_ref, sems, boxes)
    basis_copy.wait()
    high, low = halves(basis_ref[...])
    w_ref[:, :K] = high
    w_ref[:, K:] = low
    for i in range(count * CHUNKS):
        copies[i].wait()
        a_high, a_low = halves(buf_ref[i * step : (i + 1) * step, :])
        both = dot(a_high, w_ref[...], NN)
        cross = dot(a_low, w_ref[:, :K], NN)
        at = i % CHUNKS * step
        o_refs[i // CHUNKS][at : at + step, :] = both[:, :K] + (both[:, K:] + cross)


def sketch_pieces(a, b, where):
    rows, snaps = a.shape[0] // 4, a.shape[1]
    count = len(where)
    return pl.pallas_call(
        functools.partial(sketch_kernel, count),
        in_specs=[smem()] + [pl.BlockSpec(memory_space=pltpu.HBM)] * 2,
        out_specs=[vmem()] * count,
        out_shape=[jax.ShapeDtypeStruct((rows, K), F32)] * count,
        scratch_shapes=[
            pltpu.VMEM((snaps, 2 * K), BF16),
            pltpu.VMEM((snaps, K), F32),
            pltpu.VMEM((count * rows, snaps), F32),
            pltpu.SemaphoreType.DMA((count * CHUNKS,)),
            pltpu.SemaphoreType.DMA,
        ],
        compiler_params=params(),
        cost_estimate=cost(6 * count * rows * snaps * K, 4 * (count * rows + K) * snaps),
        name="sketch_pieces",
    )(scalars(*where), a, b)


def raw_kernel(count, earlier, last, where_ref, a_ref, *refs):
    refs = list(refs)
    take = lambda n: [refs.pop(0) for _ in range(n)]
    s_refs = take(count)
    prev_refs = take(1 if earlier else 0)
    gram_refs = take(earlier if last else 0)
    rows, snaps = s_refs[0].shape[0], a_ref.shape[1]
    half = snaps // 2
    if last:
        o_ref, slot_ref, both_ref, buf_ref, sems = refs
    else:
        o_ref, *g_refs = take(1 + count)
        buf_ref, sems = refs
    boxes = []
    for j in range(2):
        for i in range(count):
            at = pl.multiple_of(where_ref[i] * rows, rows)
            boxes.append((pl.ds(at, rows), pl.ds(j * half, half), pl.ds(i * rows, rows)))
    copies = start_copies(a_ref, buf_ref, sems, boxes)
    for i in range(count):
        s = s_refs[i][...]
        gram = dot(s, s, TN, HIGHEST)
        if last:
            slot_ref[where_ref[i]] = gram
        else:
            g_refs[i][...] = gram
    if last:
        for i in range(earlier):
            slot_ref[where_ref[count + i]] = gram_refs[i][...]
        gram = ((slot_ref[0] + slot_ref[1]) + slot_ref[2]) + slot_ref[3]
        for j in range(8):
            o_ref[j // 4, j % 4, K:, :] = gram[16 * j : 16 * j + 16, :]
    for j in range(2):
        cols = slice(j * half, (j + 1) * half)
        for i in range(count):
            high, low = halves(s_refs[i][...])
            copies[j * count + i].wait()
            a_high, a_low = halves(buf_ref[i * rows : (i + 1) * rows, cols])
            both = dot(jnp.concatenate([high, low], 1), a_high, TN)
            cross = dot(high, a_low, TN)
            if last:
                both_ref[:, cols] = both
                both_ref[:K, cols] = both_ref[:K, cols] + (both_ref[K:, cols] + cross)
                for k in range(4):
                    at = slice(j * half + k * K, j * half + (k + 1) * K)
                    o_ref[j, k, :K, :] = prev_refs[0][:, at] + both_ref[:K, at]
            else:
                total = both[:K] + (both[K:] + cross)
                if i > 0:
                    total = o_ref[:, cols] + total
                elif earlier:
                    total = prev_refs[0][:, cols] + total
                o_ref[:, cols] = total


def raw_pieces(a, pieces, where, prev=None, grams=(), last=False):
    count, earlier = len(pieces), len(grams)
    rows, snaps = pieces[0].shape[0], a.shape[1]
    args = list(pieces) + ([prev] if earlier else []) + (list(grams) if last else [])
    scratch = [
        pltpu.VMEM((count * rows, snaps), F32),
        pltpu.SemaphoreType.DMA((2 * count,)),
    ]
    if last:
        out_shape = [jax.ShapeDtypeStruct((2, 4, K + 16, K), F32)]
        scratch = [pltpu.VMEM((4, K, K), F32), pltpu.VMEM((2 * K, snaps), F32)] + scratch
    else:
        out_shape = [jax.ShapeDtypeStruct((K, snaps), F32)]
        out_shape += [jax.ShapeDtypeStruct((K, K), F32)] * count
    return pl.pallas_call(
        functools.partial(raw_kernel, count, earlier, last),
        in_specs=[smem(), pl.BlockSpec(memory_space=pltpu.HBM)] + [vmem()] * len(args),
        out_specs=[vmem()] * len(out_shape),
        out_shape=out_shape,
        scratch_shapes=scratch,
        compiler_params=params(),
        cost_estimate=cost(6 * count * rows * snaps * K, 4 * (count * rows + 2 * K) * snaps),
        name="raw_pieces",
    )(where, a, *args)


def inverse_factor(w_ref, o_ref):
    lane = lax.broadcasted_iota(jnp.int32, (NB, K), 1)
    row = lax.broadcasted_iota(jnp.int32, (NB, K), 0)
    for lo in range(0, K, NB):
        hi = lo + NB
        block = w_ref[lo:hi, :]
        cols = [jnp.broadcast_to(block[:, lo + c : lo + c + 1], (NB, K)) for c in range(NB)]
        inv = [jnp.where(row == c, 1.0, 0.0) for c in range(NB)]
        for k in range(NB):
            pivot = cols[k][k : k + 1, :]
            r = lax.rsqrt(pivot)
            r = r * (1.5 - 0.5 * (pivot * r) * r)
            m = jnp.where(row > k, cols[k] * r, 0.0)
            for c in range(k + 1, NB):
                cols[c] = cols[c] - m * (cols[c][k : k + 1, :] * r)
            for c in range(k + 1):
                scaled = inv[c][k : k + 1, :] * r
                inv[c] = jnp.where(row == k, scaled, inv[c] - m * scaled)
        inside = (lane >= lo) & (lane < hi)
        block = jnp.where(inside, jnp.where(lane - lo == row, 1.0, 0.0), block)
        done = inv[0] * block[0:1, :]
        for c in range(1, NB):
            done = done + inv[c] * block[c : c + 1, :]
        o_ref[lo:hi, :] = jnp.where(lane < hi, done, 0.0)
        if hi < K:
            h, m, l = thirds(done)
            left = jnp.concatenate([h, h, m, h, l, m], 0).astype(BF16)
            right = jnp.concatenate([h, m, h, l, h, m], 0).astype(BF16)
            update = dot(left, right, TN)
            below = lax.broadcasted_iota(jnp.int32, (K - hi, K), 1)
            inside = (below >= lo) & (below < hi)
            w_ref[hi:, :] = jnp.where(inside, 0.0, w_ref[hi:, :]) - update[hi:, :]


def middle_kernel(where_ref, mine_ref, other_ref, inv_ref, back_ref, gram_ref, w_ref, raw_ref):
    x, c = where_ref[0], where_ref[1]
    for half, ref in ((c, mine_ref), (1 - c, other_ref)):
        for shift in range(4):
            at = half * 4 + (x + 4 - shift) % 4
            raw_ref[:, pl.ds(pl.multiple_of(at * K, K), K)] = ref[shift, :K, :]
            w_ref[pl.ds(pl.multiple_of(at * 16, 16), 16), :] = ref[shift, K:, :]
    inverse_factor(w_ref, inv_ref)
    back = dot(inv_ref[...], raw_ref[...], NN, HIGHEST)
    back_ref[...] = back
    gram_ref[...] = dot(back, back, NT, HIGHEST)


def middle(where, mine, other):
    snaps = 8 * K
    return pl.pallas_call(
        middle_kernel,
        in_specs=[smem(), vmem(), vmem()],
        out_specs=[vmem()] * 3,
        out_shape=[
            jax.ShapeDtypeStruct((K, K), F32),
            jax.ShapeDtypeStruct((K, snaps), F32),
            jax.ShapeDtypeStruct((K, K), F32),
        ],
        scratch_shapes=[pltpu.VMEM((K, K), F32), pltpu.VMEM((K, snaps), F32)],
        compiler_params=params(),
        cost_estimate=cost(24 * snaps * K * K, 8 * snaps * K),
        name="middle",
    )(where, mine, other)


def space_kernel(where_ref, inv_ref, back_t_ref, *refs):
    s_refs, (o_ref, back_ref) = refs[:4], refs[4:]
    rows = s_refs[0].shape[0]
    inv = inv_ref[...]
    for i, ref in enumerate(s_refs):
        at = pl.multiple_of(where_ref[i] * rows, rows)
        o_ref[pl.ds(at, rows), :] = dot(ref[...], inv, NT, HIGHEST)
    back_ref[...] = back_t_ref[...].T


def space(where, inv, back_t, pieces):
    rows = 4 * pieces[0].shape[0]
    snaps = back_t.shape[1]
    return pl.pallas_call(
        space_kernel,
        in_specs=[smem()] + [vmem()] * 6,
        out_specs=[vmem()] * 2,
        out_shape=[jax.ShapeDtypeStruct((rows, K), F32), jax.ShapeDtypeStruct((snaps, K), F32)],
        compiler_params=params(),
        cost_estimate=cost(12 * rows * K * K, 8 * (rows + snaps) * K),
        name="space",
    )(where, inv, back_t, *pieces)


def time_kernel(where_ref, back_ref, *refs):
    gram_refs, (o_ref, slot_ref, w_ref, inv_ref) = refs[:4], refs[4:]
    for i, ref in enumerate(gram_refs):
        slot_ref[where_ref[i]] = ref[...]
    w_ref[...] = ((slot_ref[0] + slot_ref[1]) + slot_ref[2]) + slot_ref[3]
    inverse_factor(w_ref, inv_ref)
    o_ref[...] = dot(back_ref[...], inv_ref[...], NT, HIGHEST)


def time_basis_of(where, back, grams):
    return pl.pallas_call(
        time_kernel,
        in_specs=[smem()] + [vmem()] * 5,
        out_specs=vmem(),
        out_shape=jax.ShapeDtypeStruct(back.shape, F32),
        scratch_shapes=[
            pltpu.VMEM((4, K, K), F32),
            pltpu.VMEM((K, K), F32),
            pltpu.VMEM((K, K), F32),
        ],
        compiler_params=params(),
        cost_estimate=cost(12 * back.shape[0] * K * K, 8 * back.shape[0] * K),
        name="time_basis",
    )(where, back, *grams)


def shifted(value, axis, shift):
    n = lax.axis_size(axis)
    return lax.ppermute(value, axis, [(i, (i + shift) % n) for i in range(n)])


def pick(value, index):
    return lax.dynamic_index_in_dim(value, index, 0, keepdims=False)


def on_device(anomalies, start_basis):
    x, c, y = lax.axis_index("x"), lax.axis_index("c"), lax.axis_index("y")
    owner = [y, (y + 3) % 4, (y + 2) % 4, (y + 1) % 4]

    anomalies = pltpu.with_memory_space_constraint(anomalies, pltpu.HBM)
    start_basis = pltpu.with_memory_space_constraint(start_basis, pltpu.HBM)
    (p2,) = sketch_pieces(anomalies, start_basis, [(y + 2) % 4])
    r2 = shifted(p2, "y", 2)
    p1, p3, p0 = sketch_pieces(anomalies, start_basis, [(y + 1) % 4, (y + 3) % 4, y])
    r1, r3 = shifted(p1, "y", 1), shifted(p3, "y", 3)
    own = p0 + r2 + r1 + r3
    s2, s1, s3 = (shifted(own, "y", shift) for shift in (2, 1, 3))
    raw, g0 = raw_pieces(anomalies, [own], scalars(owner[0]))
    raw, g1, g3 = raw_pieces(anomalies, [s1, s3], scalars(owner[1], owner[3]), raw, [g0])
    (stacked,) = raw_pieces(
        anomalies, [s2], scalars(owner[2], owner[0], owner[1], owner[3]), raw, [g0, g1, g3], True
    )

    part = pick(stacked, c) + shifted(pick(stacked, 1 - c), "c", 1)
    arrived = [shifted(pick(part, (x + shift) % 4), "x", shift) for shift in (2, 1, 3)]
    part = pick(part, x) + arrived[0] + arrived[1] + arrived[2]
    copies = jnp.broadcast_to(part[None], (8,) + part.shape)
    part = jnp.sum(lax.all_to_all(copies, "z", 0, 0), 0)
    e2, e1, e3 = (shifted(part, "x", shift) for shift in (2, 1, 3))
    mine = jnp.stack([part, e1, e2, e3])
    other = shifted(mine, "c", 1)
    inv, back_t, gram = middle(scalars(x, c), mine, other)

    t2, t1, t3 = (shifted(gram, "y", shift) for shift in (2, 1, 3))
    space_basis, back = space(scalars(*owner), inv, back_t, (own, s1, s2, s3))
    time_basis = time_basis_of(scalars(*owner), back, (gram, t1, t2, t3))
    return (space_basis, time_basis)


def solution(mesh):
    split = Mesh(mesh.devices.reshape(4, 8, 2, 4), ("x", "z", "c", "y"))
    rows = ("x", "z", "c")
    return jax.shard_map(
        on_device,
        mesh=split,
        in_specs=(P(rows, "y"), P("y", None)),
        out_specs=(P(rows, None), P("y", None)),
        check_vma=False,
    )
```

time: 540 us -> 112 us (0.21)
  waiting for transfers between devices: 444 us -> 24.3 us
  other arithmetic: 47.4 us -> 0.58 us
  Pallas kernels: 0 us -> 30.9 us
  starting transfers between devices: 0.56 us -> 31.1 us
  matrix products: 29.4 us -> 0 us
  blocking collectives: 0 us -> 23.7 us
  between operations: 13.8 us -> 0.76 us
    psum x4 -> x0, waiting for transfers between devices: 444 us -> none  [the longest x1 176 us: on_device(): back = lax.psum(partial_back, 'row')]
    another operation x10 -> x6, other arithmetic: 45.7 us -> 0.41 us  [the longest x5 0.38 us: scalars(): return jnp.stack([jnp.asarray(v, jnp.int32) for v in values])]
    ppermute x0 -> x17, starting transfers between devices: none -> 31.1 us  [shifted(): return lax.ppermute(value, axis, [(i, (i + shift) % n) for i in range(n)])]
    pallas_call x0 -> x8, Pallas kernels: none -> 30.9 us  [the longest x3 8.42 us: raw_pieces(): pl.pallas_call(functools.partial(raw_kernel, count, earlier, last), in_sp...]
    dot_general x4 -> x0, matrix products: 24.4 us -> none  [the longest x1 9.82 us: on_device(): jnp.dot(anomalies, start_basis, precision=lax.Precision.HIGHEST, preferre...]
    ppermute x0 -> x17, waiting for transfers between devices: none -> 24.3 us  [shifted(): return lax.ppermute(value, axis, [(i, (i + shift) % n) for i in range(n)])]
    all_to_all x0 -> x1, blocking collectives: none -> 23.7 us  [on_device(): part = jnp.sum(lax.all_to_all(copies, 'z', 0, 0), 0)]
  transfers between devices with their start and end apart: 4 -> 17, of which waited for: 4 -> 12; matrix products, arithmetic and copies ran while one was open for 0% -> 0% of each run, Pallas kernels for 0% -> 13%
where the time goes in v2:
time: 112 us; the launch traced here: 111 us
  starting transfers between devices  31.1 us (28%)
  Pallas kernels  30.9 us (28%)
  waiting for transfers between devices  24.3 us (22%)
  blocking collectives  23.7 us (21%)
    ppermute x17, starting transfers between devices, shifted(): return lax.ppermute(value, axis, [(i, (i + shift) % n) for i in range(n)])  31.1 us
    ppermute x17, waiting for transfers between devices, shifted(): return lax.ppermute(value, axis, [(i, (i + shift) % n) for i in range(n)])  24.3 us
    all_to_all x1, blocking collectives, on_device(): part = jnp.sum(lax.all_to_all(copies, 'z', 0, 0), 0)  23.7 us
    pallas_call x3, Pallas kernels, raw_pieces(): pl.pallas_call(functools.partial(raw_kernel, count, earlier, last), in_sp...  8.42 us
    pallas_call x2, Pallas kernels, sketch_pieces(): pl.pallas_call(functools.partial(sketch_kernel, count), in_specs=[smem()]...  8 us
    pallas_call x1, Pallas kernels, time_basis_of(): pl.pallas_call(time_kernel, in_specs=[smem()] + [vmem()] * 5, out_specs=v...  6.02 us
    pallas_call x1, Pallas kernels, middle(): pl.pallas_call(middle_kernel, in_specs=[smem(), vmem(), vmem()], out_spec...  5.93 us
    pallas_call x1, Pallas kernels, space(): pl.pallas_call(space_kernel, in_specs=[smem()] + [vmem()] * 6, out_specs=...  2.54 us
  transfers between devices with their start and end apart: 17, of which 12 were waited for; matrix products, arithmetic and copies ran while one was open for 0% of the time, Pallas kernels for 13%

profile of v2, /device:TPU:1, one launch (start us, length us, event | category | flops | bytes accessed | tf_op | source)
XLA Modules:
  0.0 111.4 jit_solution(10891082875083285890)
XLA Ops:
  0.6 2.4 %sketch_pieces.3 = f32[512,128]{1,0:T(8,128)S(1)} custom-call(s32[1]{0:T(128)} %bitcast.2.where_ref, f32[2048,1024]{1,0:T(8,128)} %a_ref.9, f32[1024,128]{1,0:T(8,128)} %b_ref.3), custom_call_target="tpu_custom_call" | custom-call | flops 402653184 | bytes 2621440 | tf_op jit(solution)/shard_map/sketch_pieces/pallas_call | solution.py:95
  3.0 3.8 %collective-permute-start = (f32[512,128]{1,0:T(8,128)S(1)}, f32[512,128]{1,0:T(8,128)S(1)}, u32[]{:S(2)}, u32[]{:S(2)}) collective-permute-start(f32[512,128]{1,0:T(8,128)S(1)} %sketch_pieces.3), channel_id=1, source_target_pairs={{0,2},{1,3},{2,0},{3,1},{4,6},{5,7},{6,4},{7,5},{8,10},{9,11},{10,... | collective-permute-start | bytes 786440 | tf_op jit(solution)/shard_map/ppermute | solution.py:311
  6.9 5.6 %sketch_pieces.2 = (f32[512,128]{1,0:T(8,128)S(1)}, f32[512,128]{1,0:T(8,128)S(1)}, f32[512,128]{1,0:T(8,128)S(1)}) custom-call(s32[3]{0:T(128)S(1)} %pad_add_fusion.1.where_ref, f32[2048,1024]{1,0:T(8,128)} %a_ref.9, f32[1024,128]{1,0:T(8,128)} %b_ref.3), custom_call_target="tpu_custom_call" | custom-call | flops 1207959552 | bytes 6815744 | tf_op jit(solution)/shard_map/sketch_pieces/pallas_call | solution.py:95
  13.0 2.3 %collective-permute-start.2 = (f32[512,128]{1,0:T(8,128)S(1)}, f32[512,128]{1,0:T(8,128)S(1)}, u32[]{:S(2)}, u32[]{:S(2)}) collective-permute-start(f32[512,128]{1,0:T(8,128)S(1)} %get-tuple-element.17), channel_id=1, source_target_pairs={{0,3},{1,0},{2,1},{3,2},{4,7},{5,4},{6,5},{7,6},{8,11},{9,8},{10,9... | collective-permute-start | bytes 786440 | tf_op jit(solution)/shard_map/ppermute | solution.py:311
  15.3 5.4 %collective-permute-done.1 = f32[512,128]{1,0:T(8,128)S(1)} collective-permute-done((f32[512,128]{1,0:T(8,128)S(1)}, f32[512,128]{1,0:T(8,128)S(1)}, u32[]{:S(2)}, u32[]{:S(2)}) %collective-permute-start.1) | collective-permute-done | bytes 262176 | tf_op jit(solution)/shard_map/ppermute | solution.py:311
  20.8 2.5 %collective-permute-start.5 = (f32[512,128]{1,0:T(8,128)S(1)}, f32[512,128]{1,0:T(8,128)S(1)}, u32[]{:S(2)}, u32[]{:S(2)}) collective-permute-start(f32[512,128]{1,0:T(8,128)S(1)} %add_add_fusion.refs_0_), channel_id=1, source_target_pairs={{0,3},{1,0},{2,1},{3,2},{4,7},{5,4},{6,5},{7,6},{8,11},{9,8},{10,9... | collective-permute-start | bytes 786440 | tf_op jit(solution)/shard_map/ppermute | solution.py:311
  23.3 1.3 %collective-permute-start.3 = (f32[512,128]{1,0:T(8,128)S(1)}, f32[512,128]{1,0:T(8,128)S(1)}, u32[]{:S(2)}, u32[]{:S(2)}) collective-permute-start(f32[512,128]{1,0:T(8,128)S(1)} %add_add_fusion.refs_0_), channel_id=1, source_target_pairs={{0,2},{1,3},{2,0},{3,1},{4,6},{5,7},{6,4},{7,5},{8,10},{9,11},{10,... | collective-permute-start | bytes 786440 | tf_op jit(solution)/shard_map/ppermute | solution.py:311
  24.7 2.1 %raw_pieces.3 = (f32[128,1024]{1,0:T(8,128)S(1)}, f32[128,128]{1,0:T(8,128)S(1)}) custom-call(s32[1]{0:T(128)} %bitcast.where_ref, f32[2048,1024]{1,0:T(8,128)} %a_ref.9, f32[512,128]{1,0:T(8,128)S(1)} %add_add_fusion.refs_0_), custom_call_target="tpu_custom_call" | custom-call | flops 402653184 | bytes 3145728 | tf_op jit(solution)/shard_map/raw_pieces/pallas_call | solution.py:182
  26.8 5.5 %collective-permute-done.4.refs_0_.refs_1_ = f32[512,128]{1,0:T(8,128)S(1)} collective-permute-done((f32[512,128]{1,0:T(8,128)S(1)}, f32[512,128]{1,0:T(8,128)S(1)}, u32[]{:S(2)}, u32[]{:S(2)}) %collective-permute-start.4) | collective-permute-done | bytes 262176 | tf_op jit(solution)/shard_map/ppermute | solution.py:311
  32.3 3.7 %raw_pieces.4 = (f32[128,1024]{1,0:T(8,128)S(1)}, f32[128,128]{1,0:T(8,128)S(1)}, f32[128,128]{1,0:T(8,128)S(1)}) custom-call(s32[2]{0:T(128)S(1)} %pad_add_fusion.2.where_ref, f32[2048,1024]{1,0:T(8,128)} %a_ref.9, f32[512,128]{1,0:T(8,128)S(1)} %collective-permute-done.4.refs_0_.refs_1_, f32[512,128]{1,0:T(8,128)S(1)} %collective-permute-done.5.refs_1_.refs_3_, ...), custom_call_target="tpu_custom_call" | custom-call | flops 805306368 | bytes 5242880 | tf_op jit(solution)/shard_map/raw_pieces/pallas_call | solution.py:182
  36.1 2.6 %raw_pieces.5 = f32[2,4,144,128]{3,2,1,0:T(8,128)S(1)} custom-call(s32[4]{0:T(128)S(1)} %add_add_fusion.2.where_ref, f32[2048,1024]{1,0:T(8,128)} %a_ref.9, f32[512,128]{1,0:T(8,128)S(1)} %collective-permute-done.3.refs_0_.refs_2_, f32[128,1024]{1,0:T(8,128)S(1)} %get-tuple-element.19.refs_1_, f32[128,128]{1,0:T(8,128)S(1)} %get-tuple-element.20.refs_2_, ...), custom_call_target="tpu_custom_call" | custom-call | flops 402653184 | bytes 3145728 | tf_op jit(solution)/shard_map/raw_pieces/pallas_call | solution.py:182
  38.7 6.8 %collective-permute-start.6 = (f32[4,144,128]{2,1,0:T(8,128)S(1)}, f32[4,144,128]{2,1,0:T(8,128)S(1)}, u32[]{:S(2)}, u32[]{:S(2)}) collective-permute-start(f32[4,144,128]{2,1,0:T(8,128)S(1)} %dynamic-slice_bitcast_fusion), channel_id=1, source_target_pairs={{0,4},{4,0},{1,5},{5,1},{2,6},{6,2},{3,7},{7,3},{8,12},{12,8},{9,1... | collective-permute-start | bytes 884744 | tf_op jit(solution)/shard_map/ppermute | solution.py:311
  45.5 1.2 %collective-permute-done.6 = f32[4,144,128]{2,1,0:T(8,128)S(1)} collective-permute-done((f32[4,144,128]{2,1,0:T(8,128)S(1)}, f32[4,144,128]{2,1,0:T(8,128)S(1)}, u32[]{:S(2)}, u32[]{:S(2)}) %collective-permute-start.6) | collective-permute-done | bytes 294944 | tf_op jit(solution)/shard_map/ppermute | solution.py:311
  46.8 2.8 %collective-permute-start.7 = (f32[144,128]{1,0:T(8,128)S(1)}, f32[144,128]{1,0:T(8,128)S(1)}, u32[]{:S(2)}, u32[]{:S(2)}) collective-permute-start(f32[144,128]{1,0:T(8,128)S(1)} %get-tuple-element.28), channel_id=1, source_target_pairs={{0,128},{64,192},{128,0},{192,64},{1,129},{65,193},{129,1},{193,65... | collective-permute-start | bytes 221192 | tf_op jit(solution)/shard_map/ppermute | solution.py:311
  49.6 0.9 collective-permute-start.9
  50.5 0.6 collective-permute-start.8
  51.5 2.1 %collective-permute-done.9 = f32[144,128]{1,0:T(8,128)S(1)} collective-permute-done((f32[144,128]{1,0:T(8,128)S(1)}, f32[144,128]{1,0:T(8,128)S(1)}, u32[]{:S(2)}, u32[]{:S(2)}) %collective-permute-start.9) | collective-permute-done | bytes 73760 | tf_op jit(solution)/shard_map/ppermute | solution.py:311
  53.7 1.2 %collective-permute-done.8 = f32[144,128]{1,0:T(8,128)S(1)} collective-permute-done((f32[144,128]{1,0:T(8,128)S(1)}, f32[144,128]{1,0:T(8,128)S(1)}, u32[]{:S(2)}, u32[]{:S(2)}) %collective-permute-start.8) | collective-permute-done | bytes 73760 | tf_op jit(solution)/shard_map/ppermute | solution.py:311
  54.9 23.7 %all_to_all.5 = f32[8,144,128]{2,1,0:T(8,128)S(1)} all-to-all(f32[8,144,128]{2,1,0:T(8,128)S(1)} %broadcast_in_dim.2), channel_id=1, replica_groups=mesh['x'=4,'z'=8,'c'=2,'y'=4] {'z'}, dimensions={0} | all-to-all | bytes 1179648 | tf_op jit(solution)/shard_map/all_to_all | solution.py:340
  78.7 3.1 %collective-permute-start.12 = (f32[144,128]{1,0:T(8,128)S(1)}, f32[144,128]{1,0:T(8,128)S(1)}, u32[]{:S(2)}, u32[]{:S(2)}) collective-permute-start(f32[144,128]{1,0:T(8,128)S(1)} %reduce_sum.9), channel_id=1, source_target_pairs={{0,192},{64,0},{128,64},{192,128},{1,193},{65,1},{129,65},{193,129... | collective-permute-start | bytes 221192 | tf_op jit(solution)/shard_map/ppermute | solution.py:311
  82.0 0.7 collective-permute-start.10
  82.7 0.5 collective-permute-done.12
  83.2 3.4 %collective-permute-done.11 = f32[144,128]{1,0:T(8,128)S(1)} collective-permute-done((f32[144,128]{1,0:T(8,128)S(1)}, f32[144,128]{1,0:T(8,128)S(1)}, u32[]{:S(2)}, u32[]{:S(2)}) %collective-permute-start.11) | collective-permute-done | bytes 73760 | tf_op jit(solution)/shard_map/ppermute | solution.py:311
  86.6 0.6 collective-permute-done.10
  87.2 4.2 %collective-permute-start.13 = (f32[4,144,128]{2,1,0:T(8,128)S(1)}, f32[4,144,128]{2,1,0:T(8,128)S(1)}, u32[]{:S(2)}, u32[]{:S(2)}) collective-permute-start(f32[4,144,128]{2,1,0:T(8,128)S(1)} %pad_maximum_fusion.mine_ref), channel_id=1, source_target_pairs={{0,4},{4,0},{1,5},{5,1},{2,6},{6,2},{3,7},{7,3},{8,12},{12,8},{9,1... | collective-permute-start | bytes 884744 | tf_op jit(solution)/shard_map/ppermute | solution.py:311
  91.5 1.1 %collective-permute-done.13.other_ref = f32[4,144,128]{2,1,0:T(8,128)S(1)} collective-permute-done((f32[4,144,128]{2,1,0:T(8,128)S(1)}, f32[4,144,128]{2,1,0:T(8,128)S(1)}, u32[]{:S(2)}, u32[]{:S(2)}) %collective-permute-start.13) | collective-permute-done | bytes 294944 | tf_op jit(solution)/shard_map/ppermute | solution.py:311
  92.6 5.9 %middle.1 = (f32[128,128]{1,0:T(8,128)S(1)}, f32[128,1024]{1,0:T(8,128)S(1)}, f32[128,128]{1,0:T(8,128)S(1)}) custom-call(s32[2]{0:T(128)S(1)} %pad_add_fusion.where_ref, f32[4,144,128]{2,1,0:T(8,128)S(1)} %pad_maximum_fusion.mine_ref, f32[4,144,128]{2,1,0:T(8,128)S(1)} %collective-permute-done.13.other_ref), custom_call_target="tpu_custom_call" | custom-call | flops 402653184 | bytes 1048576 | tf_op jit(solution)/shard_map/middle/pallas_call | solution.py:243
  98.7 1.4 %collective-permute-start.14 = (f32[128,128]{1,0:T(8,128)S(1)}, f32[128,128]{1,0:T(8,128)S(1)}, u32[]{:S(2)}, u32[]{:S(2)}) collective-permute-start(f32[128,128]{1,0:T(8,128)S(1)} %get-tuple-element.27.refs_0_), channel_id=1, source_target_pairs={{0,1},{1,2},{2,3},{3,0},{4,5},{5,6},{6,7},{7,4},{8,9},{9,10},{10,1... | collective-permute-start | bytes 196616 | tf_op jit(solution)/shard_map/ppermute | solution.py:311
  100.2 2.5 %space.1 = (f32[2048,128]{1,0:T(8,128)}, f32[1024,128]{1,0:T(8,128)S(1)}) custom-call(s32[4]{0:T(128)S(1)} %add_add_fusion.1.where_ref, f32[128,128]{1,0:T(8,128)S(1)} %get-tuple-element.23.inv_ref, f32[128,1024]{1,0:T(8,128)S(1)} %get-tuple-element.24.back_t_ref, f32[512,128]{1,0:T(8,128)S(1)} %add_add_fusion.refs_0_, ...), custom_call_target="tpu_custom_call" | custom-call | flops 402653184 | bytes 3145728 | tf_op jit(solution)/shard_map/space/pallas_call | solution.py:272
  102.7 0.6 collective-permute-done.15.refs_2_
  103.3 2.1 %collective-permute-done.14.refs_1_ = f32[128,128]{1,0:T(8,128)S(1)} collective-permute-done((f32[128,128]{1,0:T(8,128)S(1)}, f32[128,128]{1,0:T(8,128)S(1)}, u32[]{:S(2)}, u32[]{:S(2)}) %collective-permute-start.14) | collective-permute-done | bytes 65568 | tf_op jit(solution)/shard_map/ppermute | solution.py:311
  105.4 6.0 %time_basis.1 = f32[1024,128]{1,0:T(8,128)} custom-call(s32[4]{0:T(128)S(1)} %add_add_fusion.1.where_ref, f32[1024,128]{1,0:T(8,128)S(1)} %get-tuple-element.26.back_ref, f32[128,128]{1,0:T(8,128)S(1)} %get-tuple-element.27.refs_0_, f32[128,128]{1,0:T(8,128)S(1)} %collective-permute-done.14.refs_1_, f32[128,128]{1,0:T(8,128)S(1)} %collective-permute-done.15.refs_2_, ...), custom_call_target="tpu_custom_call" | custom-call | flops 201326592 | bytes 1048576 | tf_op jit(solution)/shard_map/time_basis/pallas_call | solution.py:293
  (24 shorter events, 2.0 us)
Async XLA Ops:
  3.0 12.3 %collective-permute-start = (f32[512,128]{1,0:T(8,128)S(1)}, f32[512,128]{1,0:T(8,128)S(1)}, u32[]{:S(2)}, u32[]{:S(2)}) collective-permute-start(f32[512,128]{1,0:T(8,128)S(1)} %sketch_pieces.3), channel_id=1, source_target_pairs={{0,2},{1,3},{2,0},{3,1},{4,6},{5,7},{6,4},{7,5},{8,10},{9,11},{10,... | collective-permute-start | bytes 786440 | tf_op jit(solution)/shard_map/ppermute | solution.py:311
  12.6 8.1 %collective-permute-start.1 = (f32[512,128]{1,0:T(8,128)S(1)}, f32[512,128]{1,0:T(8,128)S(1)}, u32[]{:S(2)}, u32[]{:S(2)}) collective-permute-start(f32[512,128]{1,0:T(8,128)S(1)} %get-tuple-element.16), channel_id=1, source_target_pairs={{0,1},{1,2},{2,3},{3,0},{4,5},{5,6},{6,7},{7,4},{8,9},{9,10},{10,1... | collective-permute-start | bytes 786440 | tf_op jit(solution)/shard_map/ppermute | solution.py:311
  13.0 7.7 %collective-permute-start.2 = (f32[512,128]{1,0:T(8,128)S(1)}, f32[512,128]{1,0:T(8,128)S(1)}, u32[]{:S(2)}, u32[]{:S(2)}) collective-permute-start(f32[512,128]{1,0:T(8,128)S(1)} %get-tuple-element.17), channel_id=1, source_target_pairs={{0,3},{1,0},{2,1},{3,2},{4,7},{5,4},{6,5},{7,6},{8,11},{9,8},{10,9... | collective-permute-start | bytes 786440 | tf_op jit(solution)/shard_map/ppermute | solution.py:311
  20.8 6.0 %collective-permute-start.5 = (f32[512,128]{1,0:T(8,128)S(1)}, f32[512,128]{1,0:T(8,128)S(1)}, u32[]{:S(2)}, u32[]{:S(2)}) collective-permute-start(f32[512,128]{1,0:T(8,128)S(1)} %add_add_fusion.refs_0_), channel_id=1, source_target_pairs={{0,3},{1,0},{2,1},{3,2},{4,7},{5,4},{6,5},{7,6},{8,11},{9,8},{10,9... | collective-permute-start | bytes 786440 | tf_op jit(solution)/shard_map/ppermute | solution.py:311
  23.3 9.1 %collective-permute-start.4 = (f32[512,128]{1,0:T(8,128)S(1)}, f32[512,128]{1,0:T(8,128)S(1)}, u32[]{:S(2)}, u32[]{:S(2)}) collective-permute-start(f32[512,128]{1,0:T(8,128)S(1)} %add_add_fusion.refs_0_), channel_id=1, source_target_pairs={{0,1},{1,2},{2,3},{3,0},{4,5},{5,6},{6,7},{7,4},{8,9},{9,10},{10,1... | collective-permute-start | bytes 786440 | tf_op jit(solution)/shard_map/ppermute | solution.py:311
  23.3 12.8 %collective-permute-start.3 = (f32[512,128]{1,0:T(8,128)S(1)}, f32[512,128]{1,0:T(8,128)S(1)}, u32[]{:S(2)}, u32[]{:S(2)}) collective-permute-start(f32[512,128]{1,0:T(8,128)S(1)} %add_add_fusion.refs_0_), channel_id=1, source_target_pairs={{0,2},{1,3},{2,0},{3,1},{4,6},{5,7},{6,4},{7,5},{8,10},{9,11},{10,... | collective-permute-start | bytes 786440 | tf_op jit(solution)/shard_map/ppermute | solution.py:311
  38.7 8.0 %collective-permute-start.6 = (f32[4,144,128]{2,1,0:T(8,128)S(1)}, f32[4,144,128]{2,1,0:T(8,128)S(1)}, u32[]{:S(2)}, u32[]{:S(2)}) collective-permute-start(f32[4,144,128]{2,1,0:T(8,128)S(1)} %dynamic-slice_bitcast_fusion), channel_id=1, source_target_pairs={{0,4},{4,0},{1,5},{5,1},{2,6},{6,2},{3,7},{7,3},{8,12},{12,8},{9,1... | collective-permute-start | bytes 884744 | tf_op jit(solution)/shard_map/ppermute | solution.py:311
  46.8 4.8 %collective-permute-start.7 = (f32[144,128]{1,0:T(8,128)S(1)}, f32[144,128]{1,0:T(8,128)S(1)}, u32[]{:S(2)}, u32[]{:S(2)}) collective-permute-start(f32[144,128]{1,0:T(8,128)S(1)} %get-tuple-element.28), channel_id=1, source_target_pairs={{0,128},{64,192},{128,0},{192,64},{1,129},{65,193},{129,1},{193,65... | collective-permute-start | bytes 221192 | tf_op jit(solution)/shard_map/ppermute | solution.py:311
  49.6 4.1 %collective-permute-start.9 = (f32[144,128]{1,0:T(8,128)S(1)}, f32[144,128]{1,0:T(8,128)S(1)}, u32[]{:S(2)}, u32[]{:S(2)}) collective-permute-start(f32[144,128]{1,0:T(8,128)S(1)} %get-tuple-element.29), channel_id=1, source_target_pairs={{0,192},{64,0},{128,64},{192,128},{1,193},{65,1},{129,65},{193,129... | collective-permute-start | bytes 221192 | tf_op jit(solution)/shard_map/ppermute | solution.py:311
  50.5 4.4 %collective-permute-start.8 = (f32[144,128]{1,0:T(8,128)S(1)}, f32[144,128]{1,0:T(8,128)S(1)}, u32[]{:S(2)}, u32[]{:S(2)}) collective-permute-start(f32[144,128]{1,0:T(8,128)S(1)} %get-tuple-element.30), channel_id=1, source_target_pairs={{0,64},{64,128},{128,192},{192,0},{1,65},{65,129},{129,193},{193,1... | collective-permute-start | bytes 221192 | tf_op jit(solution)/shard_map/ppermute | solution.py:311
  78.7 4.5 %collective-permute-start.12 = (f32[144,128]{1,0:T(8,128)S(1)}, f32[144,128]{1,0:T(8,128)S(1)}, u32[]{:S(2)}, u32[]{:S(2)}) collective-permute-start(f32[144,128]{1,0:T(8,128)S(1)} %reduce_sum.9), channel_id=1, source_target_pairs={{0,192},{64,0},{128,64},{192,128},{1,193},{65,1},{129,65},{193,129... | collective-permute-start | bytes 221192 | tf_op jit(solution)/shard_map/ppermute | solution.py:311
  81.8 4.8 %collective-permute-start.11 = (f32[144,128]{1,0:T(8,128)S(1)}, f32[144,128]{1,0:T(8,128)S(1)}, u32[]{:S(2)}, u32[]{:S(2)}) collective-permute-start(f32[144,128]{1,0:T(8,128)S(1)} %reduce_sum.9), channel_id=1, source_target_pairs={{0,128},{64,192},{128,0},{192,64},{1,129},{65,193},{129,1},{193,65... | collective-permute-start | bytes 221192 | tf_op jit(solution)/shard_map/ppermute | solution.py:311
  82.0 5.2 %collective-permute-start.10 = (f32[144,128]{1,0:T(8,128)S(1)}, f32[144,128]{1,0:T(8,128)S(1)}, u32[]{:S(2)}, u32[]{:S(2)}) collective-permute-start(f32[144,128]{1,0:T(8,128)S(1)} %reduce_sum.9), channel_id=1, source_target_pairs={{0,64},{64,128},{128,192},{192,0},{1,65},{65,129},{129,193},{193,1... | collective-permute-start | bytes 221192 | tf_op jit(solution)/shard_map/ppermute | solution.py:311
  87.2 5.4 %collective-permute-start.13 = (f32[4,144,128]{2,1,0:T(8,128)S(1)}, f32[4,144,128]{2,1,0:T(8,128)S(1)}, u32[]{:S(2)}, u32[]{:S(2)}) collective-permute-start(f32[4,144,128]{2,1,0:T(8,128)S(1)} %pad_maximum_fusion.mine_ref), channel_id=1, source_target_pairs={{0,4},{4,0},{1,5},{5,1},{2,6},{6,2},{3,7},{7,3},{8,12},{12,8},{9,1... | collective-permute-start | bytes 884744 | tf_op jit(solution)/shard_map/ppermute | solution.py:311
  98.5 4.2 %collective-permute-start.16 = (f32[128,128]{1,0:T(8,128)S(1)}, f32[128,128]{1,0:T(8,128)S(1)}, u32[]{:S(2)}, u32[]{:S(2)}) collective-permute-start(f32[128,128]{1,0:T(8,128)S(1)} %get-tuple-element.27.refs_0_), channel_id=1, source_target_pairs={{0,3},{1,0},{2,1},{3,2},{4,7},{5,4},{6,5},{7,6},{8,11},{9,8},{10,9... | collective-permute-start | bytes 196616 | tf_op jit(solution)/shard_map/ppermute | solution.py:311
  98.6 4.7 %collective-permute-start.15 = (f32[128,128]{1,0:T(8,128)S(1)}, f32[128,128]{1,0:T(8,128)S(1)}, u32[]{:S(2)}, u32[]{:S(2)}) collective-permute-start(f32[128,128]{1,0:T(8,128)S(1)} %get-tuple-element.27.refs_0_), channel_id=1, source_target_pairs={{0,2},{1,3},{2,0},{3,1},{4,6},{5,7},{6,4},{7,5},{8,10},{9,11},{10,... | collective-permute-start | bytes 196616 | tf_op jit(solution)/shard_map/ppermute | solution.py:311
  98.7 6.7 %collective-permute-start.14 = (f32[128,128]{1,0:T(8,128)S(1)}, f32[128,128]{1,0:T(8,128)S(1)}, u32[]{:S(2)}, u32[]{:S(2)}) collective-permute-start(f32[128,128]{1,0:T(8,128)S(1)} %get-tuple-element.27.refs_0_), channel_id=1, source_target_pairs={{0,1},{1,2},{2,3},{3,0},{4,5},{5,6},{6,7},{7,4},{8,9},{9,10},{10,1... | collective-permute-start | bytes 196616 | tf_op jit(solution)/shard_map/ppermute | solution.py:311

commit v3 on v2

--- a/solution.py
+++ b/solution.py
@@ -51,6 +51,14 @@
     high = x.astype(BF16).astype(F32)
     mid = (x - high).astype(BF16).astype(F32)
     return high, mid, x - high - mid
+
+
+def gram_of(s):
+    high, mid, low = (part.astype(BF16) for part in thirds(s))
+    all_three = jnp.concatenate([high, mid, low], 1)
+    blocks = dot(all_three, jnp.concatenate([high, mid], 1), TN)
+    cross = blocks[K : 2 * K, :K] + blocks[2 * K :, :K]
+    return blocks[:K, :K] + ((cross + cross.T) + blocks[K : 2 * K, K:])
 
 
 CHUNKS = 2
@@ -110,85 +118,112 @@
     )(scalars(*where), a, b)
 
 
-def raw_kernel(count, earlier, last, where_ref, a_ref, *refs):
-    refs = list(refs)
-    take = lambda n: [refs.pop(0) for _ in range(n)]
-    s_refs = take(count)
-    prev_refs = take(1 if earlier else 0)
-    gram_refs = take(earlier if last else 0)
-    rows, snaps = s_refs[0].shape[0], a_ref.shape[1]
-    half = snaps // 2
-    if last:
-        o_ref, slot_ref, both_ref, buf_ref, sems = refs
-    else:
-        o_ref, *g_refs = take(1 + count)
-        buf_ref, sems = refs
+def own_kernel(where_ref, a_ref, s_ref, o_ref, g_ref, *refs):
+    split_refs, (buf_ref, sems) = refs[:4], refs[4:]
+    rows, snaps = s_ref.shape[0], a_ref.shape[1]
     boxes = []
-    for j in range(2):
-        for i in range(count):
-            at = pl.multiple_of(where_ref[i] * rows, rows)
-            boxes.append((pl.ds(at, rows), pl.ds(j * half, half), pl.ds(i * rows, rows)))
+    for i in range(4):
+        at = pl.multiple_of(where_ref[i] * rows, rows)
+        boxes.append((pl.ds(at, rows), pl.ds(0, snaps), pl.ds(i * rows, rows)))
     copies = start_copies(a_ref, buf_ref, sems, boxes)
-    for i in range(count):
-        s = s_refs[i][...]
-        gram = dot(s, s, TN, HIGHEST)
-        if last:
-            slot_ref[where_ref[i]] = gram
-        else:
-            g_refs[i][...] = gram
-    if last:
-        for i in range(earlier):
-            slot_ref[where_ref[count + i]] = gram_refs[i][...]
-        gram = ((slot_ref[0] + slot_ref[1]) + slot_ref[2]) + slot_ref[3]
-        for j in range(8):
-            o_ref[j // 4, j % 4, K:, :] = gram[16 * j : 16 * j + 16, :]
-    for j in range(2):
-        cols = slice(j * half, (j + 1) * half)
-        for i in range(count):
-            high, low = halves(s_refs[i][...])
-            copies[j * count + i].wait()
-            a_high, a_low = halves(buf_ref[i * rows : (i + 1) * rows, cols])
-            both = dot(jnp.concatenate([high, low], 1), a_high, TN)
-            cross = dot(high, a_low, TN)
-            if last:
-                both_ref[:, cols] = both
-                both_ref[:K, cols] = both_ref[:K, cols] + (both_ref[K:, cols] + cross)
-                for k in range(4):
-                    at = slice(j * half + k * K, j * half + (k + 1) * K)
-                    o_ref[j, k, :K, :] = prev_refs[0][:, at] + both_ref[:K, at]
-            else:
-                total = both[:K] + (both[K:] + cross)
-                if i > 0:
-                    total = o_ref[:, cols] + total
-                elif earlier:
-                    total = prev_refs[0][:, cols] + total
-                o_ref[:, cols] = total
-
-
-def raw_pieces(a, pieces, where, prev=None, grams=(), last=False):
-    count, earlier = len(pieces), len(grams)
-    rows, snaps = pieces[0].shape[0], a.shape[1]
-    args = list(pieces) + ([prev] if earlier else []) + (list(grams) if last else [])
-    scratch = [
-        pltpu.VMEM((count * rows, snaps), F32),
-        pltpu.SemaphoreType.DMA((2 * count,)),
-    ]
-    if last:
-        out_shape = [jax.ShapeDtypeStruct((2, 4, K + 16, K), F32)]
-        scratch = [pltpu.VMEM((4, K, K), F32), pltpu.VMEM((2 * K, snaps), F32)] + scratch
-    else:
-        out_shape = [jax.ShapeDtypeStruct((K, snaps), F32)]
-        out_shape += [jax.ShapeDtypeStruct((K, K), F32)] * count
-    return pl.pallas_call(
-        functools.partial(raw_kernel, count, earlier, last),
-        in_specs=[smem(), pl.BlockSpec(memory_space=pltpu.HBM)] + [vmem()] * len(args),
-        out_specs=[vmem()] * len(out_shape),
+    s = s_ref[...]
+    g_ref[...] = gram_of(s)
+    high, low = halves(s)
+    both_s = jnp.concatenate([high, low], 1)
+    copies[0].wait()
+    for lo in range(0, snaps, 256):
+        cols = slice(lo, lo + 256)
+        a_high, a_low = halves(buf_ref[:rows, cols])
+        both = dot(both_s, a_high, TN)
+        cross = dot(high, a_low, TN)
+        o_ref[:, cols] = both[:K] + (both[K:] + cross)
+    for i in range(3):
+        copies[i + 1].wait()
+        a_high, a_low = halves(buf_ref[(i + 1) * rows : (i + 2) * rows, :])
+        pair = split_refs[:2] if i < 2 else split_refs[2:]
+        at = i % 2 * rows
+        pair[0][at : at + rows, :] = a_high
+        pair[1][at : at + rows, :] = a_low
+
+
+def own_piece(a, s, where):
+    rows, snaps = s.shape[0], a.shape[1]
+    out_shape = [jax.ShapeDtypeStruct((K, snaps), F32), jax.ShapeDtypeStruct((K, K), F32)]
+    out_shape += [jax.ShapeDtypeStruct((2 * rows, snaps), BF16)] * 2
+    out_shape += [jax.ShapeDtypeStruct((rows, snaps), BF16)] * 2
+    return pl.pallas_call(
+        own_kernel,
+        in_specs=[smem(), pl.BlockSpec(memory_space=pltpu.HBM), vmem()],
+        out_specs=[vmem()] * 6,
         out_shape=out_shape,
-        scratch_shapes=scratch,
-        compiler_params=params(),
-        cost_estimate=cost(6 * count * rows * snaps * K, 4 * (count * rows + 2 * K) * snaps),
-        name="raw_pieces",
-    )(where, a, *args)
+        scratch_shapes=[pltpu.VMEM((4 * rows, snaps), F32), pltpu.SemaphoreType.DMA((4,))],
+        compiler_params=params(),
+        cost_estimate=cost(6 * rows * snaps * K, 4 * (4 * rows + 2 * K) * snaps),
+        name="own_piece",
+    )(where, a, s)
+
+
+def two_kernel(high_ref, low_ref, s1_ref, s2_ref, prev_ref, o_ref, g1_ref, g2_ref):
+    rows, snaps = s1_ref.shape[0], high_ref.shape[1]
+    s = jnp.concatenate([s1_ref[...], s2_ref[...]], 0)
+    g1_ref[...] = gram_of(s[:rows])
+    g2_ref[...] = gram_of(s[rows:])
+    high, low = halves(s)
+    both_s = jnp.concatenate([high, low], 1)
+    for lo in range(0, snaps, 256):
+        cols = slice(lo, lo + 256)
+        both = dot(both_s, high_ref[:, cols], TN)
+        cross = dot(high, low_ref[:, cols], TN)
+        o_ref[:, cols] = prev_ref[:, cols] + (both[:K] + (both[K:] + cross))
+
+
+def two_pieces(high, low, s1, s2, prev):
+    rows, snaps = s1.shape[0], high.shape[1]
+    return pl.pallas_call(
+        two_kernel,
+        in_specs=[vmem()] * 5,
+        out_specs=[vmem()] * 3,
+        out_shape=[jax.ShapeDtypeStruct((K, snaps), F32)] + [jax.ShapeDtypeStruct((K, K), F32)] * 2,
+        compiler_params=params(),
+        cost_estimate=cost(12 * rows * snaps * K, 4 * (2 * rows + 2 * K) * snaps),
+        name="two_pieces",
+    )(high, low, s1, s2, prev)
+
+
+def last_kernel(where_ref, high_ref, low_ref, s_ref, prev_ref, *refs):
+    gram_refs, (o_ref, slot_ref, both_ref) = refs[:3], refs[3:]
+    snaps = high_ref.shape[1]
+    s = s_ref[...]
+    for i in range(3):
+        slot_ref[where_ref[i]] = gram_refs[i][...]
+    slot_ref[where_ref[3]] = gram_of(s)
+    gram = ((slot_ref[0] + slot_ref[1]) + slot_ref[2]) + slot_ref[3]
+    for j in range(8):
+        o_ref[j // 4, j % 4, K:, :] = gram[16 * j : 16 * j + 16, :]
+    high, low = halves(s)
+    both_s = jnp.concatenate([high, low], 1)
+    for lo in range(0, snaps, 256):
+        cols = slice(lo, lo + 256)
+        both_ref[:, cols] = dot(both_s, high_ref[:, cols], TN)
+        cross = dot(high, low_ref[:, cols], TN)
+        both_ref[:K, cols] = both_ref[:K, cols] + (both_ref[K:, cols] + cross)
+        for j in range(lo // K, lo // K + 2):
+            at = slice(j * K, (j + 1) * K)
+            o_ref[j // 4, j % 4, :K, :] = prev_ref[:, at] + both_ref[:K, at]
+
+
+def last_piece(where, high, low, s, prev, grams):
+    rows, snaps = s.shape[0], high.shape[1]
+    return pl.pallas_call(
+        last_kernel,
+        in_specs=[smem()] + [vmem()] * 7,
+        out_specs=vmem(),
+        out_shape=jax.ShapeDtypeStruct((2, 4, K + 16, K), F32),
+        scratch_shapes=[pltpu.VMEM((4, K, K), F32), pltpu.VMEM((2 * K, snaps), F32)],
+        compiler_params=params(),
+        cost_estimate=cost(6 * rows * snaps * K, 4 * (rows + 2 * K) * snaps),
+        name="last_piece",
+    )(where, high, low, s, prev, *grams)
 
 
 def inverse_factor(w_ref, o_ref):
@@ -211,9 +246,10 @@
                 inv[c] = jnp.where(row == k, scaled, inv[c] - m * scaled)
         inside = (lane >= lo) & (lane < hi)
         block = jnp.where(inside, jnp.where(lane - lo == row, 1.0, 0.0), block)
-        done = inv[0] * block[0:1, :]
-        for c in range(1, NB):
-            done = done + inv[c] * block[c : c + 1, :]
+        terms = [inv[c] * block[c : c + 1, :] for c in range(NB)]
+        while len(terms) > 1:
+            terms = [a + b for a, b in zip(terms[::2], terms[1::2])]
+        done = terms[0]
         o_ref[lo:hi, :] = jnp.where(lane < hi, done, 0.0)
         if hi < K:
             h, m, l = thirds(done)
@@ -323,15 +359,15 @@
     start_basis = pltpu.with_memory_space_constraint(start_basis, pltpu.HBM)
     (p2,) = sketch_pieces(anomalies, start_basis, [(y + 2) % 4])
     r2 = shifted(p2, "y", 2)
-    p1, p3, p0 = sketch_pieces(anomalies, start_basis, [(y + 1) % 4, (y + 3) % 4, y])
+    p1, p3 = sketch_pieces(anomalies, start_basis, [(y + 1) % 4, (y + 3) % 4])
     r1, r3 = shifted(p1, "y", 1), shifted(p3, "y", 3)
+    (p0,) = sketch_pieces(anomalies, start_basis, [y])
     own = p0 + r2 + r1 + r3
     s2, s1, s3 = (shifted(own, "y", shift) for shift in (2, 1, 3))
-    raw, g0 = raw_pieces(anomalies, [own], scalars(owner[0]))
-    raw, g1, g3 = raw_pieces(anomalies, [s1, s3], scalars(owner[1], owner[3]), raw, [g0])
-    (stacked,) = raw_pieces(
-        anomalies, [s2], scalars(owner[2], owner[0], owner[1], owner[3]), raw, [g0, g1, g3], True
-    )
+    blocks = scalars(*owner)
+    raw, g0, high, low, high3, low3 = own_piece(anomalies, own, blocks)
+    raw, g1, g2 = two_pieces(high, low, s1, s2, raw)
+    stacked = last_piece(blocks, high3, low3, s3, raw, (g0, g1, g2))
 
     part = pick(stacked, c) + shifted(pick(stacked, 1 - c), "c", 1)
     arrived = [shifted(pick(part, (x + shift) % 4), "x", shift) for shift in (2, 1, 3)]

time: 112 us -> 105 us (0.938)
  waiting for transfers between devices: 24.3 us -> 17.9 us
  Pallas kernels: 30.9 us -> 29.7 us
    ppermute x17, waiting for transfers between devices: 24.3 us -> 17.9 us  [shifted(): return lax.ppermute(value, axis, [(i, (i + shift) % n) for i in range(n)])]
    pallas_call x3, Pallas kernels: 8.42 us -> 6.9 us  [the longest x1 4.36 us: own_piece(): pl.pallas_call(own_kernel, in_specs=[smem(), pl.BlockSpec(memory_space=pl...]
    pallas_call x2 -> x3, Pallas kernels: 8 us -> 8.45 us  [sketch_pieces(): pl.pallas_call(functools.partial(sketch_kernel, count), in_specs=[smem()]...]
  transfers between devices with their start and end apart: 17 -> 17, of which waited for: 12 -> 8; matrix products, arithmetic and copies ran while one was open for 0% -> 0% of each run, Pallas kernels for 13% -> 12%
where the time goes in v3:
time: 105 us
  starting transfers between devices  32 us (30%)
  Pallas kernels  29.7 us (28%)
  blocking collectives  23.7 us (23%)
  waiting for transfers between devices  17.9 us (17%)
    ppermute x17, starting transfers between devices, shifted(): return lax.ppermute(value, axis, [(i, (i + shift) % n) for i in range(n)])  32 us
    all_to_all x1, blocking collectives, on_device(): part = jnp.sum(lax.all_to_all(copies, 'z', 0, 0), 0)  23.7 us
    ppermute x17, waiting for transfers between devices, shifted(): return lax.ppermute(value, axis, [(i, (i + shift) % n) for i in range(n)])  17.9 us
    pallas_call x3, Pallas kernels, sketch_pieces(): pl.pallas_call(functools.partial(sketch_kernel, count), in_specs=[smem()]...  8.45 us
    pallas_call x1, Pallas kernels, time_basis_of(): pl.pallas_call(time_kernel, in_specs=[smem()] + [vmem()] * 5, out_specs=v...  5.98 us
    pallas_call x1, Pallas kernels, middle(): pl.pallas_call(middle_kernel, in_specs=[smem(), vmem(), vmem()], out_spec...  5.89 us
    pallas_call x1, Pallas kernels, own_piece(): pl.pallas_call(own_kernel, in_specs=[smem(), pl.BlockSpec(memory_space=pl...  4.36 us
    pallas_call x1, Pallas kernels, space(): pl.pallas_call(space_kernel, in_specs=[smem()] + [vmem()] * 6, out_specs=...  2.53 us
  transfers between devices with their start and end apart: 17, of which 8 were waited for; matrix products, arithmetic and copies ran while one was open for 0% of the time, Pallas kernels for 12%

profile of v3, /device:TPU:1, one launch (start us, length us, event | category | flops | bytes accessed | tf_op | source)
XLA Modules:
  0.0 104.7 jit_solution(16546357309456145092)
XLA Ops:
  0.7 3.7 %sketch_pieces.5 = (f32[512,128]{1,0:T(8,128)S(1)}, f32[512,128]{1,0:T(8,128)S(1)}) custom-call(s32[2]{0:T(128)S(1)} %pad_add_fusion.2.where_ref, f32[2048,1024]{1,0:T(8,128)} %a_ref.7, f32[1024,128]{1,0:T(8,128)} %b_ref.5), custom_call_target="tpu_custom_call" | custom-call | flops 805306368 | bytes 4718592 | tf_op jit(solution)/shard_map/sketch_pieces/pallas_call | solution.py:103
  4.5 2.2 %collective-permute-start.1 = (f32[512,128]{1,0:T(8,128)S(1)}, f32[512,128]{1,0:T(8,128)S(1)}, u32[]{:S(2)}, u32[]{:S(2)}) collective-permute-start(f32[512,128]{1,0:T(8,128)S(1)} %get-tuple-element.18), channel_id=1, source_target_pairs={{0,1},{1,2},{2,3},{3,0},{4,5},{5,6},{6,7},{7,4},{8,9},{9,10},{10,1... | collective-permute-start | bytes 786440 | tf_op jit(solution)/shard_map/ppermute | solution.py:347
  6.7 1.5 %collective-permute-start.2 = (f32[512,128]{1,0:T(8,128)S(1)}, f32[512,128]{1,0:T(8,128)S(1)}, u32[]{:S(2)}, u32[]{:S(2)}) collective-permute-start(f32[512,128]{1,0:T(8,128)S(1)} %get-tuple-element.19), channel_id=1, source_target_pairs={{0,3},{1,0},{2,1},{3,2},{4,7},{5,4},{6,5},{7,6},{8,11},{9,8},{10,9... | collective-permute-start | bytes 786440 | tf_op jit(solution)/shard_map/ppermute | solution.py:347
  8.2 2.4 %sketch_pieces.4 = f32[512,128]{1,0:T(8,128)S(1)} custom-call(s32[1]{0:T(128)} %bitcast.2.where_ref, f32[2048,1024]{1,0:T(8,128)} %a_ref.7, f32[1024,128]{1,0:T(8,128)} %b_ref.5), custom_call_target="tpu_custom_call" | custom-call | flops 402653184 | bytes 2621440 | tf_op jit(solution)/shard_map/sketch_pieces/pallas_call | solution.py:103
  10.6 1.6 %collective-permute-start = (f32[512,128]{1,0:T(8,128)S(1)}, f32[512,128]{1,0:T(8,128)S(1)}, u32[]{:S(2)}, u32[]{:S(2)}) collective-permute-start(f32[512,128]{1,0:T(8,128)S(1)} %sketch_pieces.4), channel_id=1, source_target_pairs={{0,2},{1,3},{2,0},{3,1},{4,6},{5,7},{6,4},{7,5},{8,10},{9,11},{10,... | collective-permute-start | bytes 786440 | tf_op jit(solution)/shard_map/ppermute | solution.py:347
  12.2 2.4 %sketch_pieces.3 = f32[512,128]{1,0:T(8,128)S(1)} custom-call(s32[1]{0:T(128)} %bitcast.where_ref, f32[2048,1024]{1,0:T(8,128)} %a_ref.7, f32[1024,128]{1,0:T(8,128)} %b_ref.5), custom_call_target="tpu_custom_call" | custom-call | flops 402653184 | bytes 2621440 | tf_op jit(solution)/shard_map/sketch_pieces/pallas_call | solution.py:103
  14.6 5.1 %collective-permute-done = f32[512,128]{1,0:T(8,128)S(1)} collective-permute-done((f32[512,128]{1,0:T(8,128)S(1)}, f32[512,128]{1,0:T(8,128)S(1)}, u32[]{:S(2)}, u32[]{:S(2)}) %collective-permute-start) | collective-permute-done | bytes 262176 | tf_op jit(solution)/shard_map/ppermute | solution.py:347
  19.7 1.5 %collective-permute-start.4 = (f32[512,128]{1,0:T(8,128)S(1)}, f32[512,128]{1,0:T(8,128)S(1)}, u32[]{:S(2)}, u32[]{:S(2)}) collective-permute-start(f32[512,128]{1,0:T(8,128)S(1)} %add_add_fusion.s_ref.refs_0_), channel_id=1, source_target_pairs={{0,1},{1,2},{2,3},{3,0},{4,5},{5,6},{6,7},{7,4},{8,9},{9,10},{10,1... | collective-permute-start | bytes 786440 | tf_op jit(solution)/shard_map/ppermute | solution.py:347
  21.3 2.0 %collective-permute-start.5 = (f32[512,128]{1,0:T(8,128)S(1)}, f32[512,128]{1,0:T(8,128)S(1)}, u32[]{:S(2)}, u32[]{:S(2)}) collective-permute-start(f32[512,128]{1,0:T(8,128)S(1)} %add_add_fusion.s_ref.refs_0_), channel_id=1, source_target_pairs={{0,2},{1,3},{2,0},{3,1},{4,6},{5,7},{6,4},{7,5},{8,10},{9,11},{10,... | collective-permute-start | bytes 786440 | tf_op jit(solution)/shard_map/ppermute | solution.py:347
  23.3 0.5 collective-permute-start.3
  23.9 4.4 %own_piece.1 = (f32[128,1024]{1,0:T(8,128)S(1)}, f32[128,128]{1,0:T(8,128)S(1)}, bf16[1024,1024]{1,0:T(8,128)(2,1)S(1)}, bf16[1024,1024]{1,0:T(8,128)(2,1)S(1)},...) custom-call(s32[4]{0:T(128)S(1)} %pad_add_fusion.where_ref, f32[2048,1024]{1,0:T(8,128)} %a_ref.7, ...), custom_call_target="tpu_custom_call" | custom-call | flops 402653184 | bytes 9437184 | tf_op jit(solution)/shard_map/own_piece/pallas_call | solution.py:154
  28.2 5.0 %collective-permute-done.5.s2_ref.refs_2_ = f32[512,128]{1,0:T(8,128)S(1)} collective-permute-done((f32[512,128]{1,0:T(8,128)S(1)}, f32[512,128]{1,0:T(8,128)S(1)}, u32[]{:S(2)}, u32[]{:S(2)}) %collective-permute-start.5) | collective-permute-done | bytes 262176 | tf_op jit(solution)/shard_map/ppermute | solution.py:347
  33.3 1.3 %two_pieces.1 = (f32[128,1024]{1,0:T(8,128)S(1)}, f32[128,128]{1,0:T(8,128)S(1)}, f32[128,128]{1,0:T(8,128)S(1)}) custom-call(bf16[1024,1024]{1,0:T(8,128)(2,1)S(1)} %get-tuple-element.22.high_ref, bf16[1024,1024]{1,0:T(8,128)(2,1)S(1)} %get-tuple-element.23.low_ref, f32[512,128]{1,0:T(8,128)S(1)} %collective-permute-done.4.s1_ref.refs_1_, ...), custom_call_target="tpu_custom_call" | custom-call | flops 805306368 | bytes 5242880 | tf_op jit(solution)/shard_map/two_pieces/pallas_call | solution.py:182
  34.5 1.3 %last_piece.1 = f32[2,4,144,128]{3,2,1,0:T(8,128)S(1)} custom-call(s32[4]{0:T(128)S(1)} %pad_add_fusion.where_ref, bf16[512,1024]{1,0:T(8,128)(2,1)S(1)} %get-tuple-element.20.high_ref, bf16[512,1024]{1,0:T(8,128)(2,1)S(1)} %get-tuple-element.21.low_ref, f32[512,128]{1,0:T(8,128)S(1)} %collective-permute-done.3.s_ref.refs_3_, ...), custom_call_target="tpu_custom_call" | custom-call | flops 402653184 | bytes 3145728 | tf_op jit(solution)/shard_map/last_piece/pallas_call | solution.py:217
  35.9 3.0 %collective-permute-start.6 = (f32[4,144,128]{2,1,0:T(8,128)S(1)}, f32[4,144,128]{2,1,0:T(8,128)S(1)}, u32[]{:S(2)}, u32[]{:S(2)}) collective-permute-start(f32[4,144,128]{2,1,0:T(8,128)S(1)} %dynamic-slice_bitcast_fusion), channel_id=1, source_target_pairs={{0,4},{4,0},{1,5},{5,1},{2,6},{6,2},{3,7},{7,3},{8,12},{12,8},{9,1... | collective-permute-start | bytes 884744 | tf_op jit(solution)/shard_map/ppermute | solution.py:347
  38.8 1.2 %collective-permute-done.6 = f32[4,144,128]{2,1,0:T(8,128)S(1)} collective-permute-done((f32[4,144,128]{2,1,0:T(8,128)S(1)}, f32[4,144,128]{2,1,0:T(8,128)S(1)}, u32[]{:S(2)}, u32[]{:S(2)}) %collective-permute-start.6) | collective-permute-done | bytes 294944 | tf_op jit(solution)/shard_map/ppermute | solution.py:347
  40.1 3.1 %collective-permute-start.7 = (f32[144,128]{1,0:T(8,128)S(1)}, f32[144,128]{1,0:T(8,128)S(1)}, u32[]{:S(2)}, u32[]{:S(2)}) collective-permute-start(f32[144,128]{1,0:T(8,128)S(1)} %get-tuple-element.34), channel_id=1, source_target_pairs={{0,128},{64,192},{128,0},{192,64},{1,129},{65,193},{129,1},{193,65... | collective-permute-start | bytes 221192 | tf_op jit(solution)/shard_map/ppermute | solution.py:347
  43.3 0.3 collective-permute-start.8
  43.6 2.4 %collective-permute-start.9 = (f32[144,128]{1,0:T(8,128)S(1)}, f32[144,128]{1,0:T(8,128)S(1)}, u32[]{:S(2)}, u32[]{:S(2)}) collective-permute-start(f32[144,128]{1,0:T(8,128)S(1)} %get-tuple-element.35), channel_id=1, source_target_pairs={{0,192},{64,0},{128,64},{192,128},{1,193},{65,1},{129,65},{193,129... | collective-permute-start | bytes 221192 | tf_op jit(solution)/shard_map/ppermute | solution.py:347
  46.0 1.7 %collective-permute-done.8 = f32[144,128]{1,0:T(8,128)S(1)} collective-permute-done((f32[144,128]{1,0:T(8,128)S(1)}, f32[144,128]{1,0:T(8,128)S(1)}, u32[]{:S(2)}, u32[]{:S(2)}) %collective-permute-start.8) | collective-permute-done | bytes 73760 | tf_op jit(solution)/shard_map/ppermute | solution.py:347
  47.8 23.7 %all_to_all.5 = f32[8,144,128]{2,1,0:T(8,128)S(1)} all-to-all(f32[8,144,128]{2,1,0:T(8,128)S(1)} %broadcast_in_dim.2), channel_id=1, replica_groups=mesh['x'=4,'z'=8,'c'=2,'y'=4] {'z'}, dimensions={0} | all-to-all | bytes 1179648 | tf_op jit(solution)/shard_map/all_to_all | solution.py:376
  71.5 3.8 %collective-permute-start.10 = (f32[144,128]{1,0:T(8,128)S(1)}, f32[144,128]{1,0:T(8,128)S(1)}, u32[]{:S(2)}, u32[]{:S(2)}) collective-permute-start(f32[144,128]{1,0:T(8,128)S(1)} %reduce_sum.9), channel_id=1, source_target_pairs={{0,64},{64,128},{128,192},{192,0},{1,65},{65,129},{129,193},{193,1... | collective-permute-start | bytes 221192 | tf_op jit(solution)/shard_map/ppermute | solution.py:347
  75.4 2.4 %collective-permute-start.12 = (f32[144,128]{1,0:T(8,128)S(1)}, f32[144,128]{1,0:T(8,128)S(1)}, u32[]{:S(2)}, u32[]{:S(2)}) collective-permute-start(f32[144,128]{1,0:T(8,128)S(1)} %reduce_sum.9), channel_id=1, source_target_pairs={{0,192},{64,0},{128,64},{192,128},{1,193},{65,1},{129,65},{193,129... | collective-permute-start | bytes 221192 | tf_op jit(solution)/shard_map/ppermute | solution.py:347
  77.8 2.2 %collective-permute-done.11 = f32[144,128]{1,0:T(8,128)S(1)} collective-permute-done((f32[144,128]{1,0:T(8,128)S(1)}, f32[144,128]{1,0:T(8,128)S(1)}, u32[]{:S(2)}, u32[]{:S(2)}) %collective-permute-start.11) | collective-permute-done | bytes 73760 | tf_op jit(solution)/shard_map/ppermute | solution.py:347
  80.0 4.6 %collective-permute-start.13 = (f32[4,144,128]{2,1,0:T(8,128)S(1)}, f32[4,144,128]{2,1,0:T(8,128)S(1)}, u32[]{:S(2)}, u32[]{:S(2)}) collective-permute-start(f32[4,144,128]{2,1,0:T(8,128)S(1)} %pad_maximum_fusion.mine_ref), channel_id=1, source_target_pairs={{0,4},{4,0},{1,5},{5,1},{2,6},{6,2},{3,7},{7,3},{8,12},{12,8},{9,1... | collective-permute-start | bytes 884744 | tf_op jit(solution)/shard_map/ppermute | solution.py:347
  84.7 1.1 %collective-permute-done.13.other_ref = f32[4,144,128]{2,1,0:T(8,128)S(1)} collective-permute-done((f32[4,144,128]{2,1,0:T(8,128)S(1)}, f32[4,144,128]{2,1,0:T(8,128)S(1)}, u32[]{:S(2)}, u32[]{:S(2)}) %collective-permute-start.13) | collective-permute-done | bytes 294944 | tf_op jit(solution)/shard_map/ppermute | solution.py:347
  85.8 5.9 %middle.1 = (f32[128,128]{1,0:T(8,128)S(1)}, f32[128,1024]{1,0:T(8,128)S(1)}, f32[128,128]{1,0:T(8,128)S(1)}) custom-call(s32[2]{0:T(128)S(1)} %pad_add_fusion.1.where_ref, f32[4,144,128]{2,1,0:T(8,128)S(1)} %pad_maximum_fusion.mine_ref, f32[4,144,128]{2,1,0:T(8,128)S(1)} %collective-permute-done.13.other_ref), custom_call_target="tpu_custom_call" | custom-call | flops 402653184 | bytes 1048576 | tf_op jit(solution)/shard_map/middle/pallas_call | solution.py:279
  91.8 2.9 %collective-permute-start.15 = (f32[128,128]{1,0:T(8,128)S(1)}, f32[128,128]{1,0:T(8,128)S(1)}, u32[]{:S(2)}, u32[]{:S(2)}) collective-permute-start(f32[128,128]{1,0:T(8,128)S(1)} %get-tuple-element.33.refs_0_), channel_id=1, source_target_pairs={{0,2},{1,3},{2,0},{3,1},{4,6},{5,7},{6,4},{7,5},{8,10},{9,11},{10,... | collective-permute-start | bytes 196616 | tf_op jit(solution)/shard_map/ppermute | solution.py:347
  94.7 2.5 %space.1 = (f32[2048,128]{1,0:T(8,128)}, f32[1024,128]{1,0:T(8,128)S(1)}) custom-call(s32[4]{0:T(128)S(1)} %pad_add_fusion.where_ref, f32[128,128]{1,0:T(8,128)S(1)} %get-tuple-element.29.inv_ref, f32[128,1024]{1,0:T(8,128)S(1)} %get-tuple-element.30.back_t_ref, f32[512,128]{1,0:T(8,128)S(1)} %add_add_fusion.s_ref.refs_0_, ...), custom_call_target="tpu_custom_call" | custom-call | flops 402653184 | bytes 3145728 | tf_op jit(solution)/shard_map/space/pallas_call | solution.py:308
  97.2 0.4 collective-permute-done.15.refs_2_
  97.6 1.1 %collective-permute-done.16.refs_3_ = f32[128,128]{1,0:T(8,128)S(1)} collective-permute-done((f32[128,128]{1,0:T(8,128)S(1)}, f32[128,128]{1,0:T(8,128)S(1)}, u32[]{:S(2)}, u32[]{:S(2)}) %collective-permute-start.16) | collective-permute-done | bytes 65568 | tf_op jit(solution)/shard_map/ppermute | solution.py:347
  98.7 6.0 %time_basis.1 = f32[1024,128]{1,0:T(8,128)} custom-call(s32[4]{0:T(128)S(1)} %pad_add_fusion.where_ref, f32[1024,128]{1,0:T(8,128)S(1)} %get-tuple-element.32.back_ref, f32[128,128]{1,0:T(8,128)S(1)} %get-tuple-element.33.refs_0_, f32[128,128]{1,0:T(8,128)S(1)} %collective-permute-done.14.refs_1_, f32[128,128]{1,0:T(8,128)S(1)} %collective-permute-done.15.refs_2_, ...), custom_call_target="tpu_custom_call" | custom-call | flops 201326592 | bytes 1048576 | tf_op jit(solution)/shard_map/time_basis/pallas_call | solution.py:329
  (23 shorter events, 0.7 us)
Async XLA Ops:
  4.5 10.1 %collective-permute-start.1 = (f32[512,128]{1,0:T(8,128)S(1)}, f32[512,128]{1,0:T(8,128)S(1)}, u32[]{:S(2)}, u32[]{:S(2)}) collective-permute-start(f32[512,128]{1,0:T(8,128)S(1)} %get-tuple-element.18), channel_id=1, source_target_pairs={{0,1},{1,2},{2,3},{3,0},{4,5},{5,6},{6,7},{7,4},{8,9},{9,10},{10,1... | collective-permute-start | bytes 786440 | tf_op jit(solution)/shard_map/ppermute | solution.py:347
  6.7 7.9 %collective-permute-start.2 = (f32[512,128]{1,0:T(8,128)S(1)}, f32[512,128]{1,0:T(8,128)S(1)}, u32[]{:S(2)}, u32[]{:S(2)}) collective-permute-start(f32[512,128]{1,0:T(8,128)S(1)} %get-tuple-element.19), channel_id=1, source_target_pairs={{0,3},{1,0},{2,1},{3,2},{4,7},{5,4},{6,5},{7,6},{8,11},{9,8},{10,9... | collective-permute-start | bytes 786440 | tf_op jit(solution)/shard_map/ppermute | solution.py:347
  10.6 9.1 %collective-permute-start = (f32[512,128]{1,0:T(8,128)S(1)}, f32[512,128]{1,0:T(8,128)S(1)}, u32[]{:S(2)}, u32[]{:S(2)}) collective-permute-start(f32[512,128]{1,0:T(8,128)S(1)} %sketch_pieces.4), channel_id=1, source_target_pairs={{0,2},{1,3},{2,0},{3,1},{4,6},{5,7},{6,4},{7,5},{8,10},{9,11},{10,... | collective-permute-start | bytes 786440 | tf_op jit(solution)/shard_map/ppermute | solution.py:347
  19.7 8.5 %collective-permute-start.4 = (f32[512,128]{1,0:T(8,128)S(1)}, f32[512,128]{1,0:T(8,128)S(1)}, u32[]{:S(2)}, u32[]{:S(2)}) collective-permute-start(f32[512,128]{1,0:T(8,128)S(1)} %add_add_fusion.s_ref.refs_0_), channel_id=1, source_target_pairs={{0,1},{1,2},{2,3},{3,0},{4,5},{5,6},{6,7},{7,4},{8,9},{9,10},{10,1... | collective-permute-start | bytes 786440 | tf_op jit(solution)/shard_map/ppermute | solution.py:347
  21.3 12.0 %collective-permute-start.5 = (f32[512,128]{1,0:T(8,128)S(1)}, f32[512,128]{1,0:T(8,128)S(1)}, u32[]{:S(2)}, u32[]{:S(2)}) collective-permute-start(f32[512,128]{1,0:T(8,128)S(1)} %add_add_fusion.s_ref.refs_0_), channel_id=1, source_target_pairs={{0,2},{1,3},{2,0},{3,1},{4,6},{5,7},{6,4},{7,5},{8,10},{9,11},{10,... | collective-permute-start | bytes 786440 | tf_op jit(solution)/shard_map/ppermute | solution.py:347
  23.3 11.2 %collective-permute-start.3 = (f32[512,128]{1,0:T(8,128)S(1)}, f32[512,128]{1,0:T(8,128)S(1)}, u32[]{:S(2)}, u32[]{:S(2)}) collective-permute-start(f32[512,128]{1,0:T(8,128)S(1)} %add_add_fusion.s_ref.refs_0_), channel_id=1, source_target_pairs={{0,3},{1,0},{2,1},{3,2},{4,7},{5,4},{6,5},{7,6},{8,11},{9,8},{10,9... | collective-permute-start | bytes 786440 | tf_op jit(solution)/shard_map/ppermute | solution.py:347
  35.9 4.2 %collective-permute-start.6 = (f32[4,144,128]{2,1,0:T(8,128)S(1)}, f32[4,144,128]{2,1,0:T(8,128)S(1)}, u32[]{:S(2)}, u32[]{:S(2)}) collective-permute-start(f32[4,144,128]{2,1,0:T(8,128)S(1)} %dynamic-slice_bitcast_fusion), channel_id=1, source_target_pairs={{0,4},{4,0},{1,5},{5,1},{2,6},{6,2},{3,7},{7,3},{8,12},{12,8},{9,1... | collective-permute-start | bytes 884744 | tf_op jit(solution)/shard_map/ppermute | solution.py:347
  40.1 5.8 %collective-permute-start.7 = (f32[144,128]{1,0:T(8,128)S(1)}, f32[144,128]{1,0:T(8,128)S(1)}, u32[]{:S(2)}, u32[]{:S(2)}) collective-permute-start(f32[144,128]{1,0:T(8,128)S(1)} %get-tuple-element.34), channel_id=1, source_target_pairs={{0,128},{64,192},{128,0},{192,64},{1,129},{65,193},{129,1},{193,65... | collective-permute-start | bytes 221192 | tf_op jit(solution)/shard_map/ppermute | solution.py:347
  43.3 4.4 %collective-permute-start.8 = (f32[144,128]{1,0:T(8,128)S(1)}, f32[144,128]{1,0:T(8,128)S(1)}, u32[]{:S(2)}, u32[]{:S(2)}) collective-permute-start(f32[144,128]{1,0:T(8,128)S(1)} %get-tuple-element.36), channel_id=1, source_target_pairs={{0,64},{64,128},{128,192},{192,0},{1,65},{65,129},{129,193},{193,1... | collective-permute-start | bytes 221192 | tf_op jit(solution)/shard_map/ppermute | solution.py:347
  43.6 4.1 %collective-permute-start.9 = (f32[144,128]{1,0:T(8,128)S(1)}, f32[144,128]{1,0:T(8,128)S(1)}, u32[]{:S(2)}, u32[]{:S(2)}) collective-permute-start(f32[144,128]{1,0:T(8,128)S(1)} %get-tuple-element.35), channel_id=1, source_target_pairs={{0,192},{64,0},{128,64},{192,128},{1,193},{65,1},{129,65},{193,129... | collective-permute-start | bytes 221192 | tf_op jit(solution)/shard_map/ppermute | solution.py:347
  71.5 6.3 %collective-permute-start.10 = (f32[144,128]{1,0:T(8,128)S(1)}, f32[144,128]{1,0:T(8,128)S(1)}, u32[]{:S(2)}, u32[]{:S(2)}) collective-permute-start(f32[144,128]{1,0:T(8,128)S(1)} %reduce_sum.9), channel_id=1, source_target_pairs={{0,64},{64,128},{128,192},{192,0},{1,65},{65,129},{129,193},{193,1... | collective-permute-start | bytes 221192 | tf_op jit(solution)/shard_map/ppermute | solution.py:347
  75.3 4.7 %collective-permute-start.11 = (f32[144,128]{1,0:T(8,128)S(1)}, f32[144,128]{1,0:T(8,128)S(1)}, u32[]{:S(2)}, u32[]{:S(2)}) collective-permute-start(f32[144,128]{1,0:T(8,128)S(1)} %reduce_sum.9), channel_id=1, source_target_pairs={{0,128},{64,192},{128,0},{192,64},{1,129},{65,193},{129,1},{193,65... | collective-permute-start | bytes 221192 | tf_op jit(solution)/shard_map/ppermute | solution.py:347
  75.4 4.6 %collective-permute-start.12 = (f32[144,128]{1,0:T(8,128)S(1)}, f32[144,128]{1,0:T(8,128)S(1)}, u32[]{:S(2)}, u32[]{:S(2)}) collective-permute-start(f32[144,128]{1,0:T(8,128)S(1)} %reduce_sum.9), channel_id=1, source_target_pairs={{0,192},{64,0},{128,64},{192,128},{1,193},{65,1},{129,65},{193,129... | collective-permute-start | bytes 221192 | tf_op jit(solution)/shard_map/ppermute | solution.py:347
  80.0 5.8 %collective-permute-start.13 = (f32[4,144,128]{2,1,0:T(8,128)S(1)}, f32[4,144,128]{2,1,0:T(8,128)S(1)}, u32[]{:S(2)}, u32[]{:S(2)}) collective-permute-start(f32[4,144,128]{2,1,0:T(8,128)S(1)} %pad_maximum_fusion.mine_ref), channel_id=1, source_target_pairs={{0,4},{4,0},{1,5},{5,1},{2,6},{6,2},{3,7},{7,3},{8,12},{12,8},{9,1... | collective-permute-start | bytes 884744 | tf_op jit(solution)/shard_map/ppermute | solution.py:347
  91.7 5.5 %collective-permute-start.14 = (f32[128,128]{1,0:T(8,128)S(1)}, f32[128,128]{1,0:T(8,128)S(1)}, u32[]{:S(2)}, u32[]{:S(2)}) collective-permute-start(f32[128,128]{1,0:T(8,128)S(1)} %get-tuple-element.33.refs_0_), channel_id=1, source_target_pairs={{0,1},{1,2},{2,3},{3,0},{4,5},{5,6},{6,7},{7,4},{8,9},{9,10},{10,1... | collective-permute-start | bytes 196616 | tf_op jit(solution)/shard_map/ppermute | solution.py:347
  91.8 5.8 %collective-permute-start.15 = (f32[128,128]{1,0:T(8,128)S(1)}, f32[128,128]{1,0:T(8,128)S(1)}, u32[]{:S(2)}, u32[]{:S(2)}) collective-permute-start(f32[128,128]{1,0:T(8,128)S(1)} %get-tuple-element.33.refs_0_), channel_id=1, source_target_pairs={{0,2},{1,3},{2,0},{3,1},{4,6},{5,7},{6,4},{7,5},{8,10},{9,11},{10,... | collective-permute-start | bytes 196616 | tf_op jit(solution)/shard_map/ppermute | solution.py:347
  94.7 4.1 %collective-permute-start.16 = (f32[128,128]{1,0:T(8,128)S(1)}, f32[128,128]{1,0:T(8,128)S(1)}, u32[]{:S(2)}, u32[]{:S(2)}) collective-permute-start(f32[128,128]{1,0:T(8,128)S(1)} %get-tuple-element.33.refs_0_), channel_id=1, source_target_pairs={{0,3},{1,0},{2,1},{3,2},{4,7},{5,4},{6,5},{7,6},{8,11},{9,8},{10,9... | collective-permute-start | bytes 196616 | tf_op jit(solution)/shard_map/ppermute | solution.py:347

commit v4 on v3

--- a/solution.py
+++ b/solution.py
@@ -10,7 +10,7 @@
 F32 = jnp.float32
 BF16 = jnp.bfloat16
 K = 128
-NB = 16
+NB, SB = 32, 16
 VMEM_LIMIT = 24 * 2**20
 HIGHEST = lax.Precision.HIGHEST
 TN = (((0,), (0,)), ((), ()))
@@ -53,12 +53,15 @@
     return high, mid, x - high - mid
 
 
+def folded(blocks):
+    cross = blocks[K : 2 * K, :K] + blocks[2 * K :, :K]
+    return blocks[:K, :K] + ((cross + cross.T) + blocks[K : 2 * K, K:])
+
+
 def gram_of(s):
     high, mid, low = (part.astype(BF16) for part in thirds(s))
     all_three = jnp.concatenate([high, mid, low], 1)
-    blocks = dot(all_three, jnp.concatenate([high, mid], 1), TN)
-    cross = blocks[K : 2 * K, :K] + blocks[2 * K :, :K]
-    return blocks[:K, :K] + ((cross + cross.T) + blocks[K : 2 * K, K:])
+    return folded(dot(all_three, jnp.concatenate([high, mid], 1), TN))
 
 
 CHUNKS = 2
@@ -190,16 +193,12 @@
     )(high, low, s1, s2, prev)
 
 
-def last_kernel(where_ref, high_ref, low_ref, s_ref, prev_ref, *refs):
-    gram_refs, (o_ref, slot_ref, both_ref) = refs[:3], refs[3:]
+def last_kernel(high_ref, low_ref, s_ref, prev_ref, g0_ref, g1_ref, g2_ref, o_ref, both_ref):
     snaps = high_ref.shape[1]
     s = s_ref[...]
-    for i in range(3):
-        slot_ref[where_ref[i]] = gram_refs[i][...]
-    slot_ref[where_ref[3]] = gram_of(s)
-    gram = ((slot_ref[0] + slot_ref[1]) + slot_ref[2]) + slot_ref[3]
+    gram = (g0_ref[...] + g2_ref[...]) + (g1_ref[...] + gram_of(s))
     for j in range(8):
-        o_ref[j // 4, j % 4, K:, :] = gram[16 * j : 16 * j + 16, :]
+        o_ref[j // 4, j % 4, K:, :] = gram[32 * (j % 4) : 32 * (j % 4) + 32, :]
     high, low = halves(s)
     both_s = jnp.concatenate([high, low], 1)
     for lo in range(0, snaps, 256):
@@ -212,47 +211,48 @@
             o_ref[j // 4, j % 4, :K, :] = prev_ref[:, at] + both_ref[:K, at]
 
 
-def last_piece(where, high, low, s, prev, grams):
+def last_piece(high, low, s, prev, grams):
     rows, snaps = s.shape[0], high.shape[1]
     return pl.pallas_call(
         last_kernel,
-        in_specs=[smem()] + [vmem()] * 7,
+        in_specs=[vmem()] * 7,
         out_specs=vmem(),
-        out_shape=jax.ShapeDtypeStruct((2, 4, K + 16, K), F32),
-        scratch_shapes=[pltpu.VMEM((4, K, K), F32), pltpu.VMEM((2 * K, snaps), F32)],
+        out_shape=jax.ShapeDtypeStruct((2, 4, K + 32, K), F32),
+        scratch_shapes=[pltpu.VMEM((2 * K, snaps), F32)],
         compiler_params=params(),
         cost_estimate=cost(6 * rows * snaps * K, 4 * (rows + 2 * K) * snaps),
         name="last_piece",
-    )(where, high, low, s, prev, *grams)
+    )(high, low, s, prev, *grams)
 
 
 def inverse_factor(w_ref, o_ref):
-    lane = lax.broadcasted_iota(jnp.int32, (NB, K), 1)
-    row = lax.broadcasted_iota(jnp.int32, (NB, K), 0)
     for lo in range(0, K, NB):
         hi = lo + NB
-        block = w_ref[lo:hi, :]
-        cols = [jnp.broadcast_to(block[:, lo + c : lo + c + 1], (NB, K)) for c in range(NB)]
-        inv = [jnp.where(row == c, 1.0, 0.0) for c in range(NB)]
-        for k in range(NB):
-            pivot = cols[k][k : k + 1, :]
-            r = lax.rsqrt(pivot)
-            r = r * (1.5 - 0.5 * (pivot * r) * r)
-            m = jnp.where(row > k, cols[k] * r, 0.0)
-            for c in range(k + 1, NB):
-                cols[c] = cols[c] - m * (cols[c][k : k + 1, :] * r)
-            for c in range(k + 1):
-                scaled = inv[c][k : k + 1, :] * r
-                inv[c] = jnp.where(row == k, scaled, inv[c] - m * scaled)
-        inside = (lane >= lo) & (lane < hi)
-        block = jnp.where(inside, jnp.where(lane - lo == row, 1.0, 0.0), block)
-        terms = [inv[c] * block[c : c + 1, :] for c in range(NB)]
-        while len(terms) > 1:
-            terms = [a + b for a, b in zip(terms[::2], terms[1::2])]
-        done = terms[0]
-        o_ref[lo:hi, :] = jnp.where(lane < hi, done, 0.0)
+        rest = w_ref[lo:hi, :]
+        tops = []
+        for at in range(lo, hi, SB):
+            lane = lax.broadcasted_iota(jnp.int32, (hi - at, K), 1)
+            row = lax.broadcasted_iota(jnp.int32, (hi - at, K), 0)
+            cols = [jnp.broadcast_to(rest[:, at + c : at + c + 1], rest.shape) for c in range(SB)]
+            inside = (lane >= at) & (lane < at + SB)
+            rest = jnp.where(inside, jnp.where(lane - at == row, 1.0, 0.0), rest)
+            pivots = jnp.ones((SB, K), F32)
+            for k in range(SB):
+                pivot = cols[k][k : k + 1, :]
+                pivots = jnp.where(row[:SB] == k, pivot, pivots)
+                m = jnp.where(row > k, cols[k], 0.0) * (1.0 / pivot)
+                for c in range(k + 1, SB):
+                    cols[c] = cols[c] - m * cols[c][k : k + 1, :]
+                rest = rest - m * rest[k : k + 1, :]
+            r = lax.rsqrt(pivots)
+            r = r * (1.5 - 0.5 * (pivots * r) * r)
+            top = rest[:SB] * r
+            rest = rest[SB:]
+            lane = lane[:SB]
+            o_ref[at : at + SB, :] = jnp.where(lane < at + SB, top, 0.0)
+            tops.append(jnp.where((lane >= at + SB) & (lane < hi), 0.0, top))
         if hi < K:
-            h, m, l = thirds(done)
+            h, m, l = thirds(jnp.concatenate(tops, 0))
             left = jnp.concatenate([h, h, m, h, l, m], 0).astype(BF16)
             right = jnp.concatenate([h, m, h, l, h, m], 0).astype(BF16)
             update = dot(left, right, TN)
@@ -261,35 +261,58 @@
             w_ref[hi:, :] = jnp.where(inside, 0.0, w_ref[hi:, :]) - update[hi:, :]
 
 
-def middle_kernel(where_ref, mine_ref, other_ref, inv_ref, back_ref, gram_ref, w_ref, raw_ref):
+def factor_kernel(where_ref, quarters_ref, inv_ref, w_ref):
+    for shift in range(4):
+        at = (where_ref[0] + 4 - shift) % 4
+        w_ref[pl.ds(pl.multiple_of(at * 32, 32), 32), :] = quarters_ref[shift]
+    inverse_factor(w_ref, inv_ref)
+
+
+def factor(where, quarters):
+    return pl.pallas_call(
+        factor_kernel,
+        in_specs=[smem(), vmem()],
+        out_specs=vmem(),
+        out_shape=jax.ShapeDtypeStruct((K, K), F32),
+        scratch_shapes=[pltpu.VMEM((K, K), F32)],
+        compiler_params=params(),
+        cost_estimate=cost(24 * 8 * K * K * K, 8 * K * K),
+        name="factor",
+    )(where, quarters)
+
+
+def back_kernel(where_ref, inv_ref, mine_ref, other_ref, back_ref, gram_ref, raw_ref):
     x, c = where_ref[0], where_ref[1]
     for half, ref in ((c, mine_ref), (1 - c, other_ref)):
         for shift in range(4):
             at = half * 4 + (x + 4 - shift) % 4
-            raw_ref[:, pl.ds(pl.multiple_of(at * K, K), K)] = ref[shift, :K, :]
-            w_ref[pl.ds(pl.multiple_of(at * 16, 16), 16), :] = ref[shift, K:, :]
-    inverse_factor(w_ref, inv_ref)
-    back = dot(inv_ref[...], raw_ref[...], NN, HIGHEST)
+            raw_ref[:, pl.ds(pl.multiple_of(at * K, K), K)] = ref[shift]
+    inv_high, inv_low = halves(inv_ref[...])
+    raw_high, raw_low = halves(raw_ref[...])
+    back = dot(
+        jnp.concatenate([inv_high, inv_high, inv_low], 1),
+        jnp.concatenate([raw_high, raw_low, raw_high], 0),
+        NN,
+    )
     back_ref[...] = back
-    gram_ref[...] = dot(back, back, NT, HIGHEST)
-
-
-def middle(where, mine, other):
+    high, mid, low = (part.astype(BF16) for part in thirds(back))
+    gram_ref[...] = folded(
+        dot(jnp.concatenate([high, mid, low], 0), jnp.concatenate([high, mid], 0), NT)
+    )
+
+
+def back_of(where, inv, mine, other):
     snaps = 8 * K
     return pl.pallas_call(
-        middle_kernel,
-        in_specs=[smem(), vmem(), vmem()],
-        out_specs=[vmem()] * 3,
-        out_shape=[
-            jax.ShapeDtypeStruct((K, K), F32),
-            jax.ShapeDtypeStruct((K, snaps), F32),
-            jax.ShapeDtypeStruct((K, K), F32),
-        ],
-        scratch_shapes=[pltpu.VMEM((K, K), F32), pltpu.VMEM((K, snaps), F32)],
+        back_kernel,
+        in_specs=[smem(), vmem(), vmem(), vmem()],
+        out_specs=[vmem()] * 2,
+        out_shape=[jax.ShapeDtypeStruct((K, snaps), F32), jax.ShapeDtypeStruct((K, K), F32)],
+        scratch_shapes=[pltpu.VMEM((K, snaps), F32)],
         compiler_params=params(),
         cost_estimate=cost(24 * snaps * K * K, 8 * snaps * K),
-        name="middle",
-    )(where, mine, other)
+        name="back",
+    )(where, inv, mine, other)
 
 
 def space_kernel(where_ref, inv_ref, back_t_ref, *refs):
@@ -299,7 +322,8 @@
     for i, ref in enumerate(s_refs):
         at = pl.multiple_of(where_ref[i] * rows, rows)
         o_ref[pl.ds(at, rows), :] = dot(ref[...], inv, NT, HIGHEST)
-    back_ref[...] = back_t_ref[...].T
+    high, low = halves(back_t_ref[...].T)
+    back_ref[...] = jnp.concatenate([high, high, low], 1)
 
 
 def space(where, inv, back_t, pieces):
@@ -309,37 +333,31 @@
         space_kernel,
         in_specs=[smem()] + [vmem()] * 6,
         out_specs=[vmem()] * 2,
-        out_shape=[jax.ShapeDtypeStruct((rows, K), F32), jax.ShapeDtypeStruct((snaps, K), F32)],
+        out_shape=[jax.ShapeDtypeStruct((rows, K), F32), jax.ShapeDtypeStruct((snaps, 3 * K), BF16)],
         compiler_params=params(),
         cost_estimate=cost(12 * rows * K * K, 8 * (rows + snaps) * K),
         name="space",
     )(where, inv, back_t, *pieces)
 
 
-def time_kernel(where_ref, back_ref, *refs):
-    gram_refs, (o_ref, slot_ref, w_ref, inv_ref) = refs[:4], refs[4:]
-    for i, ref in enumerate(gram_refs):
-        slot_ref[where_ref[i]] = ref[...]
-    w_ref[...] = ((slot_ref[0] + slot_ref[1]) + slot_ref[2]) + slot_ref[3]
+def time_kernel(back_ref, g0_ref, g1_ref, g2_ref, g3_ref, o_ref, w_ref, inv_ref):
+    w_ref[...] = (g0_ref[...] + g2_ref[...]) + (g1_ref[...] + g3_ref[...])
     inverse_factor(w_ref, inv_ref)
-    o_ref[...] = dot(back_ref[...], inv_ref[...], NT, HIGHEST)
-
-
-def time_basis_of(where, back, grams):
+    high, low = halves(inv_ref[...])
+    o_ref[...] = dot(back_ref[...], jnp.concatenate([high, low, high], 1), NT)
+
+
+def time_basis_of(back, grams):
     return pl.pallas_call(
         time_kernel,
-        in_specs=[smem()] + [vmem()] * 5,
+        in_specs=[vmem()] * 5,
         out_specs=vmem(),
-        out_shape=jax.ShapeDtypeStruct(back.shape, F32),
-        scratch_shapes=[
-            pltpu.VMEM((4, K, K), F32),
-            pltpu.VMEM((K, K), F32),
-            pltpu.VMEM((K, K), F32),
-        ],
+        out_shape=jax.ShapeDtypeStruct((back.shape[0], K), F32),
+        scratch_shapes=[pltpu.VMEM((K, K), F32)] * 2,
         compiler_params=params(),
         cost_estimate=cost(12 * back.shape[0] * K * K, 8 * back.shape[0] * K),
         name="time_basis",
-    )(where, back, *grams)
+    )(back, *grams)
 
 
 def shifted(value, axis, shift):
@@ -367,21 +385,24 @@
     blocks = scalars(*owner)
     raw, g0, high, low, high3, low3 = own_piece(anomalies, own, blocks)
     raw, g1, g2 = two_pieces(high, low, s1, s2, raw)
-    stacked = last_piece(blocks, high3, low3, s3, raw, (g0, g1, g2))
+    stacked = last_piece(high3, low3, s3, raw, (g0, g1, g2))
 
     part = pick(stacked, c) + shifted(pick(stacked, 1 - c), "c", 1)
-    arrived = [shifted(pick(part, (x + shift) % 4), "x", shift) for shift in (2, 1, 3)]
+    arrived = [shifted(pick(part, (x + shift) % 4), "x", shift) for shift in (1, 3, 2)]
     part = pick(part, x) + arrived[0] + arrived[1] + arrived[2]
-    copies = jnp.broadcast_to(part[None], (8,) + part.shape)
-    part = jnp.sum(lax.all_to_all(copies, "z", 0, 0), 0)
-    e2, e1, e3 = (shifted(part, "x", shift) for shift in (2, 1, 3))
-    mine = jnp.stack([part, e1, e2, e3])
+    part = part + lax.ppermute(part, "z", [(i, i ^ 1) for i in range(8)])
+    z1, z3, z2 = (shifted(part, "z", shift) for shift in (2, 6, 4))
+    part = (part + z2) + (z1 + z3)
+    e1, e3, e2 = (shifted(part, "x", shift) for shift in (1, 3, 2))
+    mine = jnp.stack([piece[:K] for piece in (part, e1, e2, e3)])
+    quarters = jnp.stack([piece[K:] for piece in (part, e1, e2, e3)])
     other = shifted(mine, "c", 1)
-    inv, back_t, gram = middle(scalars(x, c), mine, other)
-
-    t2, t1, t3 = (shifted(gram, "y", shift) for shift in (2, 1, 3))
+    inv = factor(scalars(x), quarters)
+    back_t, gram = back_of(scalars(x, c), inv, mine, other)
+
+    t1, t3, t2 = (shifted(gram, "y", shift) for shift in (1, 3, 2))
     space_basis, back = space(scalars(*owner), inv, back_t, (own, s1, s2, s3))
-    time_basis = time_basis_of(scalars(*owner), back, (gram, t1, t2, t3))
+    time_basis = time_basis_of(back, (gram, t1, t2, t3))
     return (space_basis, time_basis)
 
 

time: 105 us -> 92.9 us (0.88)
  blocking collectives: 23.7 us -> 0 us
  starting transfers between devices: 32 us -> 40 us
  waiting for transfers between devices: 17.9 us -> 25.7 us
  Pallas kernels: 29.7 us -> 25.7 us
    all_to_all x1 -> x0, blocking collectives: 23.7 us -> none  [on_device(): part = jnp.sum(lax.all_to_all(copies, 'z', 0, 0), 0)]
    ppermute x17 -> x20, starting transfers between devices: 32 us -> 38.2 us  [shifted(): return lax.ppermute(value, axis, [(i, (i + shift) % n) for i in range(n)])]
    ppermute x17 -> x20, waiting for transfers between devices: 17.9 us -> 23.9 us  [shifted(): return lax.ppermute(value, axis, [(i, (i + shift) % n) for i in range(n)])]
    pallas_call x3 -> x4, Pallas kernels: 13.2 us -> 9.1 us  [the longest x1 4.07 us: time_basis_of(): pl.pallas_call(time_kernel, in_specs=[vmem()] * 5, out_specs=vmem(), out_...]
    ppermute x0 -> x1, starting transfers between devices: none -> 1.83 us  [on_device(): part = part + lax.ppermute(part, 'z', [(i, i ^ 1) for i in range(8)])]
    ppermute x0 -> x1, waiting for transfers between devices: none -> 1.83 us  [on_device(): part = part + lax.ppermute(part, 'z', [(i, i ^ 1) for i in range(8)])]
  transfers between devices with their start and end apart: 17 -> 21, of which waited for: 8 -> 13; matrix products, arithmetic and copies ran while one was open for 0% -> 0% of each run, Pallas kernels for 12% -> 17%
where the time goes in v4:
time: 92.9 us; the launch traced here: 92.8 us
  starting transfers between devices  40 us (43%)
  Pallas kernels  25.7 us (28%)
  waiting for transfers between devices  25.7 us (28%)
    ppermute x20, starting transfers between devices, shifted(): return lax.ppermute(value, axis, [(i, (i + shift) % n) for i in range(n)])  38.2 us
    ppermute x20, waiting for transfers between devices, shifted(): return lax.ppermute(value, axis, [(i, (i + shift) % n) for i in range(n)])  23.9 us
    pallas_call x3, Pallas kernels, sketch_pieces(): pl.pallas_call(functools.partial(sketch_kernel, count), in_specs=[smem()]...  8.45 us
    pallas_call x1, Pallas kernels, own_piece(): pl.pallas_call(own_kernel, in_specs=[smem(), pl.BlockSpec(memory_space=pl...  4.36 us
    pallas_call x1, Pallas kernels, time_basis_of(): pl.pallas_call(time_kernel, in_specs=[vmem()] * 5, out_specs=vmem(), out_...  4.07 us
    pallas_call x1, Pallas kernels, factor(): pl.pallas_call(factor_kernel, in_specs=[smem(), vmem()], out_specs=vmem()...  2.92 us
    pallas_call x1, Pallas kernels, space(): pl.pallas_call(space_kernel, in_specs=[smem()] + [vmem()] * 6, out_specs=...  2.54 us
  transfers between devices with their start and end apart: 21, of which 13 were waited for; matrix products, arithmetic and copies ran while one was open for 0% of the time, Pallas kernels for 17%

profile of v4, /device:TPU:1, one launch (start us, length us, event | category | flops | bytes accessed | tf_op | source)
XLA Modules:
  0.0 92.8 jit_solution(4911829182986258494)
XLA Ops:
  0.7 3.7 %sketch_pieces.5 = (f32[512,128]{1,0:T(8,128)S(1)}, f32[512,128]{1,0:T(8,128)S(1)}) custom-call(s32[2]{0:T(128)S(1)} %pad_add_fusion.1.where_ref, f32[2048,1024]{1,0:T(8,128)} %a_ref.7, f32[1024,128]{1,0:T(8,128)} %b_ref.5), custom_call_target="tpu_custom_call" | custom-call | flops 805306368 | bytes 4718592 | tf_op jit(solution)/shard_map/sketch_pieces/pallas_call | solution.py:106
  4.5 2.2 %collective-permute-start.1 = (f32[512,128]{1,0:T(8,128)S(1)}, f32[512,128]{1,0:T(8,128)S(1)}, u32[]{:S(2)}, u32[]{:S(2)}) collective-permute-start(f32[512,128]{1,0:T(8,128)S(1)} %get-tuple-element.17), channel_id=1, source_target_pairs={{0,1},{1,2},{2,3},{3,0},{4,5},{5,6},{6,7},{7,4},{8,9},{9,10},{10,1... | collective-permute-start | bytes 786440 | tf_op jit(solution)/shard_map/ppermute | solution.py:365
  6.7 1.5 %collective-permute-start.2 = (f32[512,128]{1,0:T(8,128)S(1)}, f32[512,128]{1,0:T(8,128)S(1)}, u32[]{:S(2)}, u32[]{:S(2)}) collective-permute-start(f32[512,128]{1,0:T(8,128)S(1)} %get-tuple-element.18), channel_id=1, source_target_pairs={{0,3},{1,0},{2,1},{3,2},{4,7},{5,4},{6,5},{7,6},{8,11},{9,8},{10,9... | collective-permute-start | bytes 786440 | tf_op jit(solution)/shard_map/ppermute | solution.py:365
  8.2 2.4 %sketch_pieces.4 = f32[512,128]{1,0:T(8,128)S(1)} custom-call(s32[1]{0:T(128)} %bitcast.2.where_ref, f32[2048,1024]{1,0:T(8,128)} %a_ref.7, f32[1024,128]{1,0:T(8,128)} %b_ref.5), custom_call_target="tpu_custom_call" | custom-call | flops 402653184 | bytes 2621440 | tf_op jit(solution)/shard_map/sketch_pieces/pallas_call | solution.py:106
  10.6 1.6 %collective-permute-start = (f32[512,128]{1,0:T(8,128)S(1)}, f32[512,128]{1,0:T(8,128)S(1)}, u32[]{:S(2)}, u32[]{:S(2)}) collective-permute-start(f32[512,128]{1,0:T(8,128)S(1)} %sketch_pieces.4), channel_id=1, source_target_pairs={{0,2},{1,3},{2,0},{3,1},{4,6},{5,7},{6,4},{7,5},{8,10},{9,11},{10,... | collective-permute-start | bytes 786440 | tf_op jit(solution)/shard_map/ppermute | solution.py:365
  12.2 2.4 %sketch_pieces.3 = f32[512,128]{1,0:T(8,128)S(1)} custom-call(s32[1]{0:T(128)} %bitcast.where_ref, f32[2048,1024]{1,0:T(8,128)} %a_ref.7, f32[1024,128]{1,0:T(8,128)} %b_ref.5), custom_call_target="tpu_custom_call" | custom-call | flops 402653184 | bytes 2621440 | tf_op jit(solution)/shard_map/sketch_pieces/pallas_call | solution.py:106
  14.6 5.1 %collective-permute-done = f32[512,128]{1,0:T(8,128)S(1)} collective-permute-done((f32[512,128]{1,0:T(8,128)S(1)}, f32[512,128]{1,0:T(8,128)S(1)}, u32[]{:S(2)}, u32[]{:S(2)}) %collective-permute-start) | collective-permute-done | bytes 262176 | tf_op jit(solution)/shard_map/ppermute | solution.py:365
  19.7 1.5 %collective-permute-start.4 = (f32[512,128]{1,0:T(8,128)S(1)}, f32[512,128]{1,0:T(8,128)S(1)}, u32[]{:S(2)}, u32[]{:S(2)}) collective-permute-start(f32[512,128]{1,0:T(8,128)S(1)} %add_add_fusion.s_ref.refs_0_), channel_id=1, source_target_pairs={{0,1},{1,2},{2,3},{3,0},{4,5},{5,6},{6,7},{7,4},{8,9},{9,10},{10,1... | collective-permute-start | bytes 786440 | tf_op jit(solution)/shard_map/ppermute | solution.py:365
  21.3 2.0 %collective-permute-start.5 = (f32[512,128]{1,0:T(8,128)S(1)}, f32[512,128]{1,0:T(8,128)S(1)}, u32[]{:S(2)}, u32[]{:S(2)}) collective-permute-start(f32[512,128]{1,0:T(8,128)S(1)} %add_add_fusion.s_ref.refs_0_), channel_id=1, source_target_pairs={{0,2},{1,3},{2,0},{3,1},{4,6},{5,7},{6,4},{7,5},{8,10},{9,11},{10,... | collective-permute-start | bytes 786440 | tf_op jit(solution)/shard_map/ppermute | solution.py:365
  23.9 4.4 %own_piece.1 = (f32[128,1024]{1,0:T(8,128)S(1)}, f32[128,128]{1,0:T(8,128)S(1)}, bf16[1024,1024]{1,0:T(8,128)(2,1)S(1)}, bf16[1024,1024]{1,0:T(8,128)(2,1)S(1)},...) custom-call(s32[4]{0:T(128)S(1)} %pad_add_fusion.where_ref, f32[2048,1024]{1,0:T(8,128)} %a_ref.7, ...), custom_call_target="tpu_custom_call" | custom-call | flops 402653184 | bytes 9437184 | tf_op jit(solution)/shard_map/own_piece/pallas_call | solution.py:157
  28.2 5.0 %collective-permute-done.5.s2_ref.refs_2_ = f32[512,128]{1,0:T(8,128)S(1)} collective-permute-done((f32[512,128]{1,0:T(8,128)S(1)}, f32[512,128]{1,0:T(8,128)S(1)}, u32[]{:S(2)}, u32[]{:S(2)}) %collective-permute-start.5) | collective-permute-done | bytes 262176 | tf_op jit(solution)/shard_map/ppermute | solution.py:365
  35.3 3.0 %collective-permute-start.6 = (f32[4,160,128]{2,1,0:T(8,128)S(1)}, f32[4,160,128]{2,1,0:T(8,128)S(1)}, u32[]{:S(2)}, u32[]{:S(2)}) collective-permute-start(f32[4,160,128]{2,1,0:T(8,128)S(1)} %dynamic-slice_bitcast_fusion), channel_id=1, source_target_pairs={{0,4},{4,0},{1,5},{5,1},{2,6},{6,2},{3,7},{7,3},{8,12},{12,8},{9,1... | collective-permute-start | bytes 983048 | tf_op jit(solution)/shard_map/ppermute | solution.py:365
  38.3 1.3 %collective-permute-done.6 = f32[4,160,128]{2,1,0:T(8,128)S(1)} collective-permute-done((f32[4,160,128]{2,1,0:T(8,128)S(1)}, f32[4,160,128]{2,1,0:T(8,128)S(1)}, u32[]{:S(2)}, u32[]{:S(2)}) %collective-permute-start.6) | collective-permute-done | bytes 327712 | tf_op jit(solution)/shard_map/ppermute | solution.py:365
  39.6 1.6 %collective-permute-start.7 = (f32[160,128]{1,0:T(8,128)S(1)}, f32[160,128]{1,0:T(8,128)S(1)}, u32[]{:S(2)}, u32[]{:S(2)}) collective-permute-start(f32[160,128]{1,0:T(8,128)S(1)} %get-tuple-element.32), channel_id=1, source_target_pairs={{0,64},{64,128},{128,192},{192,0},{1,65},{65,129},{129,193},{193,1... | collective-permute-start | bytes 245768 | tf_op jit(solution)/shard_map/ppermute | solution.py:365
  41.3 1.4 %collective-permute-start.8 = (f32[160,128]{1,0:T(8,128)S(1)}, f32[160,128]{1,0:T(8,128)S(1)}, u32[]{:S(2)}, u32[]{:S(2)}) collective-permute-start(f32[160,128]{1,0:T(8,128)S(1)} %get-tuple-element.34), channel_id=1, source_target_pairs={{0,192},{64,0},{128,64},{192,128},{1,193},{65,1},{129,65},{193,129... | collective-permute-start | bytes 245768 | tf_op jit(solution)/shard_map/ppermute | solution.py:365
  42.6 1.6 %collective-permute-start.9 = (f32[160,128]{1,0:T(8,128)S(1)}, f32[160,128]{1,0:T(8,128)S(1)}, u32[]{:S(2)}, u32[]{:S(2)}) collective-permute-start(f32[160,128]{1,0:T(8,128)S(1)} %get-tuple-element.33), channel_id=1, source_target_pairs={{0,128},{64,192},{128,0},{192,64},{1,129},{65,193},{129,1},{193,65... | collective-permute-start | bytes 245768 | tf_op jit(solution)/shard_map/ppermute | solution.py:365
  44.8 2.6 %collective-permute-done.9 = f32[160,128]{1,0:T(8,128)S(1)} collective-permute-done((f32[160,128]{1,0:T(8,128)S(1)}, f32[160,128]{1,0:T(8,128)S(1)}, u32[]{:S(2)}, u32[]{:S(2)}) %collective-permute-start.9) | collective-permute-done | bytes 81952 | tf_op jit(solution)/shard_map/ppermute | solution.py:365
  47.4 1.8 %collective-permute-start.10 = (f32[160,128]{1,0:T(8,128)S(1)}, f32[160,128]{1,0:T(8,128)S(1)}, u32[]{:S(2)}, u32[]{:S(2)}) collective-permute-start(f32[160,128]{1,0:T(8,128)S(1)} %fusion.1), channel_id=1, source_target_pairs={{0,8},{8,0},{16,24},{24,16},{32,40},{40,32},{48,56},{56,48},{1,9},... | collective-permute-start | bytes 245768 | tf_op jit(solution)/shard_map/ppermute | solution.py:393
  49.3 1.8 %collective-permute-done.10 = f32[160,128]{1,0:T(8,128)S(1)} collective-permute-done((f32[160,128]{1,0:T(8,128)S(1)}, f32[160,128]{1,0:T(8,128)S(1)}, u32[]{:S(2)}, u32[]{:S(2)}) %collective-permute-start.10) | collective-permute-done | bytes 81952 | tf_op jit(solution)/shard_map/ppermute | solution.py:393
  51.1 6.8 %collective-permute-start.11 = (f32[160,128]{1,0:T(8,128)S(1)}, f32[160,128]{1,0:T(8,128)S(1)}, u32[]{:S(2)}, u32[]{:S(2)}) collective-permute-start(f32[160,128]{1,0:T(8,128)S(1)} %add.122), channel_id=1, source_target_pairs={{0,32},{8,40},{16,48},{24,56},{32,0},{40,8},{48,16},{56,24},{1,33}... | collective-permute-start | bytes 245768 | tf_op jit(solution)/shard_map/ppermute | solution.py:365
  59.1 2.4 %collective-permute-start.13 = (f32[160,128]{1,0:T(8,128)S(1)}, f32[160,128]{1,0:T(8,128)S(1)}, u32[]{:S(2)}, u32[]{:S(2)}) collective-permute-start(f32[160,128]{1,0:T(8,128)S(1)} %add.122), channel_id=1, source_target_pairs={{0,48},{8,56},{16,0},{24,8},{32,16},{40,24},{48,32},{56,40},{1,49}... | collective-permute-start | bytes 245768 | tf_op jit(solution)/shard_map/ppermute | solution.py:365
  61.6 3.6 %collective-permute-done.12 = f32[160,128]{1,0:T(8,128)S(1)} collective-permute-done((f32[160,128]{1,0:T(8,128)S(1)}, f32[160,128]{1,0:T(8,128)S(1)}, u32[]{:S(2)}, u32[]{:S(2)}) %collective-permute-start.12) | collective-permute-done | bytes 81952 | tf_op jit(solution)/shard_map/ppermute | solution.py:365
  65.2 1.7 %collective-permute-start.16 = (f32[160,128]{1,0:T(8,128)S(1)}, f32[160,128]{1,0:T(8,128)S(1)}, u32[]{:S(2)}, u32[]{:S(2)}) collective-permute-start(f32[160,128]{1,0:T(8,128)S(1)} %add_add_fusion.1), channel_id=1, source_target_pairs={{0,192},{64,0},{128,64},{192,128},{1,193},{65,1},{129,65},{193,129... | collective-permute-start | bytes 245768 | tf_op jit(solution)/shard_map/ppermute | solution.py:365
  67.0 1.6 %collective-permute-start.15 = (f32[160,128]{1,0:T(8,128)S(1)}, f32[160,128]{1,0:T(8,128)S(1)}, u32[]{:S(2)}, u32[]{:S(2)}) collective-permute-start(f32[160,128]{1,0:T(8,128)S(1)} %add_add_fusion.1), channel_id=1, source_target_pairs={{0,128},{64,192},{128,0},{192,64},{1,129},{65,193},{129,1},{193,65... | collective-permute-start | bytes 245768 | tf_op jit(solution)/shard_map/ppermute | solution.py:365
  68.6 3.1 %collective-permute-done.15 = f32[160,128]{1,0:T(8,128)S(1)} collective-permute-done((f32[160,128]{1,0:T(8,128)S(1)}, f32[160,128]{1,0:T(8,128)S(1)}, u32[]{:S(2)}, u32[]{:S(2)}) %collective-permute-start.15) | collective-permute-done | bytes 81952 | tf_op jit(solution)/shard_map/ppermute | solution.py:365
  71.8 1.3 %collective-permute-done.14 = f32[160,128]{1,0:T(8,128)S(1)} collective-permute-done((f32[160,128]{1,0:T(8,128)S(1)}, f32[160,128]{1,0:T(8,128)S(1)}, u32[]{:S(2)}, u32[]{:S(2)}) %collective-permute-start.14) | collective-permute-done | bytes 81952 | tf_op jit(solution)/shard_map/ppermute | solution.py:365
  73.1 4.5 %collective-permute-start.17 = (f32[4,128,128]{2,1,0:T(8,128)S(1)}, f32[4,128,128]{2,1,0:T(8,128)S(1)}, u32[]{:S(2)}, u32[]{:S(2)}) collective-permute-start(f32[4,128,128]{2,1,0:T(8,128)S(1)} %pad_maximum_fusion.mine_ref), channel_id=1, source_target_pairs={{0,4},{4,0},{1,5},{5,1},{2,6},{6,2},{3,7},{7,3},{8,12},{12,8},{9,1... | collective-permute-start | bytes 786440 | tf_op jit(solution)/shard_map/ppermute | solution.py:365
  77.6 2.9 %factor.1.inv_ref = f32[128,128]{1,0:T(8,128)S(1)} custom-call(s32[1]{0:T(128)} %bitcast.4.where_ref, f32[4,32,128]{2,1,0:T(8,128)S(1)} %pad_maximum_fusion.1.quarters_ref), custom_call_target="tpu_custom_call" | custom-call | flops 402653184 | bytes 131072 | tf_op jit(solution)/shard_map/factor/pallas_call | solution.py:272
  80.5 1.4 %back.1 = (f32[128,1024]{1,0:T(8,128)S(1)}, f32[128,128]{1,0:T(8,128)S(1)}) custom-call(s32[2]{0:T(128)S(1)} %pad_add_fusion.2.where_ref, f32[128,128]{1,0:T(8,128)S(1)} %factor.1.inv_ref, f32[4,128,128]{2,1,0:T(8,128)S(1)} %pad_maximum_fusion.mine_ref, f32[4,128,128]{2,1,0:T(8,128)S(1)} %collective-permute-done.17.other_ref), custom_call_target="tpu_custom_call" | custom-call | flops 402653184 | bytes 1048576 | tf_op jit(solution)/shard_map/back/pallas_call | solution.py:306
  82.0 2.9 %collective-permute-start.19 = (f32[128,128]{1,0:T(8,128)S(1)}, f32[128,128]{1,0:T(8,128)S(1)}, u32[]{:S(2)}, u32[]{:S(2)}) collective-permute-start(f32[128,128]{1,0:T(8,128)S(1)} %get-tuple-element.31.g0_ref), channel_id=1, source_target_pairs={{0,2},{1,3},{2,0},{3,1},{4,6},{5,7},{6,4},{7,5},{8,10},{9,11},{10,... | collective-permute-start | bytes 196616 | tf_op jit(solution)/shard_map/ppermute | solution.py:365
  84.9 2.5 %space.1 = (f32[2048,128]{1,0:T(8,128)}, bf16[1024,384]{1,0:T(8,128)(2,1)S(1)}) custom-call(s32[4]{0:T(128)S(1)} %pad_add_fusion.where_ref, f32[128,128]{1,0:T(8,128)S(1)} %factor.1.inv_ref, f32[128,1024]{1,0:T(8,128)S(1)} %get-tuple-element.28.back_t_ref, f32[512,128]{1,0:T(8,128)S(1)} %add_add_fusion.s_ref.refs_0_, ...), custom_call_target="tpu_custom_call" | custom-call | flops 402653184 | bytes 3145728 | tf_op jit(solution)/shard_map/space/pallas_call | solution.py:332
  88.7 4.1 %time_basis.1 = f32[1024,128]{1,0:T(8,128)} custom-call(bf16[1024,384]{1,0:T(8,128)(2,1)S(1)} %get-tuple-element.30.back_ref, f32[128,128]{1,0:T(8,128)S(1)} %get-tuple-element.31.g0_ref, f32[128,128]{1,0:T(8,128)S(1)} %collective-permute-done.18.g1_ref, f32[128,128]{1,0:T(8,128)S(1)} %collective-permute-done.19.g2_ref, ...), custom_call_target="tpu_custom_call" | custom-call | flops 201326592 | bytes 1048576 | tf_op jit(solution)/shard_map/time_basis/pallas_call | solution.py:351
  (40 shorter events, 6.2 us)
Async XLA Ops:
  4.5 10.1 %collective-permute-start.1 = (f32[512,128]{1,0:T(8,128)S(1)}, f32[512,128]{1,0:T(8,128)S(1)}, u32[]{:S(2)}, u32[]{:S(2)}) collective-permute-start(f32[512,128]{1,0:T(8,128)S(1)} %get-tuple-element.17), channel_id=1, source_target_pairs={{0,1},{1,2},{2,3},{3,0},{4,5},{5,6},{6,7},{7,4},{8,9},{9,10},{10,1... | collective-permute-start | bytes 786440 | tf_op jit(solution)/shard_map/ppermute | solution.py:365
  6.7 7.9 %collective-permute-start.2 = (f32[512,128]{1,0:T(8,128)S(1)}, f32[512,128]{1,0:T(8,128)S(1)}, u32[]{:S(2)}, u32[]{:S(2)}) collective-permute-start(f32[512,128]{1,0:T(8,128)S(1)} %get-tuple-element.18), channel_id=1, source_target_pairs={{0,3},{1,0},{2,1},{3,2},{4,7},{5,4},{6,5},{7,6},{8,11},{9,8},{10,9... | collective-permute-start | bytes 786440 | tf_op jit(solution)/shard_map/ppermute | solution.py:365
  10.6 9.1 %collective-permute-start = (f32[512,128]{1,0:T(8,128)S(1)}, f32[512,128]{1,0:T(8,128)S(1)}, u32[]{:S(2)}, u32[]{:S(2)}) collective-permute-start(f32[512,128]{1,0:T(8,128)S(1)} %sketch_pieces.4), channel_id=1, source_target_pairs={{0,2},{1,3},{2,0},{3,1},{4,6},{5,7},{6,4},{7,5},{8,10},{9,11},{10,... | collective-permute-start | bytes 786440 | tf_op jit(solution)/shard_map/ppermute | solution.py:365
  19.7 8.5 %collective-permute-start.4 = (f32[512,128]{1,0:T(8,128)S(1)}, f32[512,128]{1,0:T(8,128)S(1)}, u32[]{:S(2)}, u32[]{:S(2)}) collective-permute-start(f32[512,128]{1,0:T(8,128)S(1)} %add_add_fusion.s_ref.refs_0_), channel_id=1, source_target_pairs={{0,1},{1,2},{2,3},{3,0},{4,5},{5,6},{6,7},{7,4},{8,9},{9,10},{10,1... | collective-permute-start | bytes 786440 | tf_op jit(solution)/shard_map/ppermute | solution.py:365
  21.3 12.0 %collective-permute-start.5 = (f32[512,128]{1,0:T(8,128)S(1)}, f32[512,128]{1,0:T(8,128)S(1)}, u32[]{:S(2)}, u32[]{:S(2)}) collective-permute-start(f32[512,128]{1,0:T(8,128)S(1)} %add_add_fusion.s_ref.refs_0_), channel_id=1, source_target_pairs={{0,2},{1,3},{2,0},{3,1},{4,6},{5,7},{6,4},{7,5},{8,10},{9,11},{10,... | collective-permute-start | bytes 786440 | tf_op jit(solution)/shard_map/ppermute | solution.py:365
  23.3 11.2 %collective-permute-start.3 = (f32[512,128]{1,0:T(8,128)S(1)}, f32[512,128]{1,0:T(8,128)S(1)}, u32[]{:S(2)}, u32[]{:S(2)}) collective-permute-start(f32[512,128]{1,0:T(8,128)S(1)} %add_add_fusion.s_ref.refs_0_), channel_id=1, source_target_pairs={{0,3},{1,0},{2,1},{3,2},{4,7},{5,4},{6,5},{7,6},{8,11},{9,8},{10,9... | collective-permute-start | bytes 786440 | tf_op jit(solution)/shard_map/ppermute | solution.py:365
  35.3 4.2 %collective-permute-start.6 = (f32[4,160,128]{2,1,0:T(8,128)S(1)}, f32[4,160,128]{2,1,0:T(8,128)S(1)}, u32[]{:S(2)}, u32[]{:S(2)}) collective-permute-start(f32[4,160,128]{2,1,0:T(8,128)S(1)} %dynamic-slice_bitcast_fusion), channel_id=1, source_target_pairs={{0,4},{4,0},{1,5},{5,1},{2,6},{6,2},{3,7},{7,3},{8,12},{12,8},{9,1... | collective-permute-start | bytes 983048 | tf_op jit(solution)/shard_map/ppermute | solution.py:365
  39.6 5.1 %collective-permute-start.7 = (f32[160,128]{1,0:T(8,128)S(1)}, f32[160,128]{1,0:T(8,128)S(1)}, u32[]{:S(2)}, u32[]{:S(2)}) collective-permute-start(f32[160,128]{1,0:T(8,128)S(1)} %get-tuple-element.32), channel_id=1, source_target_pairs={{0,64},{64,128},{128,192},{192,0},{1,65},{65,129},{129,193},{193,1... | collective-permute-start | bytes 245768 | tf_op jit(solution)/shard_map/ppermute | solution.py:365
  41.3 3.6 %collective-permute-start.8 = (f32[160,128]{1,0:T(8,128)S(1)}, f32[160,128]{1,0:T(8,128)S(1)}, u32[]{:S(2)}, u32[]{:S(2)}) collective-permute-start(f32[160,128]{1,0:T(8,128)S(1)} %get-tuple-element.34), channel_id=1, source_target_pairs={{0,192},{64,0},{128,64},{192,128},{1,193},{65,1},{129,65},{193,129... | collective-permute-start | bytes 245768 | tf_op jit(solution)/shard_map/ppermute | solution.py:365
  42.6 4.8 %collective-permute-start.9 = (f32[160,128]{1,0:T(8,128)S(1)}, f32[160,128]{1,0:T(8,128)S(1)}, u32[]{:S(2)}, u32[]{:S(2)}) collective-permute-start(f32[160,128]{1,0:T(8,128)S(1)} %get-tuple-element.33), channel_id=1, source_target_pairs={{0,128},{64,192},{128,0},{192,64},{1,129},{65,193},{129,1},{193,65... | collective-permute-start | bytes 245768 | tf_op jit(solution)/shard_map/ppermute | solution.py:365
  47.4 3.7 %collective-permute-start.10 = (f32[160,128]{1,0:T(8,128)S(1)}, f32[160,128]{1,0:T(8,128)S(1)}, u32[]{:S(2)}, u32[]{:S(2)}) collective-permute-start(f32[160,128]{1,0:T(8,128)S(1)} %fusion.1), channel_id=1, source_target_pairs={{0,8},{8,0},{16,24},{24,16},{32,40},{40,32},{48,56},{56,48},{1,9},... | collective-permute-start | bytes 245768 | tf_op jit(solution)/shard_map/ppermute | solution.py:393
  51.1 10.5 %collective-permute-start.11 = (f32[160,128]{1,0:T(8,128)S(1)}, f32[160,128]{1,0:T(8,128)S(1)}, u32[]{:S(2)}, u32[]{:S(2)}) collective-permute-start(f32[160,128]{1,0:T(8,128)S(1)} %add.122), channel_id=1, source_target_pairs={{0,32},{8,40},{16,48},{24,56},{32,0},{40,8},{48,16},{56,24},{1,33}... | collective-permute-start | bytes 245768 | tf_op jit(solution)/shard_map/ppermute | solution.py:365
  57.9 7.3 %collective-permute-start.12 = (f32[160,128]{1,0:T(8,128)S(1)}, f32[160,128]{1,0:T(8,128)S(1)}, u32[]{:S(2)}, u32[]{:S(2)}) collective-permute-start(f32[160,128]{1,0:T(8,128)S(1)} %add.122), channel_id=1, source_target_pairs={{0,16},{8,24},{16,32},{24,40},{32,48},{40,56},{48,0},{56,8},{1,17}... | collective-permute-start | bytes 245768 | tf_op jit(solution)/shard_map/ppermute | solution.py:365
  59.1 6.1 %collective-permute-start.13 = (f32[160,128]{1,0:T(8,128)S(1)}, f32[160,128]{1,0:T(8,128)S(1)}, u32[]{:S(2)}, u32[]{:S(2)}) collective-permute-start(f32[160,128]{1,0:T(8,128)S(1)} %add.122), channel_id=1, source_target_pairs={{0,48},{8,56},{16,0},{24,8},{32,16},{40,24},{48,32},{56,40},{1,49}... | collective-permute-start | bytes 245768 | tf_op jit(solution)/shard_map/ppermute | solution.py:365
  65.2 3.4 %collective-permute-start.16 = (f32[160,128]{1,0:T(8,128)S(1)}, f32[160,128]{1,0:T(8,128)S(1)}, u32[]{:S(2)}, u32[]{:S(2)}) collective-permute-start(f32[160,128]{1,0:T(8,128)S(1)} %add_add_fusion.1), channel_id=1, source_target_pairs={{0,192},{64,0},{128,64},{192,128},{1,193},{65,1},{129,65},{193,129... | collective-permute-start | bytes 245768 | tf_op jit(solution)/shard_map/ppermute | solution.py:365
  67.0 4.8 %collective-permute-start.15 = (f32[160,128]{1,0:T(8,128)S(1)}, f32[160,128]{1,0:T(8,128)S(1)}, u32[]{:S(2)}, u32[]{:S(2)}) collective-permute-start(f32[160,128]{1,0:T(8,128)S(1)} %add_add_fusion.1), channel_id=1, source_target_pairs={{0,128},{64,192},{128,0},{192,64},{1,129},{65,193},{129,1},{193,65... | collective-permute-start | bytes 245768 | tf_op jit(solution)/shard_map/ppermute | solution.py:365
  68.5 4.5 %collective-permute-start.14 = (f32[160,128]{1,0:T(8,128)S(1)}, f32[160,128]{1,0:T(8,128)S(1)}, u32[]{:S(2)}, u32[]{:S(2)}) collective-permute-start(f32[160,128]{1,0:T(8,128)S(1)} %add_add_fusion.1), channel_id=1, source_target_pairs={{0,64},{64,128},{128,192},{192,0},{1,65},{65,129},{129,193},{193,1... | collective-permute-start | bytes 245768 | tf_op jit(solution)/shard_map/ppermute | solution.py:365
  73.1 7.5 %collective-permute-start.17 = (f32[4,128,128]{2,1,0:T(8,128)S(1)}, f32[4,128,128]{2,1,0:T(8,128)S(1)}, u32[]{:S(2)}, u32[]{:S(2)}) collective-permute-start(f32[4,128,128]{2,1,0:T(8,128)S(1)} %pad_maximum_fusion.mine_ref), channel_id=1, source_target_pairs={{0,4},{4,0},{1,5},{5,1},{2,6},{6,2},{3,7},{7,3},{8,12},{12,8},{9,1... | collective-permute-start | bytes 786440 | tf_op jit(solution)/shard_map/ppermute | solution.py:365
  81.9 5.5 %collective-permute-start.18 = (f32[128,128]{1,0:T(8,128)S(1)}, f32[128,128]{1,0:T(8,128)S(1)}, u32[]{:S(2)}, u32[]{:S(2)}) collective-permute-start(f32[128,128]{1,0:T(8,128)S(1)} %get-tuple-element.31.g0_ref), channel_id=1, source_target_pairs={{0,1},{1,2},{2,3},{3,0},{4,5},{5,6},{6,7},{7,4},{8,9},{9,10},{10,1... | collective-permute-start | bytes 196616 | tf_op jit(solution)/shard_map/ppermute | solution.py:365
  82.0 6.5 %collective-permute-start.19 = (f32[128,128]{1,0:T(8,128)S(1)}, f32[128,128]{1,0:T(8,128)S(1)}, u32[]{:S(2)}, u32[]{:S(2)}) collective-permute-start(f32[128,128]{1,0:T(8,128)S(1)} %get-tuple-element.31.g0_ref), channel_id=1, source_target_pairs={{0,2},{1,3},{2,0},{3,1},{4,6},{5,7},{6,4},{7,5},{8,10},{9,11},{10,... | collective-permute-start | bytes 196616 | tf_op jit(solution)/shard_map/ppermute | solution.py:365
  84.9 3.8 %collective-permute-start.20 = (f32[128,128]{1,0:T(8,128)S(1)}, f32[128,128]{1,0:T(8,128)S(1)}, u32[]{:S(2)}, u32[]{:S(2)}) collective-permute-start(f32[128,128]{1,0:T(8,128)S(1)} %get-tuple-element.31.g0_ref), channel_id=1, source_target_pairs={{0,3},{1,0},{2,1},{3,2},{4,7},{5,4},{6,5},{7,6},{8,11},{9,8},{10,9... | collective-permute-start | bytes 196616 | tf_op jit(solution)/shard_map/ppermute | solution.py:365

commit v5 on v4

--- a/solution.py
+++ b/solution.py
@@ -376,11 +376,14 @@
     anomalies = pltpu.with_memory_space_constraint(anomalies, pltpu.HBM)
     start_basis = pltpu.with_memory_space_constraint(start_basis, pltpu.HBM)
     (p2,) = sketch_pieces(anomalies, start_basis, [(y + 2) % 4])
-    r2 = shifted(p2, "y", 2)
+    half = p2.shape[0] // 2
+    top, bottom = shifted(p2[:half], "y", 1), shifted(p2[half:], "y", 3)
     p1, p3 = sketch_pieces(anomalies, start_basis, [(y + 1) % 4, (y + 3) % 4])
+    p1 = jnp.concatenate([p1[:half] + top, p1[half:]], 0)
+    p3 = jnp.concatenate([p3[:half], p3[half:] + bottom], 0)
     r1, r3 = shifted(p1, "y", 1), shifted(p3, "y", 3)
     (p0,) = sketch_pieces(anomalies, start_basis, [y])
-    own = p0 + r2 + r1 + r3
+    own = p0 + r1 + r3
     s2, s1, s3 = (shifted(own, "y", shift) for shift in (2, 1, 3))
     blocks = scalars(*owner)
     raw, g0, high, low, high3, low3 = own_piece(anomalies, own, blocks)
@@ -389,9 +392,10 @@
 
     part = pick(stacked, c) + shifted(pick(stacked, 1 - c), "c", 1)
     arrived = [shifted(pick(part, (x + shift) % 4), "x", shift) for shift in (1, 3, 2)]
-    part = pick(part, x) + arrived[0] + arrived[1] + arrived[2]
+    near = lax.optimization_barrier(pick(part, x) + arrived[0] + arrived[1])
+    part = near + arrived[2]
     part = part + lax.ppermute(part, "z", [(i, i ^ 1) for i in range(8)])
-    z1, z3, z2 = (shifted(part, "z", shift) for shift in (2, 6, 4))
+    z2, z1, z3 = (shifted(part, "z", shift) for shift in (4, 2, 6))
     part = (part + z2) + (z1 + z3)
     e1, e3, e2 = (shifted(part, "x", shift) for shift in (1, 3, 2))
     mine = jnp.stack([piece[:K] for piece in (part, e1, e2, e3)])

time: 92.9 us -> 91.9 us (0.989)
  waiting for transfers between devices: 25.7 us -> 20.3 us
  starting transfers between devices: 40 us -> 44.2 us
    ppermute x20 -> x21, waiting for transfers between devices: 23.9 us -> 18.5 us  [shifted(): return lax.ppermute(value, axis, [(i, (i + shift) % n) for i in range(n)])]
    ppermute x20 -> x21, starting transfers between devices: 38.2 us -> 42.4 us  [shifted(): return lax.ppermute(value, axis, [(i, (i + shift) % n) for i in range(n)])]
  transfers between devices with their start and end apart: 21 -> 22, of which waited for: 13 -> 13; matrix products, arithmetic and copies ran while one was open for 0% -> 0% of each run, Pallas kernels for 17% -> 19%
where the time goes in v5:
time: 91.9 us; the launch traced here: 91.7 us
  starting transfers between devices  44.2 us (48%)
  Pallas kernels  25.7 us (28%)
  waiting for transfers between devices  20.3 us (22%)
    ppermute x21, starting transfers between devices, shifted(): return lax.ppermute(value, axis, [(i, (i + shift) % n) for i in range(n)])  42.4 us
    ppermute x21, waiting for transfers between devices, shifted(): return lax.ppermute(value, axis, [(i, (i + shift) % n) for i in range(n)])  18.5 us
    pallas_call x3, Pallas kernels, sketch_pieces(): pl.pallas_call(functools.partial(sketch_kernel, count), in_specs=[smem()]...  8.45 us
    pallas_call x1, Pallas kernels, own_piece(): pl.pallas_call(own_kernel, in_specs=[smem(), pl.BlockSpec(memory_space=pl...  4.36 us
    pallas_call x1, Pallas kernels, time_basis_of(): pl.pallas_call(time_kernel, in_specs=[vmem()] * 5, out_specs=vmem(), out_...  4.08 us
    pallas_call x1, Pallas kernels, factor(): pl.pallas_call(factor_kernel, in_specs=[smem(), vmem()], out_specs=vmem()...  2.92 us
    pallas_call x1, Pallas kernels, space(): pl.pallas_call(space_kernel, in_specs=[smem()] + [vmem()] * 6, out_specs=...  2.54 us
  transfers between devices with their start and end apart: 22, of which 13 were waited for; matrix products, arithmetic and copies ran while one was open for 0% of the time, Pallas kernels for 19%

profile of v5, /device:TPU:1, one launch (start us, length us, event | category | flops | bytes accessed | tf_op | source)
XLA Modules:
  0.0 91.7 jit_solution(5912752955226345528)
XLA Ops:
  0.6 2.4 %sketch_pieces.5 = f32[512,128]{1,0:T(8,128)S(1)} custom-call(s32[1]{0:T(128)} %bitcast.2.where_ref, f32[2048,1024]{1,0:T(8,128)} %a_ref.7, f32[1024,128]{1,0:T(8,128)} %b_ref.5), custom_call_target="tpu_custom_call" | custom-call | flops 402653184 | bytes 2621440 | tf_op jit(solution)/shard_map/sketch_pieces/pallas_call | solution.py:106
  3.0 2.2 %collective-permute-start = (f32[256,128]{1,0:T(8,128)S(1)}, f32[256,128]{1,0:T(8,128)S(1)}, u32[]{:S(2)}, u32[]{:S(2)}) collective-permute-start(f32[256,128]{1,0:T(8,128)S(1)} %get-tuple-element.37), channel_id=1, source_target_pairs={{0,1},{1,2},{2,3},{3,0},{4,5},{5,6},{6,7},{7,4},{8,9},{9,10},{10,1... | collective-permute-start | bytes 393224 | tf_op jit(solution)/shard_map/ppermute | solution.py:365
  5.2 1.5 %collective-permute-start.2 = (f32[256,128]{1,0:T(8,128)S(1)}, f32[256,128]{1,0:T(8,128)S(1)}, u32[]{:S(2)}, u32[]{:S(2)}) collective-permute-start(f32[256,128]{1,0:T(8,128)S(1)} %get-tuple-element.38), channel_id=1, source_target_pairs={{0,3},{1,0},{2,1},{3,2},{4,7},{5,4},{6,5},{7,6},{8,11},{9,8},{10,9... | collective-permute-start | bytes 393224 | tf_op jit(solution)/shard_map/ppermute | solution.py:365
  6.9 3.7 %sketch_pieces.4 = (f32[512,128]{1,0:T(8,128)S(1)}, f32[512,128]{1,0:T(8,128)S(1)}) custom-call(s32[2]{0:T(128)S(1)} %pad_add_fusion.1.where_ref, f32[2048,1024]{1,0:T(8,128)} %a_ref.7, f32[1024,128]{1,0:T(8,128)} %b_ref.5), custom_call_target="tpu_custom_call" | custom-call | flops 805306368 | bytes 4718592 | tf_op jit(solution)/shard_map/sketch_pieces/pallas_call | solution.py:106
  10.8 2.7 %collective-permute-start.3 = (f32[512,128]{1,0:T(8,128)S(1)}, f32[512,128]{1,0:T(8,128)S(1)}, u32[]{:S(2)}, u32[]{:S(2)}) collective-permute-start(f32[512,128]{1,0:T(8,128)S(1)} %pad_maximum_fusion.1), channel_id=1, source_target_pairs={{0,3},{1,0},{2,1},{3,2},{4,7},{5,4},{6,5},{7,6},{8,11},{9,8},{10,9... | collective-permute-start | bytes 786440 | tf_op jit(solution)/shard_map/ppermute | solution.py:365
  13.5 2.4 %sketch_pieces.3 = f32[512,128]{1,0:T(8,128)S(1)} custom-call(s32[1]{0:T(128)} %bitcast.where_ref, f32[2048,1024]{1,0:T(8,128)} %a_ref.7, f32[1024,128]{1,0:T(8,128)} %b_ref.5), custom_call_target="tpu_custom_call" | custom-call | flops 402653184 | bytes 2621440 | tf_op jit(solution)/shard_map/sketch_pieces/pallas_call | solution.py:106
  15.9 1.3 %collective-permute-done.1 = f32[512,128]{1,0:T(8,128)S(1)} collective-permute-done((f32[512,128]{1,0:T(8,128)S(1)}, f32[512,128]{1,0:T(8,128)S(1)}, u32[]{:S(2)}, u32[]{:S(2)}) %collective-permute-start.1) | collective-permute-done | bytes 262176 | tf_op jit(solution)/shard_map/ppermute | solution.py:365
  17.7 3.5 %collective-permute-start.6 = (f32[512,128]{1,0:T(8,128)S(1)}, f32[512,128]{1,0:T(8,128)S(1)}, u32[]{:S(2)}, u32[]{:S(2)}) collective-permute-start(f32[512,128]{1,0:T(8,128)S(1)} %add_add_fusion.s_ref.refs_0_), channel_id=1, source_target_pairs={{0,2},{1,3},{2,0},{3,1},{4,6},{5,7},{6,4},{7,5},{8,10},{9,11},{10,... | collective-permute-start | bytes 786440 | tf_op jit(solution)/shard_map/ppermute | solution.py:365
  21.4 4.4 %own_piece.1 = (f32[128,1024]{1,0:T(8,128)S(1)}, f32[128,128]{1,0:T(8,128)S(1)}, bf16[1024,1024]{1,0:T(8,128)(2,1)S(1)}, bf16[1024,1024]{1,0:T(8,128)(2,1)S(1)},...) custom-call(s32[4]{0:T(128)S(1)} %pad_add_fusion.where_ref, f32[2048,1024]{1,0:T(8,128)} %a_ref.7, ...), custom_call_target="tpu_custom_call" | custom-call | flops 402653184 | bytes 9437184 | tf_op jit(solution)/shard_map/own_piece/pallas_call | solution.py:157
  25.7 2.9 %collective-permute-done.6.s2_ref.refs_2_ = f32[512,128]{1,0:T(8,128)S(1)} collective-permute-done((f32[512,128]{1,0:T(8,128)S(1)}, f32[512,128]{1,0:T(8,128)S(1)}, u32[]{:S(2)}, u32[]{:S(2)}) %collective-permute-start.6) | collective-permute-done | bytes 262176 | tf_op jit(solution)/shard_map/ppermute | solution.py:365
  28.7 1.3 %two_pieces.1 = (f32[128,1024]{1,0:T(8,128)S(1)}, f32[128,128]{1,0:T(8,128)S(1)}, f32[128,128]{1,0:T(8,128)S(1)}) custom-call(bf16[1024,1024]{1,0:T(8,128)(2,1)S(1)} %get-tuple-element.21.high_ref, bf16[1024,1024]{1,0:T(8,128)(2,1)S(1)} %get-tuple-element.22.low_ref, f32[512,128]{1,0:T(8,128)S(1)} %collective-permute-done.5.s1_ref.refs_1_, ...), custom_call_target="tpu_custom_call" | custom-call | flops 805306368 | bytes 5242880 | tf_op jit(solution)/shard_map/two_pieces/pallas_call | solution.py:185
  30.8 5.6 %collective-permute-start.7 = (f32[4,160,128]{2,1,0:T(8,128)S(1)}, f32[4,160,128]{2,1,0:T(8,128)S(1)}, u32[]{:S(2)}, u32[]{:S(2)}) collective-permute-start(f32[4,160,128]{2,1,0:T(8,128)S(1)} %dynamic-slice_bitcast_fusion), channel_id=1, source_target_pairs={{0,4},{4,0},{1,5},{5,1},{2,6},{6,2},{3,7},{7,3},{8,12},{12,8},{9,1... | collective-permute-start | bytes 983048 | tf_op jit(solution)/shard_map/ppermute | solution.py:365
  36.3 1.3 %collective-permute-done.7 = f32[4,160,128]{2,1,0:T(8,128)S(1)} collective-permute-done((f32[4,160,128]{2,1,0:T(8,128)S(1)}, f32[4,160,128]{2,1,0:T(8,128)S(1)}, u32[]{:S(2)}, u32[]{:S(2)}) %collective-permute-start.7) | collective-permute-done | bytes 327712 | tf_op jit(solution)/shard_map/ppermute | solution.py:365
  37.7 2.5 %collective-permute-start.8 = (f32[160,128]{1,0:T(8,128)S(1)}, f32[160,128]{1,0:T(8,128)S(1)}, u32[]{:S(2)}, u32[]{:S(2)}) collective-permute-start(f32[160,128]{1,0:T(8,128)S(1)} %get-tuple-element.34), channel_id=1, source_target_pairs={{0,64},{64,128},{128,192},{192,0},{1,65},{65,129},{129,193},{193,1... | collective-permute-start | bytes 245768 | tf_op jit(solution)/shard_map/ppermute | solution.py:365
  40.2 1.3 %collective-permute-start.9 = (f32[160,128]{1,0:T(8,128)S(1)}, f32[160,128]{1,0:T(8,128)S(1)}, u32[]{:S(2)}, u32[]{:S(2)}) collective-permute-start(f32[160,128]{1,0:T(8,128)S(1)} %get-tuple-element.33), channel_id=1, source_target_pairs={{0,192},{64,0},{128,64},{192,128},{1,193},{65,1},{129,65},{193,129... | collective-permute-start | bytes 245768 | tf_op jit(solution)/shard_map/ppermute | solution.py:365
  41.5 1.6 %collective-permute-start.10 = (f32[160,128]{1,0:T(8,128)S(1)}, f32[160,128]{1,0:T(8,128)S(1)}, u32[]{:S(2)}, u32[]{:S(2)}) collective-permute-start(f32[160,128]{1,0:T(8,128)S(1)} %get-tuple-element.32), channel_id=1, source_target_pairs={{0,128},{64,192},{128,0},{192,64},{1,129},{65,193},{129,1},{193,65... | collective-permute-start | bytes 245768 | tf_op jit(solution)/shard_map/ppermute | solution.py:365
  44.0 2.3 %collective-permute-done.10 = f32[160,128]{1,0:T(8,128)S(1)} collective-permute-done((f32[160,128]{1,0:T(8,128)S(1)}, f32[160,128]{1,0:T(8,128)S(1)}, u32[]{:S(2)}, u32[]{:S(2)}) %collective-permute-start.10) | collective-permute-done | bytes 81952 | tf_op jit(solution)/shard_map/ppermute | solution.py:365
  46.3 1.8 %collective-permute-start.11 = (f32[160,128]{1,0:T(8,128)S(1)}, f32[160,128]{1,0:T(8,128)S(1)}, u32[]{:S(2)}, u32[]{:S(2)}) collective-permute-start(f32[160,128]{1,0:T(8,128)S(1)} %add.125), channel_id=1, source_target_pairs={{0,8},{8,0},{16,24},{24,16},{32,40},{40,32},{48,56},{56,48},{1,9},... | collective-permute-start | bytes 245768 | tf_op jit(solution)/shard_map/ppermute | solution.py:397
  48.1 1.8 %collective-permute-done.11 = f32[160,128]{1,0:T(8,128)S(1)} collective-permute-done((f32[160,128]{1,0:T(8,128)S(1)}, f32[160,128]{1,0:T(8,128)S(1)}, u32[]{:S(2)}, u32[]{:S(2)}) %collective-permute-start.11) | collective-permute-done | bytes 81952 | tf_op jit(solution)/shard_map/ppermute | solution.py:397
  50.0 6.8 %collective-permute-start.12 = (f32[160,128]{1,0:T(8,128)S(1)}, f32[160,128]{1,0:T(8,128)S(1)}, u32[]{:S(2)}, u32[]{:S(2)}) collective-permute-start(f32[160,128]{1,0:T(8,128)S(1)} %add.126), channel_id=1, source_target_pairs={{0,32},{8,40},{16,48},{24,56},{32,0},{40,8},{48,16},{56,24},{1,33}... | collective-permute-start | bytes 245768 | tf_op jit(solution)/shard_map/ppermute | solution.py:365
  56.8 1.2 %collective-permute-start.13 = (f32[160,128]{1,0:T(8,128)S(1)}, f32[160,128]{1,0:T(8,128)S(1)}, u32[]{:S(2)}, u32[]{:S(2)}) collective-permute-start(f32[160,128]{1,0:T(8,128)S(1)} %add.126), channel_id=1, source_target_pairs={{0,16},{8,24},{16,32},{24,40},{32,48},{40,56},{48,0},{56,8},{1,17}... | collective-permute-start | bytes 245768 | tf_op jit(solution)/shard_map/ppermute | solution.py:365
  58.0 2.4 %collective-permute-start.14 = (f32[160,128]{1,0:T(8,128)S(1)}, f32[160,128]{1,0:T(8,128)S(1)}, u32[]{:S(2)}, u32[]{:S(2)}) collective-permute-start(f32[160,128]{1,0:T(8,128)S(1)} %add.126), channel_id=1, source_target_pairs={{0,48},{8,56},{16,0},{24,8},{32,16},{40,24},{48,32},{56,40},{1,49}... | collective-permute-start | bytes 245768 | tf_op jit(solution)/shard_map/ppermute | solution.py:365
  60.5 3.6 %collective-permute-done.13 = f32[160,128]{1,0:T(8,128)S(1)} collective-permute-done((f32[160,128]{1,0:T(8,128)S(1)}, f32[160,128]{1,0:T(8,128)S(1)}, u32[]{:S(2)}, u32[]{:S(2)}) %collective-permute-start.13) | collective-permute-done | bytes 81952 | tf_op jit(solution)/shard_map/ppermute | solution.py:365
  64.6 1.3 %collective-permute-start.17 = (f32[160,128]{1,0:T(8,128)S(1)}, f32[160,128]{1,0:T(8,128)S(1)}, u32[]{:S(2)}, u32[]{:S(2)}) collective-permute-start(f32[160,128]{1,0:T(8,128)S(1)} %add_add_fusion.1), channel_id=1, source_target_pairs={{0,192},{64,0},{128,64},{192,128},{1,193},{65,1},{129,65},{193,129... | collective-permute-start | bytes 245768 | tf_op jit(solution)/shard_map/ppermute | solution.py:365
  65.8 1.5 %collective-permute-start.16 = (f32[160,128]{1,0:T(8,128)S(1)}, f32[160,128]{1,0:T(8,128)S(1)}, u32[]{:S(2)}, u32[]{:S(2)}) collective-permute-start(f32[160,128]{1,0:T(8,128)S(1)} %add_add_fusion.1), channel_id=1, source_target_pairs={{0,128},{64,192},{128,0},{192,64},{1,129},{65,193},{129,1},{193,65... | collective-permute-start | bytes 245768 | tf_op jit(solution)/shard_map/ppermute | solution.py:365
  67.9 2.7 %collective-permute-done.16 = f32[160,128]{1,0:T(8,128)S(1)} collective-permute-done((f32[160,128]{1,0:T(8,128)S(1)}, f32[160,128]{1,0:T(8,128)S(1)}, u32[]{:S(2)}, u32[]{:S(2)}) %collective-permute-start.16) | collective-permute-done | bytes 81952 | tf_op jit(solution)/shard_map/ppermute | solution.py:365
  71.8 4.8 %collective-permute-start.18 = (f32[4,128,128]{2,1,0:T(8,128)S(1)}, f32[4,128,128]{2,1,0:T(8,128)S(1)}, u32[]{:S(2)}, u32[]{:S(2)}) collective-permute-start(f32[4,128,128]{2,1,0:T(8,128)S(1)} %pad_maximum_fusion.2.mine_ref), channel_id=1, source_target_pairs={{0,4},{4,0},{1,5},{5,1},{2,6},{6,2},{3,7},{7,3},{8,12},{12,8},{9,1... | collective-permute-start | bytes 786440 | tf_op jit(solution)/shard_map/ppermute | solution.py:365
  76.7 2.9 %factor.1.inv_ref = f32[128,128]{1,0:T(8,128)S(1)} custom-call(s32[1]{0:T(128)} %bitcast.4.where_ref, f32[4,32,128]{2,1,0:T(8,128)S(1)} %pad_maximum_fusion.3.quarters_ref), custom_call_target="tpu_custom_call" | custom-call | flops 402653184 | bytes 131072 | tf_op jit(solution)/shard_map/factor/pallas_call | solution.py:272
  79.7 1.4 %back.1 = (f32[128,1024]{1,0:T(8,128)S(1)}, f32[128,128]{1,0:T(8,128)S(1)}) custom-call(s32[2]{0:T(128)S(1)} %pad_add_fusion.2.where_ref, f32[128,128]{1,0:T(8,128)S(1)} %factor.1.inv_ref, f32[4,128,128]{2,1,0:T(8,128)S(1)} %pad_maximum_fusion.2.mine_ref, f32[4,128,128]{2,1,0:T(8,128)S(1)} %collective-permute-done.18.other_ref), custom_call_target="tpu_custom_call" | custom-call | flops 402653184 | bytes 1048576 | tf_op jit(solution)/shard_map/back/pallas_call | solution.py:306
  81.1 1.9 %collective-permute-start.20 = (f32[128,128]{1,0:T(8,128)S(1)}, f32[128,128]{1,0:T(8,128)S(1)}, u32[]{:S(2)}, u32[]{:S(2)}) collective-permute-start(f32[128,128]{1,0:T(8,128)S(1)} %get-tuple-element.31.g0_ref), channel_id=1, source_target_pairs={{0,2},{1,3},{2,0},{3,1},{4,6},{5,7},{6,4},{7,5},{8,10},{9,11},{10,... | collective-permute-start | bytes 196616 | tf_op jit(solution)/shard_map/ppermute | solution.py:365
  83.8 2.5 %space.1 = (f32[2048,128]{1,0:T(8,128)}, bf16[1024,384]{1,0:T(8,128)(2,1)S(1)}) custom-call(s32[4]{0:T(128)S(1)} %pad_add_fusion.where_ref, f32[128,128]{1,0:T(8,128)S(1)} %factor.1.inv_ref, f32[128,1024]{1,0:T(8,128)S(1)} %get-tuple-element.28.back_t_ref, f32[512,128]{1,0:T(8,128)S(1)} %add_add_fusion.s_ref.refs_0_, ...), custom_call_target="tpu_custom_call" | custom-call | flops 402653184 | bytes 3145728 | tf_op jit(solution)/shard_map/space/pallas_call | solution.py:332
  87.6 4.1 %time_basis.1 = f32[1024,128]{1,0:T(8,128)} custom-call(bf16[1024,384]{1,0:T(8,128)(2,1)S(1)} %get-tuple-element.30.back_ref, f32[128,128]{1,0:T(8,128)S(1)} %get-tuple-element.31.g0_ref, f32[128,128]{1,0:T(8,128)S(1)} %collective-permute-done.19.g1_ref, f32[128,128]{1,0:T(8,128)S(1)} %collective-permute-done.20.g2_ref, ...), custom_call_target="tpu_custom_call" | custom-call | flops 201326592 | bytes 1048576 | tf_op jit(solution)/shard_map/time_basis/pallas_call | solution.py:351
  (47 shorter events, 7.2 us)
Async XLA Ops:
  3.0 7.5 %collective-permute-start = (f32[256,128]{1,0:T(8,128)S(1)}, f32[256,128]{1,0:T(8,128)S(1)}, u32[]{:S(2)}, u32[]{:S(2)}) collective-permute-start(f32[256,128]{1,0:T(8,128)S(1)} %get-tuple-element.37), channel_id=1, source_target_pairs={{0,1},{1,2},{2,3},{3,0},{4,5},{5,6},{6,7},{7,4},{8,9},{9,10},{10,1... | collective-permute-start | bytes 393224 | tf_op jit(solution)/shard_map/ppermute | solution.py:365
  5.2 5.3 %collective-permute-start.2 = (f32[256,128]{1,0:T(8,128)S(1)}, f32[256,128]{1,0:T(8,128)S(1)}, u32[]{:S(2)}, u32[]{:S(2)}) collective-permute-start(f32[256,128]{1,0:T(8,128)S(1)} %get-tuple-element.38), channel_id=1, source_target_pairs={{0,3},{1,0},{2,1},{3,2},{4,7},{5,4},{6,5},{7,6},{8,11},{9,8},{10,9... | collective-permute-start | bytes 393224 | tf_op jit(solution)/shard_map/ppermute | solution.py:365
  10.7 6.5 %collective-permute-start.1 = (f32[512,128]{1,0:T(8,128)S(1)}, f32[512,128]{1,0:T(8,128)S(1)}, u32[]{:S(2)}, u32[]{:S(2)}) collective-permute-start(f32[512,128]{1,0:T(8,128)S(1)} %pad_maximum_fusion), channel_id=1, source_target_pairs={{0,1},{1,2},{2,3},{3,0},{4,5},{5,6},{6,7},{7,4},{8,9},{9,10},{10,1... | collective-permute-start | bytes 786440 | tf_op jit(solution)/shard_map/ppermute | solution.py:365
  10.8 6.4 %collective-permute-start.3 = (f32[512,128]{1,0:T(8,128)S(1)}, f32[512,128]{1,0:T(8,128)S(1)}, u32[]{:S(2)}, u32[]{:S(2)}) collective-permute-start(f32[512,128]{1,0:T(8,128)S(1)} %pad_maximum_fusion.1), channel_id=1, source_target_pairs={{0,3},{1,0},{2,1},{3,2},{4,7},{5,4},{6,5},{7,6},{8,11},{9,8},{10,9... | collective-permute-start | bytes 786440 | tf_op jit(solution)/shard_map/ppermute | solution.py:365
  17.3 8.5 %collective-permute-start.5 = (f32[512,128]{1,0:T(8,128)S(1)}, f32[512,128]{1,0:T(8,128)S(1)}, u32[]{:S(2)}, u32[]{:S(2)}) collective-permute-start(f32[512,128]{1,0:T(8,128)S(1)} %add_add_fusion.s_ref.refs_0_), channel_id=1, source_target_pairs={{0,1},{1,2},{2,3},{3,0},{4,5},{5,6},{6,7},{7,4},{8,9},{9,10},{10,1... | collective-permute-start | bytes 786440 | tf_op jit(solution)/shard_map/ppermute | solution.py:365
  17.7 10.9 %collective-permute-start.6 = (f32[512,128]{1,0:T(8,128)S(1)}, f32[512,128]{1,0:T(8,128)S(1)}, u32[]{:S(2)}, u32[]{:S(2)}) collective-permute-start(f32[512,128]{1,0:T(8,128)S(1)} %add_add_fusion.s_ref.refs_0_), channel_id=1, source_target_pairs={{0,2},{1,3},{2,0},{3,1},{4,6},{5,7},{6,4},{7,5},{8,10},{9,11},{10,... | collective-permute-start | bytes 786440 | tf_op jit(solution)/shard_map/ppermute | solution.py:365
  21.3 8.7 %collective-permute-start.4 = (f32[512,128]{1,0:T(8,128)S(1)}, f32[512,128]{1,0:T(8,128)S(1)}, u32[]{:S(2)}, u32[]{:S(2)}) collective-permute-start(f32[512,128]{1,0:T(8,128)S(1)} %add_add_fusion.s_ref.refs_0_), channel_id=1, source_target_pairs={{0,3},{1,0},{2,1},{3,2},{4,7},{5,4},{6,5},{7,6},{8,11},{9,8},{10,9... | collective-permute-start | bytes 786440 | tf_op jit(solution)/shard_map/ppermute | solution.py:365
  30.8 6.8 %collective-permute-start.7 = (f32[4,160,128]{2,1,0:T(8,128)S(1)}, f32[4,160,128]{2,1,0:T(8,128)S(1)}, u32[]{:S(2)}, u32[]{:S(2)}) collective-permute-start(f32[4,160,128]{2,1,0:T(8,128)S(1)} %dynamic-slice_bitcast_fusion), channel_id=1, source_target_pairs={{0,4},{4,0},{1,5},{5,1},{2,6},{6,2},{3,7},{7,3},{8,12},{12,8},{9,1... | collective-permute-start | bytes 983048 | tf_op jit(solution)/shard_map/ppermute | solution.py:365
  37.7 6.3 %collective-permute-start.8 = (f32[160,128]{1,0:T(8,128)S(1)}, f32[160,128]{1,0:T(8,128)S(1)}, u32[]{:S(2)}, u32[]{:S(2)}) collective-permute-start(f32[160,128]{1,0:T(8,128)S(1)} %get-tuple-element.34), channel_id=1, source_target_pairs={{0,64},{64,128},{128,192},{192,0},{1,65},{65,129},{129,193},{193,1... | collective-permute-start | bytes 245768 | tf_op jit(solution)/shard_map/ppermute | solution.py:365
  40.2 3.8 %collective-permute-start.9 = (f32[160,128]{1,0:T(8,128)S(1)}, f32[160,128]{1,0:T(8,128)S(1)}, u32[]{:S(2)}, u32[]{:S(2)}) collective-permute-start(f32[160,128]{1,0:T(8,128)S(1)} %get-tuple-element.33), channel_id=1, source_target_pairs={{0,192},{64,0},{128,64},{192,128},{1,193},{65,1},{129,65},{193,129... | collective-permute-start | bytes 245768 | tf_op jit(solution)/shard_map/ppermute | solution.py:365
  41.5 4.8 %collective-permute-start.10 = (f32[160,128]{1,0:T(8,128)S(1)}, f32[160,128]{1,0:T(8,128)S(1)}, u32[]{:S(2)}, u32[]{:S(2)}) collective-permute-start(f32[160,128]{1,0:T(8,128)S(1)} %get-tuple-element.32), channel_id=1, source_target_pairs={{0,128},{64,192},{128,0},{192,64},{1,129},{65,193},{129,1},{193,65... | collective-permute-start | bytes 245768 | tf_op jit(solution)/shard_map/ppermute | solution.py:365
  46.3 3.7 %collective-permute-start.11 = (f32[160,128]{1,0:T(8,128)S(1)}, f32[160,128]{1,0:T(8,128)S(1)}, u32[]{:S(2)}, u32[]{:S(2)}) collective-permute-start(f32[160,128]{1,0:T(8,128)S(1)} %add.125), channel_id=1, source_target_pairs={{0,8},{8,0},{16,24},{24,16},{32,40},{40,32},{48,56},{56,48},{1,9},... | collective-permute-start | bytes 245768 | tf_op jit(solution)/shard_map/ppermute | solution.py:397
  50.0 10.5 %collective-permute-start.12 = (f32[160,128]{1,0:T(8,128)S(1)}, f32[160,128]{1,0:T(8,128)S(1)}, u32[]{:S(2)}, u32[]{:S(2)}) collective-permute-start(f32[160,128]{1,0:T(8,128)S(1)} %add.126), channel_id=1, source_target_pairs={{0,32},{8,40},{16,48},{24,56},{32,0},{40,8},{48,16},{56,24},{1,33}... | collective-permute-start | bytes 245768 | tf_op jit(solution)/shard_map/ppermute | solution.py:365
  56.8 7.3 %collective-permute-start.13 = (f32[160,128]{1,0:T(8,128)S(1)}, f32[160,128]{1,0:T(8,128)S(1)}, u32[]{:S(2)}, u32[]{:S(2)}) collective-permute-start(f32[160,128]{1,0:T(8,128)S(1)} %add.126), channel_id=1, source_target_pairs={{0,16},{8,24},{16,32},{24,40},{32,48},{40,56},{48,0},{56,8},{1,17}... | collective-permute-start | bytes 245768 | tf_op jit(solution)/shard_map/ppermute | solution.py:365
  58.0 6.5 %collective-permute-start.14 = (f32[160,128]{1,0:T(8,128)S(1)}, f32[160,128]{1,0:T(8,128)S(1)}, u32[]{:S(2)}, u32[]{:S(2)}) collective-permute-start(f32[160,128]{1,0:T(8,128)S(1)} %add.126), channel_id=1, source_target_pairs={{0,48},{8,56},{16,0},{24,8},{32,16},{40,24},{48,32},{56,40},{1,49}... | collective-permute-start | bytes 245768 | tf_op jit(solution)/shard_map/ppermute | solution.py:365
  64.6 3.4 %collective-permute-start.17 = (f32[160,128]{1,0:T(8,128)S(1)}, f32[160,128]{1,0:T(8,128)S(1)}, u32[]{:S(2)}, u32[]{:S(2)}) collective-permute-start(f32[160,128]{1,0:T(8,128)S(1)} %add_add_fusion.1), channel_id=1, source_target_pairs={{0,192},{64,0},{128,64},{192,128},{1,193},{65,1},{129,65},{193,129... | collective-permute-start | bytes 245768 | tf_op jit(solution)/shard_map/ppermute | solution.py:365
  65.8 4.8 %collective-permute-start.16 = (f32[160,128]{1,0:T(8,128)S(1)}, f32[160,128]{1,0:T(8,128)S(1)}, u32[]{:S(2)}, u32[]{:S(2)}) collective-permute-start(f32[160,128]{1,0:T(8,128)S(1)} %add_add_fusion.1), channel_id=1, source_target_pairs={{0,128},{64,192},{128,0},{192,64},{1,129},{65,193},{129,1},{193,65... | collective-permute-start | bytes 245768 | tf_op jit(solution)/shard_map/ppermute | solution.py:365
  67.3 4.5 %collective-permute-start.15 = (f32[160,128]{1,0:T(8,128)S(1)}, f32[160,128]{1,0:T(8,128)S(1)}, u32[]{:S(2)}, u32[]{:S(2)}) collective-permute-start(f32[160,128]{1,0:T(8,128)S(1)} %add_add_fusion.1), channel_id=1, source_target_pairs={{0,64},{64,128},{128,192},{192,0},{1,65},{65,129},{129,193},{193,1... | collective-permute-start | bytes 245768 | tf_op jit(solution)/shard_map/ppermute | solution.py:365
  71.8 7.8 %collective-permute-start.18 = (f32[4,128,128]{2,1,0:T(8,128)S(1)}, f32[4,128,128]{2,1,0:T(8,128)S(1)}, u32[]{:S(2)}, u32[]{:S(2)}) collective-permute-start(f32[4,128,128]{2,1,0:T(8,128)S(1)} %pad_maximum_fusion.2.mine_ref), channel_id=1, source_target_pairs={{0,4},{4,0},{1,5},{5,1},{2,6},{6,2},{3,7},{7,3},{8,12},{12,8},{9,1... | collective-permute-start | bytes 786440 | tf_op jit(solution)/shard_map/ppermute | solution.py:365
  81.0 6.4 %collective-permute-start.19 = (f32[128,128]{1,0:T(8,128)S(1)}, f32[128,128]{1,0:T(8,128)S(1)}, u32[]{:S(2)}, u32[]{:S(2)}) collective-permute-start(f32[128,128]{1,0:T(8,128)S(1)} %get-tuple-element.31.g0_ref), channel_id=1, source_target_pairs={{0,1},{1,2},{2,3},{3,0},{4,5},{5,6},{6,7},{7,4},{8,9},{9,10},{10,1... | collective-permute-start | bytes 196616 | tf_op jit(solution)/shard_map/ppermute | solution.py:365
  81.1 6.3 %collective-permute-start.20 = (f32[128,128]{1,0:T(8,128)S(1)}, f32[128,128]{1,0:T(8,128)S(1)}, u32[]{:S(2)}, u32[]{:S(2)}) collective-permute-start(f32[128,128]{1,0:T(8,128)S(1)} %get-tuple-element.31.g0_ref), channel_id=1, source_target_pairs={{0,2},{1,3},{2,0},{3,1},{4,6},{5,7},{6,4},{7,5},{8,10},{9,11},{10,... | collective-permute-start | bytes 196616 | tf_op jit(solution)/shard_map/ppermute | solution.py:365
  83.0 4.7 %collective-permute-start.21 = (f32[128,128]{1,0:T(8,128)S(1)}, f32[128,128]{1,0:T(8,128)S(1)}, u32[]{:S(2)}, u32[]{:S(2)}) collective-permute-start(f32[128,128]{1,0:T(8,128)S(1)} %get-tuple-element.31.g0_ref), channel_id=1, source_target_pairs={{0,3},{1,0},{2,1},{3,2},{4,7},{5,4},{6,5},{7,6},{8,11},{9,8},{10,9... | collective-permute-start | bytes 196616 | tf_op jit(solution)/shard_map/ppermute | solution.py:365

commit v6 on v5

--- a/solution.py
+++ b/solution.py
@@ -340,20 +340,34 @@
     )(where, inv, back_t, *pieces)
 
 
-def time_kernel(back_ref, g0_ref, g1_ref, g2_ref, g3_ref, o_ref, w_ref, inv_ref):
+def time_kernel(back_ref, g0_ref, g1_ref, g2_ref, g3_ref, o_ref, w_ref, inv_ref, buf_ref, sems):
     w_ref[...] = (g0_ref[...] + g2_ref[...]) + (g1_ref[...] + g3_ref[...])
     inverse_factor(w_ref, inv_ref)
     high, low = halves(inv_ref[...])
-    o_ref[...] = dot(back_ref[...], jnp.concatenate([high, low, high], 1), NT)
+    right = jnp.concatenate([high, low, high], 1)
+    step = buf_ref.shape[0] // 4
+    copies = []
+    for i in range(4):
+        at = pl.ds(i * step, step)
+        buf_ref[at, :] = dot(back_ref[at, :], right, NT)
+        copies.append(pltpu.make_async_copy(buf_ref.at[at, :], o_ref.at[at, :], sems.at[i]))
+        copies[i].start()
+    for copy in copies:
+        copy.wait()
 
 
 def time_basis_of(back, grams):
     return pl.pallas_call(
         time_kernel,
         in_specs=[vmem()] * 5,
-        out_specs=vmem(),
+        out_specs=pl.BlockSpec(memory_space=pltpu.HBM),
         out_shape=jax.ShapeDtypeStruct((back.shape[0], K), F32),
-        scratch_shapes=[pltpu.VMEM((K, K), F32)] * 2,
+        scratch_shapes=[
+            pltpu.VMEM((K, K), F32),
+            pltpu.VMEM((K, K), F32),
+            pltpu.VMEM((back.shape[0], K), F32),
+            pltpu.SemaphoreType.DMA((4,)),
+        ],
         compiler_params=params(),
         cost_estimate=cost(12 * back.shape[0] * K * K, 8 * back.shape[0] * K),
         name="time_basis",

time: 91.9 us -> 91.9 us (level)
  no operation moved by 1% of the time
where the time goes in v6:
time: 91.9 us; the launch traced here: 91.8 us
  starting transfers between devices  44.2 us (48%)
  Pallas kernels  25.6 us (28%)
  waiting for transfers between devices  20.3 us (22%)
  between operations  1.03 us (1%)
    ppermute x21, starting transfers between devices, shifted(): return lax.ppermute(value, axis, [(i, (i + shift) % n) for i in range(n)])  42.4 us
    ppermute x21, waiting for transfers between devices, shifted(): return lax.ppermute(value, axis, [(i, (i + shift) % n) for i in range(n)])  18.5 us
    pallas_call x3, Pallas kernels, sketch_pieces(): pl.pallas_call(functools.partial(sketch_kernel, count), in_specs=[smem()]...  8.45 us
    pallas_call x1, Pallas kernels, own_piece(): pl.pallas_call(own_kernel, in_specs=[smem(), pl.BlockSpec(memory_space=pl...  4.36 us
    pallas_call x1, Pallas kernels, time_basis_of(): pl.pallas_call(time_kernel, in_specs=[vmem()] * 5, out_specs=pl.BlockSpec...  3.96 us
    pallas_call x1, Pallas kernels, factor(): pl.pallas_call(factor_kernel, in_specs=[smem(), vmem()], out_specs=vmem()...  2.92 us
    pallas_call x1, Pallas kernels, space(): pl.pallas_call(space_kernel, in_specs=[smem()] + [vmem()] * 6, out_specs=...  2.54 us
  transfers between devices with their start and end apart: 22, of which 13 were waited for; matrix products, arithmetic and copies ran while one was open for 0% of the time, Pallas kernels for 19%

profile of v6, /device:TPU:1, one launch (start us, length us, event | category | flops | bytes accessed | tf_op | source)
XLA Modules:
  0.0 91.8 jit_solution(5232549897267325050)
XLA Ops:
  0.6 2.4 %sketch_pieces.5 = f32[512,128]{1,0:T(8,128)S(1)} custom-call(s32[1]{0:T(128)} %bitcast.2.where_ref, f32[2048,1024]{1,0:T(8,128)} %a_ref.7, f32[1024,128]{1,0:T(8,128)} %b_ref.5), custom_call_target="tpu_custom_call" | custom-call | flops 402653184 | bytes 2621440 | tf_op jit(solution)/shard_map/sketch_pieces/pallas_call | solution.py:106
  3.0 2.2 %collective-permute-start = (f32[256,128]{1,0:T(8,128)S(1)}, f32[256,128]{1,0:T(8,128)S(1)}, u32[]{:S(2)}, u32[]{:S(2)}) collective-permute-start(f32[256,128]{1,0:T(8,128)S(1)} %get-tuple-element.37), channel_id=1, source_target_pairs={{0,1},{1,2},{2,3},{3,0},{4,5},{5,6},{6,7},{7,4},{8,9},{9,10},{10,1... | collective-permute-start | bytes 393224 | tf_op jit(solution)/shard_map/ppermute | solution.py:379
  5.2 1.5 %collective-permute-start.2 = (f32[256,128]{1,0:T(8,128)S(1)}, f32[256,128]{1,0:T(8,128)S(1)}, u32[]{:S(2)}, u32[]{:S(2)}) collective-permute-start(f32[256,128]{1,0:T(8,128)S(1)} %get-tuple-element.38), channel_id=1, source_target_pairs={{0,3},{1,0},{2,1},{3,2},{4,7},{5,4},{6,5},{7,6},{8,11},{9,8},{10,9... | collective-permute-start | bytes 393224 | tf_op jit(solution)/shard_map/ppermute | solution.py:379
  6.9 3.7 %sketch_pieces.4 = (f32[512,128]{1,0:T(8,128)S(1)}, f32[512,128]{1,0:T(8,128)S(1)}) custom-call(s32[2]{0:T(128)S(1)} %pad_add_fusion.1.where_ref, f32[2048,1024]{1,0:T(8,128)} %a_ref.7, f32[1024,128]{1,0:T(8,128)} %b_ref.5), custom_call_target="tpu_custom_call" | custom-call | flops 805306368 | bytes 4718592 | tf_op jit(solution)/shard_map/sketch_pieces/pallas_call | solution.py:106
  10.8 2.7 %collective-permute-start.3 = (f32[512,128]{1,0:T(8,128)S(1)}, f32[512,128]{1,0:T(8,128)S(1)}, u32[]{:S(2)}, u32[]{:S(2)}) collective-permute-start(f32[512,128]{1,0:T(8,128)S(1)} %pad_maximum_fusion.1), channel_id=1, source_target_pairs={{0,3},{1,0},{2,1},{3,2},{4,7},{5,4},{6,5},{7,6},{8,11},{9,8},{10,9... | collective-permute-start | bytes 786440 | tf_op jit(solution)/shard_map/ppermute | solution.py:379
  13.5 2.4 %sketch_pieces.3 = f32[512,128]{1,0:T(8,128)S(1)} custom-call(s32[1]{0:T(128)} %bitcast.where_ref, f32[2048,1024]{1,0:T(8,128)} %a_ref.7, f32[1024,128]{1,0:T(8,128)} %b_ref.5), custom_call_target="tpu_custom_call" | custom-call | flops 402653184 | bytes 2621440 | tf_op jit(solution)/shard_map/sketch_pieces/pallas_call | solution.py:106
  15.9 1.3 %collective-permute-done.1 = f32[512,128]{1,0:T(8,128)S(1)} collective-permute-done((f32[512,128]{1,0:T(8,128)S(1)}, f32[512,128]{1,0:T(8,128)S(1)}, u32[]{:S(2)}, u32[]{:S(2)}) %collective-permute-start.1) | collective-permute-done | bytes 262176 | tf_op jit(solution)/shard_map/ppermute | solution.py:379
  17.7 3.5 %collective-permute-start.6 = (f32[512,128]{1,0:T(8,128)S(1)}, f32[512,128]{1,0:T(8,128)S(1)}, u32[]{:S(2)}, u32[]{:S(2)}) collective-permute-start(f32[512,128]{1,0:T(8,128)S(1)} %add_add_fusion.s_ref.refs_0_), channel_id=1, source_target_pairs={{0,2},{1,3},{2,0},{3,1},{4,6},{5,7},{6,4},{7,5},{8,10},{9,11},{10,... | collective-permute-start | bytes 786440 | tf_op jit(solution)/shard_map/ppermute | solution.py:379
  21.4 4.4 %own_piece.1 = (f32[128,1024]{1,0:T(8,128)S(1)}, f32[128,128]{1,0:T(8,128)S(1)}, bf16[1024,1024]{1,0:T(8,128)(2,1)S(1)}, bf16[1024,1024]{1,0:T(8,128)(2,1)S(1)},...) custom-call(s32[4]{0:T(128)S(1)} %pad_add_fusion.where_ref, f32[2048,1024]{1,0:T(8,128)} %a_ref.7, ...), custom_call_target="tpu_custom_call" | custom-call | flops 402653184 | bytes 9437184 | tf_op jit(solution)/shard_map/own_piece/pallas_call | solution.py:157
  25.7 2.9 %collective-permute-done.6.s2_ref.refs_2_ = f32[512,128]{1,0:T(8,128)S(1)} collective-permute-done((f32[512,128]{1,0:T(8,128)S(1)}, f32[512,128]{1,0:T(8,128)S(1)}, u32[]{:S(2)}, u32[]{:S(2)}) %collective-permute-start.6) | collective-permute-done | bytes 262176 | tf_op jit(solution)/shard_map/ppermute | solution.py:379
  28.7 1.3 %two_pieces.1 = (f32[128,1024]{1,0:T(8,128)S(1)}, f32[128,128]{1,0:T(8,128)S(1)}, f32[128,128]{1,0:T(8,128)S(1)}) custom-call(bf16[1024,1024]{1,0:T(8,128)(2,1)S(1)} %get-tuple-element.21.high_ref, bf16[1024,1024]{1,0:T(8,128)(2,1)S(1)} %get-tuple-element.22.low_ref, f32[512,128]{1,0:T(8,128)S(1)} %collective-permute-done.5.s1_ref.refs_1_, ...), custom_call_target="tpu_custom_call" | custom-call | flops 805306368 | bytes 5242880 | tf_op jit(solution)/shard_map/two_pieces/pallas_call | solution.py:185
  30.8 5.6 %collective-permute-start.7 = (f32[4,160,128]{2,1,0:T(8,128)S(1)}, f32[4,160,128]{2,1,0:T(8,128)S(1)}, u32[]{:S(2)}, u32[]{:S(2)}) collective-permute-start(f32[4,160,128]{2,1,0:T(8,128)S(1)} %dynamic-slice_bitcast_fusion), channel_id=1, source_target_pairs={{0,4},{4,0},{1,5},{5,1},{2,6},{6,2},{3,7},{7,3},{8,12},{12,8},{9,1... | collective-permute-start | bytes 983048 | tf_op jit(solution)/shard_map/ppermute | solution.py:379
  36.3 1.3 %collective-permute-done.7 = f32[4,160,128]{2,1,0:T(8,128)S(1)} collective-permute-done((f32[4,160,128]{2,1,0:T(8,128)S(1)}, f32[4,160,128]{2,1,0:T(8,128)S(1)}, u32[]{:S(2)}, u32[]{:S(2)}) %collective-permute-start.7) | collective-permute-done | bytes 327712 | tf_op jit(solution)/shard_map/ppermute | solution.py:379
  37.7 2.5 %collective-permute-start.8 = (f32[160,128]{1,0:T(8,128)S(1)}, f32[160,128]{1,0:T(8,128)S(1)}, u32[]{:S(2)}, u32[]{:S(2)}) collective-permute-start(f32[160,128]{1,0:T(8,128)S(1)} %get-tuple-element.34), channel_id=1, source_target_pairs={{0,64},{64,128},{128,192},{192,0},{1,65},{65,129},{129,193},{193,1... | collective-permute-start | bytes 245768 | tf_op jit(solution)/shard_map/ppermute | solution.py:379
  40.2 1.3 %collective-permute-start.9 = (f32[160,128]{1,0:T(8,128)S(1)}, f32[160,128]{1,0:T(8,128)S(1)}, u32[]{:S(2)}, u32[]{:S(2)}) collective-permute-start(f32[160,128]{1,0:T(8,128)S(1)} %get-tuple-element.33), channel_id=1, source_target_pairs={{0,192},{64,0},{128,64},{192,128},{1,193},{65,1},{129,65},{193,129... | collective-permute-start | bytes 245768 | tf_op jit(solution)/shard_map/ppermute | solution.py:379
  41.5 1.6 %collective-permute-start.10 = (f32[160,128]{1,0:T(8,128)S(1)}, f32[160,128]{1,0:T(8,128)S(1)}, u32[]{:S(2)}, u32[]{:S(2)}) collective-permute-start(f32[160,128]{1,0:T(8,128)S(1)} %get-tuple-element.32), channel_id=1, source_target_pairs={{0,128},{64,192},{128,0},{192,64},{1,129},{65,193},{129,1},{193,65... | collective-permute-start | bytes 245768 | tf_op jit(solution)/shard_map/ppermute | solution.py:379
  44.0 2.3 %collective-permute-done.10 = f32[160,128]{1,0:T(8,128)S(1)} collective-permute-done((f32[160,128]{1,0:T(8,128)S(1)}, f32[160,128]{1,0:T(8,128)S(1)}, u32[]{:S(2)}, u32[]{:S(2)}) %collective-permute-start.10) | collective-permute-done | bytes 81952 | tf_op jit(solution)/shard_map/ppermute | solution.py:379
  46.3 1.8 %collective-permute-start.11 = (f32[160,128]{1,0:T(8,128)S(1)}, f32[160,128]{1,0:T(8,128)S(1)}, u32[]{:S(2)}, u32[]{:S(2)}) collective-permute-start(f32[160,128]{1,0:T(8,128)S(1)} %add.125), channel_id=1, source_target_pairs={{0,8},{8,0},{16,24},{24,16},{32,40},{40,32},{48,56},{56,48},{1,9},... | collective-permute-start | bytes 245768 | tf_op jit(solution)/shard_map/ppermute | solution.py:411
  48.1 1.8 %collective-permute-done.11 = f32[160,128]{1,0:T(8,128)S(1)} collective-permute-done((f32[160,128]{1,0:T(8,128)S(1)}, f32[160,128]{1,0:T(8,128)S(1)}, u32[]{:S(2)}, u32[]{:S(2)}) %collective-permute-start.11) | collective-permute-done | bytes 81952 | tf_op jit(solution)/shard_map/ppermute | solution.py:411
  50.0 6.8 %collective-permute-start.12 = (f32[160,128]{1,0:T(8,128)S(1)}, f32[160,128]{1,0:T(8,128)S(1)}, u32[]{:S(2)}, u32[]{:S(2)}) collective-permute-start(f32[160,128]{1,0:T(8,128)S(1)} %add.126), channel_id=1, source_target_pairs={{0,32},{8,40},{16,48},{24,56},{32,0},{40,8},{48,16},{56,24},{1,33}... | collective-permute-start | bytes 245768 | tf_op jit(solution)/shard_map/ppermute | solution.py:379
  56.8 1.2 %collective-permute-start.13 = (f32[160,128]{1,0:T(8,128)S(1)}, f32[160,128]{1,0:T(8,128)S(1)}, u32[]{:S(2)}, u32[]{:S(2)}) collective-permute-start(f32[160,128]{1,0:T(8,128)S(1)} %add.126), channel_id=1, source_target_pairs={{0,16},{8,24},{16,32},{24,40},{32,48},{40,56},{48,0},{56,8},{1,17}... | collective-permute-start | bytes 245768 | tf_op jit(solution)/shard_map/ppermute | solution.py:379
  58.0 2.4 %collective-permute-start.14 = (f32[160,128]{1,0:T(8,128)S(1)}, f32[160,128]{1,0:T(8,128)S(1)}, u32[]{:S(2)}, u32[]{:S(2)}) collective-permute-start(f32[160,128]{1,0:T(8,128)S(1)} %add.126), channel_id=1, source_target_pairs={{0,48},{8,56},{16,0},{24,8},{32,16},{40,24},{48,32},{56,40},{1,49}... | collective-permute-start | bytes 245768 | tf_op jit(solution)/shard_map/ppermute | solution.py:379
  60.5 3.6 %collective-permute-done.13 = f32[160,128]{1,0:T(8,128)S(1)} collective-permute-done((f32[160,128]{1,0:T(8,128)S(1)}, f32[160,128]{1,0:T(8,128)S(1)}, u32[]{:S(2)}, u32[]{:S(2)}) %collective-permute-start.13) | collective-permute-done | bytes 81952 | tf_op jit(solution)/shard_map/ppermute | solution.py:379
  64.6 1.3 %collective-permute-start.17 = (f32[160,128]{1,0:T(8,128)S(1)}, f32[160,128]{1,0:T(8,128)S(1)}, u32[]{:S(2)}, u32[]{:S(2)}) collective-permute-start(f32[160,128]{1,0:T(8,128)S(1)} %add_add_fusion.1), channel_id=1, source_target_pairs={{0,192},{64,0},{128,64},{192,128},{1,193},{65,1},{129,65},{193,129... | collective-permute-start | bytes 245768 | tf_op jit(solution)/shard_map/ppermute | solution.py:379
  65.8 1.5 %collective-permute-start.16 = (f32[160,128]{1,0:T(8,128)S(1)}, f32[160,128]{1,0:T(8,128)S(1)}, u32[]{:S(2)}, u32[]{:S(2)}) collective-permute-start(f32[160,128]{1,0:T(8,128)S(1)} %add_add_fusion.1), channel_id=1, source_target_pairs={{0,128},{64,192},{128,0},{192,64},{1,129},{65,193},{129,1},{193,65... | collective-permute-start | bytes 245768 | tf_op jit(solution)/shard_map/ppermute | solution.py:379
  67.9 2.7 %collective-permute-done.16 = f32[160,128]{1,0:T(8,128)S(1)} collective-permute-done((f32[160,128]{1,0:T(8,128)S(1)}, f32[160,128]{1,0:T(8,128)S(1)}, u32[]{:S(2)}, u32[]{:S(2)}) %collective-permute-start.16) | collective-permute-done | bytes 81952 | tf_op jit(solution)/shard_map/ppermute | solution.py:379
  71.8 4.8 %collective-permute-start.18 = (f32[4,128,128]{2,1,0:T(8,128)S(1)}, f32[4,128,128]{2,1,0:T(8,128)S(1)}, u32[]{:S(2)}, u32[]{:S(2)}) collective-permute-start(f32[4,128,128]{2,1,0:T(8,128)S(1)} %pad_maximum_fusion.2.mine_ref), channel_id=1, source_target_pairs={{0,4},{4,0},{1,5},{5,1},{2,6},{6,2},{3,7},{7,3},{8,12},{12,8},{9,1... | collective-permute-start | bytes 786440 | tf_op jit(solution)/shard_map/ppermute | solution.py:379
  76.7 2.9 %factor.1.inv_ref = f32[128,128]{1,0:T(8,128)S(1)} custom-call(s32[1]{0:T(128)} %bitcast.4.where_ref, f32[4,32,128]{2,1,0:T(8,128)S(1)} %pad_maximum_fusion.3.quarters_ref), custom_call_target="tpu_custom_call" | custom-call | flops 402653184 | bytes 131072 | tf_op jit(solution)/shard_map/factor/pallas_call | solution.py:272
  79.7 1.4 %back.1 = (f32[128,1024]{1,0:T(8,128)S(1)}, f32[128,128]{1,0:T(8,128)S(1)}) custom-call(s32[2]{0:T(128)S(1)} %pad_add_fusion.2.where_ref, f32[128,128]{1,0:T(8,128)S(1)} %factor.1.inv_ref, f32[4,128,128]{2,1,0:T(8,128)S(1)} %pad_maximum_fusion.2.mine_ref, f32[4,128,128]{2,1,0:T(8,128)S(1)} %collective-permute-done.18.other_ref), custom_call_target="tpu_custom_call" | custom-call | flops 402653184 | bytes 1048576 | tf_op jit(solution)/shard_map/back/pallas_call | solution.py:306
  81.1 1.9 %collective-permute-start.20 = (f32[128,128]{1,0:T(8,128)S(1)}, f32[128,128]{1,0:T(8,128)S(1)}, u32[]{:S(2)}, u32[]{:S(2)}) collective-permute-start(f32[128,128]{1,0:T(8,128)S(1)} %get-tuple-element.31.g0_ref), channel_id=1, source_target_pairs={{0,2},{1,3},{2,0},{3,1},{4,6},{5,7},{6,4},{7,5},{8,10},{9,11},{10,... | collective-permute-start | bytes 196616 | tf_op jit(solution)/shard_map/ppermute | solution.py:379
  83.8 2.5 %space.1 = (f32[2048,128]{1,0:T(8,128)}, bf16[1024,384]{1,0:T(8,128)(2,1)S(1)}) custom-call(s32[4]{0:T(128)S(1)} %pad_add_fusion.where_ref, f32[128,128]{1,0:T(8,128)S(1)} %factor.1.inv_ref, f32[128,1024]{1,0:T(8,128)S(1)} %get-tuple-element.28.back_t_ref, f32[512,128]{1,0:T(8,128)S(1)} %add_add_fusion.s_ref.refs_0_, ...), custom_call_target="tpu_custom_call" | custom-call | flops 402653184 | bytes 3145728 | tf_op jit(solution)/shard_map/space/pallas_call | solution.py:332
  87.6 4.0 %time_basis.1 = f32[1024,128]{1,0:T(8,128)} custom-call(bf16[1024,384]{1,0:T(8,128)(2,1)S(1)} %get-tuple-element.30.back_ref, f32[128,128]{1,0:T(8,128)S(1)} %get-tuple-element.31.g0_ref, f32[128,128]{1,0:T(8,128)S(1)} %collective-permute-done.19.g1_ref, f32[128,128]{1,0:T(8,128)S(1)} %collective-permute-done.20.g2_ref, ...), custom_call_target="tpu_custom_call" | custom-call | flops 201326592 | bytes 1048576 | tf_op jit(solution)/shard_map/time_basis/pallas_call | solution.py:360
  (47 shorter events, 7.2 us)
Async XLA Ops:
  3.0 7.5 %collective-permute-start = (f32[256,128]{1,0:T(8,128)S(1)}, f32[256,128]{1,0:T(8,128)S(1)}, u32[]{:S(2)}, u32[]{:S(2)}) collective-permute-start(f32[256,128]{1,0:T(8,128)S(1)} %get-tuple-element.37), channel_id=1, source_target_pairs={{0,1},{1,2},{2,3},{3,0},{4,5},{5,6},{6,7},{7,4},{8,9},{9,10},{10,1... | collective-permute-start | bytes 393224 | tf_op jit(solution)/shard_map/ppermute | solution.py:379
  5.2 5.3 %collective-permute-start.2 = (f32[256,128]{1,0:T(8,128)S(1)}, f32[256,128]{1,0:T(8,128)S(1)}, u32[]{:S(2)}, u32[]{:S(2)}) collective-permute-start(f32[256,128]{1,0:T(8,128)S(1)} %get-tuple-element.38), channel_id=1, source_target_pairs={{0,3},{1,0},{2,1},{3,2},{4,7},{5,4},{6,5},{7,6},{8,11},{9,8},{10,9... | collective-permute-start | bytes 393224 | tf_op jit(solution)/shard_map/ppermute | solution.py:379
  10.7 6.5 %collective-permute-start.1 = (f32[512,128]{1,0:T(8,128)S(1)}, f32[512,128]{1,0:T(8,128)S(1)}, u32[]{:S(2)}, u32[]{:S(2)}) collective-permute-start(f32[512,128]{1,0:T(8,128)S(1)} %pad_maximum_fusion), channel_id=1, source_target_pairs={{0,1},{1,2},{2,3},{3,0},{4,5},{5,6},{6,7},{7,4},{8,9},{9,10},{10,1... | collective-permute-start | bytes 786440 | tf_op jit(solution)/shard_map/ppermute | solution.py:379
  10.8 6.4 %collective-permute-start.3 = (f32[512,128]{1,0:T(8,128)S(1)}, f32[512,128]{1,0:T(8,128)S(1)}, u32[]{:S(2)}, u32[]{:S(2)}) collective-permute-start(f32[512,128]{1,0:T(8,128)S(1)} %pad_maximum_fusion.1), channel_id=1, source_target_pairs={{0,3},{1,0},{2,1},{3,2},{4,7},{5,4},{6,5},{7,6},{8,11},{9,8},{10,9... | collective-permute-start | bytes 786440 | tf_op jit(solution)/shard_map/ppermute | solution.py:379
  17.3 8.5 %collective-permute-start.5 = (f32[512,128]{1,0:T(8,128)S(1)}, f32[512,128]{1,0:T(8,128)S(1)}, u32[]{:S(2)}, u32[]{:S(2)}) collective-permute-start(f32[512,128]{1,0:T(8,128)S(1)} %add_add_fusion.s_ref.refs_0_), channel_id=1, source_target_pairs={{0,1},{1,2},{2,3},{3,0},{4,5},{5,6},{6,7},{7,4},{8,9},{9,10},{10,1... | collective-permute-start | bytes 786440 | tf_op jit(solution)/shard_map/ppermute | solution.py:379
  17.7 10.9 %collective-permute-start.6 = (f32[512,128]{1,0:T(8,128)S(1)}, f32[512,128]{1,0:T(8,128)S(1)}, u32[]{:S(2)}, u32[]{:S(2)}) collective-permute-start(f32[512,128]{1,0:T(8,128)S(1)} %add_add_fusion.s_ref.refs_0_), channel_id=1, source_target_pairs={{0,2},{1,3},{2,0},{3,1},{4,6},{5,7},{6,4},{7,5},{8,10},{9,11},{10,... | collective-permute-start | bytes 786440 | tf_op jit(solution)/shard_map/ppermute | solution.py:379
  21.3 8.7 %collective-permute-start.4 = (f32[512,128]{1,0:T(8,128)S(1)}, f32[512,128]{1,0:T(8,128)S(1)}, u32[]{:S(2)}, u32[]{:S(2)}) collective-permute-start(f32[512,128]{1,0:T(8,128)S(1)} %add_add_fusion.s_ref.refs_0_), channel_id=1, source_target_pairs={{0,3},{1,0},{2,1},{3,2},{4,7},{5,4},{6,5},{7,6},{8,11},{9,8},{10,9... | collective-permute-start | bytes 786440 | tf_op jit(solution)/shard_map/ppermute | solution.py:379
  30.8 6.8 %collective-permute-start.7 = (f32[4,160,128]{2,1,0:T(8,128)S(1)}, f32[4,160,128]{2,1,0:T(8,128)S(1)}, u32[]{:S(2)}, u32[]{:S(2)}) collective-permute-start(f32[4,160,128]{2,1,0:T(8,128)S(1)} %dynamic-slice_bitcast_fusion), channel_id=1, source_target_pairs={{0,4},{4,0},{1,5},{5,1},{2,6},{6,2},{3,7},{7,3},{8,12},{12,8},{9,1... | collective-permute-start | bytes 983048 | tf_op jit(solution)/shard_map/ppermute | solution.py:379
  37.7 6.3 %collective-permute-start.8 = (f32[160,128]{1,0:T(8,128)S(1)}, f32[160,128]{1,0:T(8,128)S(1)}, u32[]{:S(2)}, u32[]{:S(2)}) collective-permute-start(f32[160,128]{1,0:T(8,128)S(1)} %get-tuple-element.34), channel_id=1, source_target_pairs={{0,64},{64,128},{128,192},{192,0},{1,65},{65,129},{129,193},{193,1... | collective-permute-start | bytes 245768 | tf_op jit(solution)/shard_map/ppermute | solution.py:379
  40.2 3.8 %collective-permute-start.9 = (f32[160,128]{1,0:T(8,128)S(1)}, f32[160,128]{1,0:T(8,128)S(1)}, u32[]{:S(2)}, u32[]{:S(2)}) collective-permute-start(f32[160,128]{1,0:T(8,128)S(1)} %get-tuple-element.33), channel_id=1, source_target_pairs={{0,192},{64,0},{128,64},{192,128},{1,193},{65,1},{129,65},{193,129... | collective-permute-start | bytes 245768 | tf_op jit(solution)/shard_map/ppermute | solution.py:379
  41.5 4.8 %collective-permute-start.10 = (f32[160,128]{1,0:T(8,128)S(1)}, f32[160,128]{1,0:T(8,128)S(1)}, u32[]{:S(2)}, u32[]{:S(2)}) collective-permute-start(f32[160,128]{1,0:T(8,128)S(1)} %get-tuple-element.32), channel_id=1, source_target_pairs={{0,128},{64,192},{128,0},{192,64},{1,129},{65,193},{129,1},{193,65... | collective-permute-start | bytes 245768 | tf_op jit(solution)/shard_map/ppermute | solution.py:379
  46.3 3.7 %collective-permute-start.11 = (f32[160,128]{1,0:T(8,128)S(1)}, f32[160,128]{1,0:T(8,128)S(1)}, u32[]{:S(2)}, u32[]{:S(2)}) collective-permute-start(f32[160,128]{1,0:T(8,128)S(1)} %add.125), channel_id=1, source_target_pairs={{0,8},{8,0},{16,24},{24,16},{32,40},{40,32},{48,56},{56,48},{1,9},... | collective-permute-start | bytes 245768 | tf_op jit(solution)/shard_map/ppermute | solution.py:411
  50.0 10.5 %collective-permute-start.12 = (f32[160,128]{1,0:T(8,128)S(1)}, f32[160,128]{1,0:T(8,128)S(1)}, u32[]{:S(2)}, u32[]{:S(2)}) collective-permute-start(f32[160,128]{1,0:T(8,128)S(1)} %add.126), channel_id=1, source_target_pairs={{0,32},{8,40},{16,48},{24,56},{32,0},{40,8},{48,16},{56,24},{1,33}... | collective-permute-start | bytes 245768 | tf_op jit(solution)/shard_map/ppermute | solution.py:379
  56.8 7.3 %collective-permute-start.13 = (f32[160,128]{1,0:T(8,128)S(1)}, f32[160,128]{1,0:T(8,128)S(1)}, u32[]{:S(2)}, u32[]{:S(2)}) collective-permute-start(f32[160,128]{1,0:T(8,128)S(1)} %add.126), channel_id=1, source_target_pairs={{0,16},{8,24},{16,32},{24,40},{32,48},{40,56},{48,0},{56,8},{1,17}... | collective-permute-start | bytes 245768 | tf_op jit(solution)/shard_map/ppermute | solution.py:379
  58.0 6.5 %collective-permute-start.14 = (f32[160,128]{1,0:T(8,128)S(1)}, f32[160,128]{1,0:T(8,128)S(1)}, u32[]{:S(2)}, u32[]{:S(2)}) collective-permute-start(f32[160,128]{1,0:T(8,128)S(1)} %add.126), channel_id=1, source_target_pairs={{0,48},{8,56},{16,0},{24,8},{32,16},{40,24},{48,32},{56,40},{1,49}... | collective-permute-start | bytes 245768 | tf_op jit(solution)/shard_map/ppermute | solution.py:379
  64.6 3.4 %collective-permute-start.17 = (f32[160,128]{1,0:T(8,128)S(1)}, f32[160,128]{1,0:T(8,128)S(1)}, u32[]{:S(2)}, u32[]{:S(2)}) collective-permute-start(f32[160,128]{1,0:T(8,128)S(1)} %add_add_fusion.1), channel_id=1, source_target_pairs={{0,192},{64,0},{128,64},{192,128},{1,193},{65,1},{129,65},{193,129... | collective-permute-start | bytes 245768 | tf_op jit(solution)/shard_map/ppermute | solution.py:379
  65.8 4.8 %collective-permute-start.16 = (f32[160,128]{1,0:T(8,128)S(1)}, f32[160,128]{1,0:T(8,128)S(1)}, u32[]{:S(2)}, u32[]{:S(2)}) collective-permute-start(f32[160,128]{1,0:T(8,128)S(1)} %add_add_fusion.1), channel_id=1, source_target_pairs={{0,128},{64,192},{128,0},{192,64},{1,129},{65,193},{129,1},{193,65... | collective-permute-start | bytes 245768 | tf_op jit(solution)/shard_map/ppermute | solution.py:379
  67.3 4.5 %collective-permute-start.15 = (f32[160,128]{1,0:T(8,128)S(1)}, f32[160,128]{1,0:T(8,128)S(1)}, u32[]{:S(2)}, u32[]{:S(2)}) collective-permute-start(f32[160,128]{1,0:T(8,128)S(1)} %add_add_fusion.1), channel_id=1, source_target_pairs={{0,64},{64,128},{128,192},{192,0},{1,65},{65,129},{129,193},{193,1... | collective-permute-start | bytes 245768 | tf_op jit(solution)/shard_map/ppermute | solution.py:379
  71.8 7.8 %collective-permute-start.18 = (f32[4,128,128]{2,1,0:T(8,128)S(1)}, f32[4,128,128]{2,1,0:T(8,128)S(1)}, u32[]{:S(2)}, u32[]{:S(2)}) collective-permute-start(f32[4,128,128]{2,1,0:T(8,128)S(1)} %pad_maximum_fusion.2.mine_ref), channel_id=1, source_target_pairs={{0,4},{4,0},{1,5},{5,1},{2,6},{6,2},{3,7},{7,3},{8,12},{12,8},{9,1... | collective-permute-start | bytes 786440 | tf_op jit(solution)/shard_map/ppermute | solution.py:379
  81.0 6.4 %collective-permute-start.19 = (f32[128,128]{1,0:T(8,128)S(1)}, f32[128,128]{1,0:T(8,128)S(1)}, u32[]{:S(2)}, u32[]{:S(2)}) collective-permute-start(f32[128,128]{1,0:T(8,128)S(1)} %get-tuple-element.31.g0_ref), channel_id=1, source_target_pairs={{0,1},{1,2},{2,3},{3,0},{4,5},{5,6},{6,7},{7,4},{8,9},{9,10},{10,1... | collective-permute-start | bytes 196616 | tf_op jit(solution)/shard_map/ppermute | solution.py:379
  81.1 6.3 %collective-permute-start.20 = (f32[128,128]{1,0:T(8,128)S(1)}, f32[128,128]{1,0:T(8,128)S(1)}, u32[]{:S(2)}, u32[]{:S(2)}) collective-permute-start(f32[128,128]{1,0:T(8,128)S(1)} %get-tuple-element.31.g0_ref), channel_id=1, source_target_pairs={{0,2},{1,3},{2,0},{3,1},{4,6},{5,7},{6,4},{7,5},{8,10},{9,11},{10,... | collective-permute-start | bytes 196616 | tf_op jit(solution)/shard_map/ppermute | solution.py:379
  83.0 4.7 %collective-permute-start.21 = (f32[128,128]{1,0:T(8,128)S(1)}, f32[128,128]{1,0:T(8,128)S(1)}, u32[]{:S(2)}, u32[]{:S(2)}) collective-permute-start(f32[128,128]{1,0:T(8,128)S(1)} %get-tuple-element.31.g0_ref), channel_id=1, source_target_pairs={{0,3},{1,0},{2,1},{3,2},{4,7},{5,4},{6,5},{7,6},{8,11},{9,8},{10,9... | collective-permute-start | bytes 196616 | tf_op jit(solution)/shard_map/ppermute | solution.py:379
